TPU v7x, 32 devices: a whole 2x2x4 slice. The times are simulated.
32 devices in a mesh: groups: 2 (over y), occ: 4 (over z), vir: 2 (over x), rep: 2 (over core).
Axes of the slice: x: 2, y: 2, z: 4, core: 2. Of those that a mesh axis runs over, the one named last changes fastest.
Arguments:
- amps: float32 [8, 800, 800], P(('groups', 'occ'), ('vir', 'rep')), parts along dimension 0
- drive: float32 [8, 800, 800], P(('groups', 'occ'), ('vir', 'rep')), parts along dimension 0, may hold values from -6 to 6
- cycle_w: float32 [8, 8, 800, 800], P(('groups', 'occ'), None, None, ('vir', 'rep')), parts along dimension 0, may hold values from -0.21875 to 0.21875
- cycle_src: int32 [8, 8], P(('groups', 'occ')), parts along dimension 0, may hold values from 0 to 3
- cycle_count: int32 [8], P(('groups', 'occ')), parts along dimension 0, may hold values from 1 to 8, as said below
- ladder_src: int32 [8, 1], P(('groups', 'occ')), parts along dimension 0, may hold values from 0 to 3
- ladder_coef: float32 [8, 1], P(('groups', 'occ')), parts along dimension 0, may hold values from -1 to 1
- eps_vir: float32 [1600], P('groups'), parts along dimension 0, may hold values from 0.5 to 3
- pair_energy: float32 [8], P(('groups', 'occ')), parts along dimension 0, may hold values from -4 to -0.8
Outputs:
- residual: float32 [8, 800, 800], P(('groups', 'occ'), ('vir', 'rep')), parts along dimension 0
- update: float32 [8, 800, 800], P(('groups', 'occ'), ('vir', 'rep')), parts along dimension 0
There are 2 independent parts, one for each index of `groups`. A program takes and returns all parts, laid end to end along the dimension named above; each array names one. Nothing has to cross between parts.
Inputs may be any that keep to these rules, and one draw needn't show every extreme that they name: `cycle_src`: pair indices. Only the first cycle_count[n] blocks of pair n count; some pair keeps all 8. `ladder_src`: pair indices.
All inputs are finite; a program needn't handle non-finite values.
Results may differ from a plain program's by a relative error of at most 0.00005.
Values sent between devices are 32-bit elements; how exact they have to be, the bound alone decides.
No kernel may reach another device: no remote copies, remote signals or barrier semaphores. Data moves between devices by JAX's collectives and lax.ppermute only.
A program may use at most 64 MiB of HBM per device.

v0:
```python
import math

import jax
import jax.numpy as jnp
from jax import lax
from jax.sharding import PartitionSpec as P

clip_level = 0.5


def body(
    amps, drive, cycle_w, cycle_src, cycle_count, ladder_src, ladder_coef, eps_vir, pair_energy
):
    largest_value = lax.Precision.HIGHEST
    pairs_per_unit, rows, width = amps.shape
    nring = cycle_w.shape[1]
    n_occ = lax.axis_size("occ")
    npair = pairs_per_unit * n_occ
    flattened_sources = cycle_src.reshape(-1)
    indicator_matrix = (ladder_src[:, :, None] == jnp.arange(npair)[None, None, :]).astype(
        jnp.float32
    )
    own_ladder = jnp.sum(ladder_coef[:, :, None] * indicator_matrix, axis=1)
    all_rows = lax.all_gather(amps, "occ", axis=0, tiled=True)
    full_ladder = lax.all_gather(own_ladder, "occ", axis=0, tiled=True)
    spread = lax.all_to_all(amps, "occ", split_axis=2, concat_axis=0, tiled=True)
    mixed = jnp.einsum("nm,mce->nce", full_ladder, spread, precision=largest_value)
    ladder = lax.all_to_all(mixed, "occ", split_axis=0, concat_axis=2, tiled=True)
    selected_rows = jnp.take(all_rows, flattened_sources, axis=0).reshape(
        pairs_per_unit, nring, rows, width
    )
    live = (jnp.arange(nring)[None, :] < cycle_count[:, None]).astype(jnp.float32)
    partial_value = jnp.einsum(
        "ptac,ptcb->pab", cycle_w * live[:, :, None, None], selected_rows, precision=largest_value
    )
    cycle = lax.psum_scatter(partial_value, ("vir", "rep"), scatter_dimension=1, tiled=True)
    first_row = lax.axis_index(("vir", "rep")) * rows
    eps_rows = lax.dynamic_slice_in_dim(eps_vir, first_row, rows)
    denom = eps_rows[None, :, None] + eps_vir[None, None, :] - pair_energy[:, None, None]
    residual = drive + cycle + ladder - denom * amps
    total = lax.psum(jnp.sum(residual * residual), ("occ", "vir", "rep"))
    scale = jnp.minimum(1.0, clip_level * width * math.sqrt(npair) / jnp.sqrt(total))
    update = scale * residual / denom
    return (residual, update)


def solution(mesh):
    in_specs = (
        P(("groups", "occ"), ("vir", "rep"), None),
        P(("groups", "occ"), ("vir", "rep"), None),
        P(("groups", "occ"), None, None, ("vir", "rep")),
        P(("groups", "occ"), None),
        P(("groups", "occ")),
        P(("groups", "occ"), None),
        P(("groups", "occ"), None),
        P("groups"),
        P(("groups", "occ")),
    )
    out_specs = (
        P(("groups", "occ"), ("vir", "rep"), None),
        P(("groups", "occ"), ("vir", "rep"), None),
    )
    return jax.shard_map(body, mesh=mesh, in_specs=in_specs, out_specs=out_specs, check_vma=False)
```

profile of v0, /device:TPU:0, one launch (start us, length us, event | category | flops | bytes accessed | tf_op | source)
XLA Modules:
  0.0 197.5 jit_solution(11460997854377217401)
XLA Ops:
  7.2 0.0 all-gather.3.cloned.1.call-start
  7.2 0.7 all-gather.3.cloned.1.call-update
  7.9 0.0 reduce-scatter.5.cloned.1.call-start
  8.6 0.7 fusion.15
  9.3 0.7 compare_and_fusion
  9.9 61.3 %all-gather.3.cloned.1.call-done = f32[4,200,800]{2,1,0:T(8,128)} async-done(((f32[1,200,800]{2,1,0:T(8,128)}), f32[4,200,800]{2,1,0:T(8,128)}) %all-gather.3.cloned.1.call-update) | async-done | bytes 2560016 | tf_op jit(solution)/shard_map/all_gather | solution.py:24
  71.2 5.2 %gather_fusion = f32[8,200,800]{2,1,0:T(8,128)} fusion(f32[4,200,800]{2,1,0:T(8,128)} %all-gather.3.cloned.1.call-done, s32[1024]{0:T(1024)S(1)} %pad_clamp_fusion), kind=kCustom, calls=%fused_computation | custom fusion | bytes 10240032 | tf_op jit(solution)/shard_map/jit(_take)/gather | solution.py:29
  76.4 0.0 copy-start
  76.4 25.2 %fusion.7 = f32[1,800,800]{2,1,0:T(8,128)} fusion(f32[8,200,800]{2,1,0:T(8,128)} %gather_fusion, pred[8]{0:T(512)(128)(4,1)S(1)} %get-tuple-element.4, f32[1,8,800,200]{2,3,1,0:T(8,128)} %param.11, f32[8]{0:T(128)S(1)} %get-tuple-element.5), kind=kOutput, calls=%fused_computation.8 | convolution fusion | flops 12290560000 | bytes 12800040 | tf_op jit(solution)/shard_map/ptac,ptcb->pab/dot_general | solution.py:33
  101.7 0.0 reduce-scatter.5.cloned.1.call-update
  101.7 0.0 copy-done
  101.7 0.0 copy-start.2
  101.7 1.9 copy.11
  103.6 3.5 %all-to-all-start = ((f32[1,200,800]{1,0,2:T(1,128)}), f32[1,200,800]{1,0,2:T(1,128)S(1)}, u32[]{:S(2)}, u32[]{:S(2)}) async-start(f32[1,200,800]{1,0,2:T(1,128)} %copy.11), calls=%async_computation | async-start | bytes 1638400 | tf_op jit(solution)/shard_map/all_to_all | solution.py:26
  108.4 18.1 %all-gather = f32[4,1,4]{2,1,0:T(1,128)S(1)} all-gather(f32[1,1,4]{2,1,0:T(1,128)S(1)} %fusion.14), channel_id=1, replica_groups=mesh['groups'=2,'occ'=4,'vir'=2,'rep'=2] {'occ'}, dimensions={0}, use_global_device_ids=true | all-gather | bytes 80 | tf_op jit(solution)/shard_map/all_gather | solution.py:25
  126.6 1.6 all-to-all-done
  128.2 0.1 copy.18
  128.2 0.4 copy.15
  128.6 1.4 fusion.12
  130.1 1.0 copy.13
  131.1 4.8 %all-to-all-start.1 = ((f32[4,200,200]{2,1,0:T(8,128)}), f32[4,200,200]{2,1,0:T(8,128)S(1)}, u32[]{:S(2)}, u32[]{:S(2)}) async-start(f32[4,200,200]{2,1,0:T(8,128)} %copy.13), calls=%async_computation.1 | async-start | bytes 1638400 | tf_op jit(solution)/shard_map/all_to_all | solution.py:28
  136.6 0.0 copy-done.2
  136.6 0.1 dynamic_slice.3
  136.7 19.0 %all-to-all-done.1 = f32[4,200,200]{2,1,0:T(8,128)S(1)} async-done(((f32[4,200,200]{2,1,0:T(8,128)}), f32[4,200,200]{2,1,0:T(8,128)S(1)}, u32[]{:S(2)}, u32[]{:S(2)}) %all-to-all-start.1) | async-done | bytes 640032 | tf_op jit(solution)/shard_map/all_to_all | solution.py:28
  155.6 0.3 copy.14
  155.9 0.5 all_to_all.33
  156.4 0.0 reduce-scatter.5.cloned.1.call-done
  156.5 2.3 %multiply_reduce_fusion = (f32[]{:T(128)}, f32[1,200,800]{2,1,0:T(8,128)S(1)}) fusion(f32[1,200,800]{2,1,0:T(8,128)S(1)} %copy-done, f32[]{:T(128)} %bitcast.38, f32[800]{0:T(1024)S(1)} %copy-done.2, f32[200]{0:T(256)S(1)} %dynamic_slice.3, f32[1,200,800]{2,1,0:T(8,128)S(1)} %all_to_all.33, f32[1,200,800]{2,1,0:T(8,128)} %param.10, ...), kind=kLoop, calls=%fused_computation.12 | loop fusion | flops 1279999 | bytes 3204008 | tf_op jit(solution)/shard_map/reduce_sum | solution.py:41
  158.8 0.0 copy-start.1
  158.8 30.1 %psum.7 = f32[]{:T(128)} all-reduce(f32[]{:T(128)} %get-tuple-element.2), channel_id=1, replica_groups=mesh['groups'=2,'occ'=4,'vir'=2,'rep'=2] {'occ','vir','rep'}, use_global_device_ids=true, to_apply=%region_2.3 | all-reduce | flops 1 | bytes 8 | tf_op jit(solution)/shard_map/psum | solution.py:41
  189.6 1.0 multiply_divide_fusion
  190.6 0.0 copy-done.1
  (2 shorter events, 0.0 us)
Async XLA Ops:
  7.2 64.0 %all-gather.3.cloned.1.call-start = ((), (), s32[]{:S(2)}) async-start(), calls=%async_computation.3 | async-start | bytes 3584000 | tf_op jit(solution)/shard_map/all_gather | solution.py:24
  7.9 148.6 %reduce-scatter.5.cloned.1.call-start = ((), (), s32[]{:S(2)}) async-start(), calls=%async_computation.4 | async-start | bytes 3584000
  76.4 25.3 %copy-start = (f32[1,200,800]{2,1,0:T(8,128)S(1)}, f32[1,200,800]{2,1,0:T(8,128)}, u32[]{:S(2)}) copy-start(f32[1,200,800]{2,1,0:T(8,128)} %param.9) | copy-start | bytes 1920004
  101.7 34.9 %copy-start.2 = (f32[800]{0:T(1024)S(1)}, f32[800]{0:T(1024)}, u32[]{:S(2)}) copy-start(f32[800]{0:T(1024)} %param.16) | copy-start | bytes 9604
  103.6 24.6 %all-to-all-start = ((f32[1,200,800]{1,0,2:T(1,128)}), f32[1,200,800]{1,0,2:T(1,128)S(1)}, u32[]{:S(2)}, u32[]{:S(2)}) async-start(f32[1,200,800]{1,0,2:T(1,128)} %copy.11), calls=%async_computation | async-start | bytes 1638400 | tf_op jit(solution)/shard_map/all_to_all | solution.py:26
  131.1 24.5 %all-to-all-start.1 = ((f32[4,200,200]{2,1,0:T(8,128)}), f32[4,200,200]{2,1,0:T(8,128)S(1)}, u32[]{:S(2)}, u32[]{:S(2)}) async-start(f32[4,200,200]{2,1,0:T(8,128)} %copy.13), calls=%async_computation.1 | async-start | bytes 1638400 | tf_op jit(solution)/shard_map/all_to_all | solution.py:28
  158.8 31.8 %copy-start.1 = (f32[1,200,800]{2,1,0:T(8,128)}, f32[1,200,800]{2,1,0:T(8,128)S(1)}, u32[]{:S(2)}) copy-start(f32[1,200,800]{2,1,0:T(8,128)S(1)} %get-tuple-element.3) | copy-start | bytes 1920004
Sparse Core Ops, SparseCore 0:
  9.6 61.5 all-gather.2
  101.8 34.9 reduce-scatter.4
where the time goes:
time: 198 us; the launch traced here: 197 us
  waiting for transfers between devices  82.6 us (42%)
  blocking collectives  48.2 us (24%)
  matrix products  26.7 us (13%)
  between operations  17.4 us (9%)
  local copies, waits for them, and re-layouts  9.46 us (5%)
  starting transfers between devices  8.39 us (4%)
  other arithmetic  4.69 us (2%)
    all_gather x1, waiting for transfers between devices, body(): all_rows = lax.all_gather(amps, 'occ', axis=0, tiled=True)  61.3 us
    psum x1, blocking collectives, body(): total = lax.psum(jnp.sum(residual * residual), ('occ', 'vir', 'rep'))  30.1 us
    dot_general x1, matrix products, body(): jnp.einsum('ptac,ptcb->pab', cycle_w * live[:, :, None, None], selected_r...  25.2 us
    all_to_all x1, waiting for transfers between devices, body(): lax.all_to_all(mixed, 'occ', split_axis=0, concat_axis=2, tiled=True)  19 us
    all_gather x1, blocking collectives, body(): full_ladder = lax.all_gather(own_ladder, 'occ', axis=0, tiled=True)  18.1 us
    gather x1, local copies, waits for them, and re-layouts, body(): jnp.take(all_rows, flattened_sources, axis=0)  5.2 us
    all_to_all x1, starting transfers between devices, body(): lax.all_to_all(mixed, 'occ', split_axis=0, concat_axis=2, tiled=True)  4.79 us
  transfers between devices with their start and end apart: 4, of which 3 were waited for; matrix products, arithmetic and copies ran while one was open for 3% of the time, Pallas kernels for 0%

commit v1 on v0

v1 whole, which is shorter than its diff:
```python
import functools
import math

import jax
import jax.numpy as jnp
from jax import lax
from jax.experimental import pallas as pl
from jax.experimental.pallas import tpu as pltpu
from jax.sharding import PartitionSpec as P

clip_level = 0.5
LANES = 128
SMEM = pl.BlockSpec(memory_space=pltpu.SMEM)
SWAP = [(0, 1), (1, 0)]
ENDS = [(0, 1), (1, 0), (2, 3), (3, 2)]
MIDDLE = [(1, 2), (2, 1)]
OUTWARD = [(1, 0), (2, 3)]
ACROSS = [(0, 2), (2, 0), (1, 3), (3, 1)]


def limit(n):
    return pltpu.CompilerParams(vmem_limit_bytes=n << 20)


class Chunk:
    def __init__(self, rows, width, first, count, rest):
        self.rows, self.first, self.count = rows, first, count
        self.rest = width % LANES if rest else 0
        self.at = width - self.rest
        self.group = -(-rows // 32) * 8
        self.length = rows * count + (self.group if self.rest else 0)
        self.width = LANES * count + self.rest

    def take(self, ref):
        parts = [ref[:, self.first * LANES : (self.first + self.count) * LANES]]
        if self.rest:
            parts.append(ref[:, self.at : self.at + self.rest])
        return jnp.concatenate(parts, axis=1) if len(parts) > 1 else parts[0]

    def put(self, ref, value):
        span = LANES * self.count
        ref[:, self.first * LANES : self.first * LANES + span] = value[:, :span]
        if self.rest:
            ref[:, self.at : self.at + self.rest] = value[:, span:]

    def load(self, read):
        parts = [read(t * self.rows, self.rows) for t in range(self.count)]
        if self.rest:
            packed = read(self.count * self.rows, self.group)
            rest = [packed[:, g * self.rest : (g + 1) * self.rest] for g in range(4)]
            parts.append(jnp.concatenate(rest, axis=0)[: self.rows])
        return jnp.concatenate(parts, axis=1)

    def store(self, write, value):
        for t in range(self.count):
            write(t * self.rows, self.rows, value[:, t * LANES : (t + 1) * LANES])
        if self.rest:
            rest = value[:, self.count * LANES :]
            short = 4 * self.group - self.rows
            rest = jnp.concatenate([rest, jnp.zeros((short, self.rest), rest.dtype)], axis=0)
            groups = [rest[g * self.group : (g + 1) * self.group] for g in range(4)]
            write(self.count * self.rows, self.group, jnp.concatenate(groups, axis=1))


def reader(ref, lead=()):
    return lambda start, size: ref[(*lead, pl.ds(start, size), slice(None))]


def writer(ref, lead=()):
    def write(start, size, value):
        ref[(*lead, pl.ds(start, size), slice(None))] = value

    return write


def split(value):
    high = value.astype(jnp.bfloat16)
    return high, (value - high.astype(jnp.float32)).astype(jnp.bfloat16)


def product(high, low, x_high, x_low):
    dot = functools.partial(jnp.dot, preferred_element_type=jnp.float32)
    return dot(high, x_high) + (dot(low, x_high) + dot(high, x_low))


def pack(amps, chunks):
    def kernel(amps_ref, *outs):
        for chunk, out in zip(chunks, outs, strict=True):
            chunk.store(writer(out), chunk.take(amps_ref))

    return pl.pallas_call(
        kernel,
        out_shape=[jax.ShapeDtypeStruct((c.length, LANES), jnp.float32) for c in chunks],
        name="pack",
    )(amps)


def sum_by_source(cycle_w, cycle_src, cycle_count, npair, blocks):
    nring, height, depth = cycle_w.shape
    rows = height // blocks

    def kernel(src_ref, count_ref, w_ref, high_ref, low_ref, total):
        total[...] = jnp.zeros_like(total)
        for s in range(nring):

            @pl.when(s < count_ref[0])
            def _():
                source = src_ref[0, s]
                total[source] = total[source] + w_ref[s]

        for m in range(npair):
            high, low = split(total[m])
            high_ref[m, 0] = high
            low_ref[m, 0] = low

    block = pl.BlockSpec((npair, 1, rows, depth), lambda j: (0, j, 0, 0))
    shape = jax.ShapeDtypeStruct((npair, blocks, rows, depth), jnp.bfloat16)
    return pl.pallas_call(
        kernel,
        grid=(blocks,),
        in_specs=[SMEM, SMEM, pl.BlockSpec((nring, rows, depth), lambda j: (0, j, 0))],
        out_specs=[block, block],
        out_shape=[shape, shape],
        scratch_shapes=[pltpu.VMEM((npair, rows, depth), jnp.float32)],
        compiler_params=limit(32),
        name="sum_by_source",
    )(cycle_src, cycle_count, cycle_w)


def ladder_weight(source, lad_src, lad_coef):
    weight = jnp.float32(0)
    for entry in range(lad_src.shape[1]):
        weight = weight + jnp.where(lad_src[0, entry] == source, lad_coef[0, entry], 0.0)
    return weight


def first_stage(chunk, meta, lad_src, lad_coef, energy, weights, own, near, drive, eps_row, eps_col):
    high, low = weights
    _, blocks, rows, depth = high.shape

    def kernel(meta, lad_src, lad_coef, energy, h0, l0, h1, l1, own, near, drive, eps_row, eps_col, away, keep, xs):
        j = pl.program_id(0)

        @pl.when(j == 0)
        def _():
            for i, ref in enumerate((own, near)):
                xs[2 * i], xs[2 * i + 1] = split(chunk.load(reader(ref)))

        value = product(h0[0, 0], l0[0, 0], xs[0], xs[1]) + product(h1[0, 0], l1[0, 0], xs[2], xs[3])

        @pl.when(j < 2)
        def _():
            chunk.store(writer(away, (0,)), value)

        @pl.when(j == 2)
        def _():
            chunk.store(writer(keep, (0,)), value)

        @pl.when(j == 3)
        def _():
            mine = chunk.load(reader(own))
            denom = eps_col[...] + chunk.take(eps_row) - energy[0]
            base = chunk.take(drive) - denom * mine
            base = base + ladder_weight(meta[0], lad_src, lad_coef) * mine
            base = base + ladder_weight(meta[1], lad_src, lad_coef) * chunk.load(reader(near))
            chunk.store(writer(keep, (0,)), value + base)

    def weight_block(k):
        return pl.BlockSpec((1, 1, rows, depth), lambda j, meta: (meta[k], meta[5 + j], 0, 0))

    def whole(a):
        return pl.BlockSpec(a.shape, lambda j, meta: (0,) * a.ndim)

    out = jax.ShapeDtypeStruct((2, chunk.length, LANES), jnp.float32)
    return pl.pallas_call(
        kernel,
        grid_spec=pltpu.PrefetchScalarGridSpec(
            num_scalar_prefetch=1,
            grid=(blocks,),
            in_specs=[SMEM, SMEM, SMEM]
            + [weight_block(0), weight_block(0), weight_block(1), weight_block(1)]
            + [whole(a) for a in (own, near, drive, eps_row, eps_col)],
            out_specs=[
                pl.BlockSpec((1, chunk.length, LANES), lambda j, meta: (jnp.minimum(j, 1), 0, 0)),
                pl.BlockSpec((1, chunk.length, LANES), lambda j, meta: (jnp.maximum(j - 2, 0), 0, 0)),
            ],
            scratch_shapes=[pltpu.VMEM((4, rows, chunk.width), jnp.bfloat16)],
        ),
        out_shape=[out, out],
        compiler_params=limit(32),
        name="first_stage",
    )(meta, lad_src, lad_coef, energy, high, low, high, low, own, near, drive, eps_row, eps_col)


def next_stage(chunk, k, meta, lad_src, lad_coef, weights, inner, outer, away, keep):
    high, low = weights
    _, blocks, rows, depth = high.shape

    def kernel(meta, lad_src, lad_coef, h, l, inner, outer, away_in, keep_in, away, keep, xs, x):
        j = pl.program_id(0)

        @pl.when(j == 0)
        def _():
            @pl.when(meta[4] == 1)
            def _():
                x[...] = chunk.load(reader(inner))

            @pl.when(meta[4] == 0)
            def _():
                x[...] = chunk.load(reader(outer))

            xs[0], xs[1] = split(x[...])

        value = product(h[0, 0], l[0, 0], xs[0], xs[1])

        @pl.when(j < 2)
        def _():
            chunk.store(writer(away, (0,)), value + chunk.load(reader(away_in, (0,))))

        @pl.when(j >= 2)
        def _():
            weight = jnp.where(j == 3, ladder_weight(meta[k], lad_src, lad_coef), 0.0)
            chunk.store(writer(keep, (0,)), value + weight * x[...] + chunk.load(reader(keep_in, (0,))))

    def whole(a):
        return pl.BlockSpec(a.shape, lambda j, meta: (0,) * a.ndim)

    weight_block = pl.BlockSpec((1, 1, rows, depth), lambda j, meta: (meta[k], meta[5 + j], 0, 0))
    sums = [
        pl.BlockSpec((1, chunk.length, LANES), lambda j, meta: (jnp.minimum(j, 1), 0, 0)),
        pl.BlockSpec((1, chunk.length, LANES), lambda j, meta: (jnp.maximum(j - 2, 0), 0, 0)),
    ]
    out = jax.ShapeDtypeStruct((2, chunk.length, LANES), jnp.float32)
    return pl.pallas_call(
        kernel,
        grid_spec=pltpu.PrefetchScalarGridSpec(
            num_scalar_prefetch=1,
            grid=(blocks,),
            in_specs=[SMEM, SMEM, weight_block, weight_block, whole(inner), whole(outer), *sums],
            out_specs=sums,
            scratch_shapes=[
                pltpu.VMEM((2, rows, chunk.width), jnp.bfloat16),
                pltpu.VMEM((rows, chunk.width), jnp.float32),
            ],
        ),
        out_shape=[out, out],
        compiler_params=limit(32),
        name="next_stage",
    )(meta, lad_src, lad_coef, high, low, inner, outer, away, keep)


def finish(chunks, pieces, shape):
    def kernel(*refs):
        *ins, out, total_ref = refs
        total = jnp.float32(0)
        for i, chunk in enumerate(chunks):
            keep, got, far = ins[3 * i : 3 * i + 3]
            value = chunk.load(reader(keep, (1,))) + chunk.load(reader(got, (1,))) + chunk.load(reader(far))
            chunk.put(out, value)
            total = total + jnp.sum(value * value)
        total_ref[...] = jnp.broadcast_to(total, total_ref.shape)

    return pl.pallas_call(
        kernel,
        out_shape=[
            jax.ShapeDtypeStruct(shape, jnp.float32),
            jax.ShapeDtypeStruct((8, LANES), jnp.float32),
        ],
        compiler_params=limit(32),
        name="finish",
    )(*pieces)


def jacobi(residual, total, energy, eps_row, eps_col, bound):
    def kernel(energy, residual, total, eps_row, eps_col, out):
        scale = jnp.minimum(1.0, bound / jnp.sqrt(total[0:1, 0:1]))
        denom = eps_col[...] + eps_row[...] - energy[0]
        out[...] = scale * residual[...] / denom

    vmem = pl.BlockSpec(memory_space=pltpu.VMEM)
    return pl.pallas_call(
        kernel,
        in_specs=[SMEM, vmem, vmem, vmem, vmem],
        out_shape=jax.ShapeDtypeStruct(residual.shape, jnp.float32),
        compiler_params=limit(32),
        name="jacobi",
    )(energy, residual, total, eps_row, eps_col)


def chain_body(amps, drive, cycle_w, cycle_src, cycle_count, ladder_src, ladder_coef, eps_vir, pair_energy):
    _, rows, width = amps.shape
    npair, blocks = lax.axis_size("occ"), width // rows
    place, chip, core = lax.axis_index("occ"), lax.axis_index("vir"), lax.axis_index("rep")
    low_half = place < 2
    order = [
        place,
        place ^ 1,
        jnp.where(low_half, 2, 1),
        jnp.where(low_half, 3, 0),
        ((place == 1) | (place == 2)).astype(jnp.int32),
        2 * (1 - chip) + (1 - core),
        2 * chip + (1 - core),
        2 * (1 - chip) + core,
        2 * chip + core,
    ]
    meta = jnp.stack([jnp.asarray(v, jnp.int32) for v in order])
    eps_row = eps_vir.reshape(1, width)
    eps_col = lax.dynamic_slice_in_dim(eps_vir, (2 * chip + core) * rows, rows).reshape(rows, 1)

    tiles = width // LANES
    half = tiles // 2
    chunks = [Chunk(rows, width, 0, half, True), Chunk(rows, width, half, tiles - half, False)]
    own = pack(amps[0], chunks)
    weights = sum_by_source(cycle_w[0], cycle_src, cycle_count, npair, blocks)

    send = functools.partial(lax.ppermute, axis_name="occ")
    ends = [send(x, perm=ENDS) for x in own]
    middle = [send(x, perm=MIDDLE) for x in own]
    second = [send(x, perm=OUTWARD) for x in middle]
    across = [send(x, perm=MIDDLE) for x in ends]
    third = [send(x, perm=OUTWARD) for x in across]

    pieces = []
    for i, chunk in enumerate(chunks):
        sums = first_stage(
            chunk, meta, ladder_src, ladder_coef, pair_energy, weights,
            own[i], ends[i], drive[0], eps_row, eps_col,
        )
        sums = next_stage(chunk, 2, meta, ladder_src, ladder_coef, weights, middle[i], second[i], *sums)
        away, keep = next_stage(chunk, 3, meta, ladder_src, ladder_coef, weights, across[i], third[i], *sums)
        got = lax.ppermute(away, "rep", SWAP)
        far = lax.ppermute(keep[0] + got[0], "vir", SWAP)
        pieces += [keep, got, far]
    residual, total = finish(chunks, pieces, (rows, width))
    for axis, perm in (("rep", SWAP), ("vir", SWAP), ("occ", ENDS), ("occ", ACROSS)):
        total = total + lax.ppermute(total, axis, perm)
    update = jacobi(residual, total, pair_energy, eps_row, eps_col, clip_level * width * math.sqrt(npair))
    return residual[None], update[None]


def any_body(amps, drive, cycle_w, cycle_src, cycle_count, ladder_src, ladder_coef, eps_vir, pair_energy):
    largest_value = lax.Precision.HIGHEST
    pairs_per_unit, rows, width = amps.shape
    nring = cycle_w.shape[1]
    npair = pairs_per_unit * lax.axis_size("occ")
    all_rows = lax.all_gather(amps, "occ", axis=0, tiled=True)
    ladder = jnp.sum(ladder_coef[:, :, None, None] * all_rows[ladder_src], axis=1)
    selected_rows = jnp.take(all_rows, cycle_src.reshape(-1), axis=0).reshape(
        pairs_per_unit, nring, rows, width
    )
    live = (jnp.arange(nring)[None, :] < cycle_count[:, None]).astype(jnp.float32)
    partial_value = jnp.einsum(
        "ptac,ptcb->pab", cycle_w * live[:, :, None, None], selected_rows, precision=largest_value
    )
    cycle = lax.psum_scatter(partial_value, ("vir", "rep"), scatter_dimension=1, tiled=True)
    first_row = lax.axis_index(("vir", "rep")) * rows
    eps_rows = lax.dynamic_slice_in_dim(eps_vir, first_row, rows)
    denom = eps_rows[None, :, None] + eps_vir[None, None, :] - pair_energy[:, None, None]
    residual = drive + cycle + ladder - denom * amps
    total = lax.psum(jnp.sum(residual * residual), ("occ", "vir", "rep"))
    scale = jnp.minimum(1.0, clip_level * width * math.sqrt(npair) / jnp.sqrt(total))
    return residual, scale * residual / denom


def body(*args):
    amps, cycle_w = args[0], args[2]
    pairs_per_unit, rows, width = amps.shape
    chain = (
        pairs_per_unit == 1
        and (lax.axis_size("occ"), lax.axis_size("vir"), lax.axis_size("rep")) == (4, 2, 2)
        and cycle_w.shape[1] >= 4
        and rows % 8 == 0
        and width % LANES == LANES // 4
        and width >= 2 * LANES
    )
    return (chain_body if chain else any_body)(*args)


def solution(mesh):
    in_specs = (
        P(("groups", "occ"), ("vir", "rep"), None),
        P(("groups", "occ"), ("vir", "rep"), None),
        P(("groups", "occ"), None, None, ("vir", "rep")),
        P(("groups", "occ"), None),
        P(("groups", "occ")),
        P(("groups", "occ"), None),
        P(("groups", "occ"), None),
        P("groups"),
        P(("groups", "occ")),
    )
    out_specs = (
        P(("groups", "occ"), ("vir", "rep"), None),
        P(("groups", "occ"), ("vir", "rep"), None),
    )
    return jax.shard_map(body, mesh=mesh, in_specs=in_specs, out_specs=out_specs, check_vma=False)
```

time: 198 us -> 108 us (0.55)
  waiting for transfers between devices: 82.6 us -> 31.1 us
  blocking collectives: 48.2 us -> 0 us
  Pallas kernels: 0 us -> 27.4 us
  matrix products: 26.7 us -> 0 us
  starting transfers between devices: 8.39 us -> 30.5 us
  between operations: 17.4 us -> 3.5 us
  local copies, waits for them, and re-layouts: 9.46 us -> 14.7 us
  other arithmetic: 4.69 us -> 0.09 us
    all_gather x1 -> x0, waiting for transfers between devices: 61.3 us -> none  [body(): all_rows = lax.all_gather(amps, 'occ', axis=0, tiled=True)]
    ppermute x0 -> x18, waiting for transfers between devices: none -> 31.1 us  [the longest x2 13.3 us: chain_body(): far = lax.ppermute(keep[0] + got[0], 'vir', SWAP)]
    ppermute x0 -> x18, starting transfers between devices: none -> 30.5 us  [the longest x4 9.08 us: chain_body(): total = total + lax.ppermute(total, axis, perm)]
    psum x1 -> x0, blocking collectives: 30.1 us -> none  [body(): total = lax.psum(jnp.sum(residual * residual), ('occ', 'vir', 'rep'))]
    pallas_call x0 -> x10, Pallas kernels: none -> 27.4 us  [the longest x4 13.8 us: next_stage(): pl.pallas_call(kernel, grid_spec=pltpu.PrefetchScalarGridSpec(num_scalar_...]
    dot_general x2 -> x0, matrix products: 26.7 us -> none  [the longest x1 25.2 us: body(): jnp.einsum('ptac,ptcb->pab', cycle_w * live[:, :, None, None], selected_r...]
    all_to_all x2 -> x0, waiting for transfers between devices: 20.6 us -> none  [the longest x1 19 us: body(): lax.all_to_all(mixed, 'occ', split_axis=0, concat_axis=2, tiled=True)]
    all_gather x1 -> x0, blocking collectives: 18.1 us -> none  [body(): full_ladder = lax.all_gather(own_ladder, 'occ', axis=0, tiled=True)]
  transfers between devices with their start and end apart: 4 -> 18, of which waited for: 3 -> 8; matrix products, arithmetic and copies ran while one was open for 3% -> 7% of each run, Pallas kernels for 0% -> 22%
where the time goes in v1:
time: 108 us; the launch traced here: 107 us
  waiting for transfers between devices  31.1 us (29%)
  starting transfers between devices  30.5 us (28%)
  Pallas kernels  27.4 us (25%)
  local copies, waits for them, and re-layouts  14.7 us (14%)
  between operations  3.5 us (3%)
    unnamed x21, local copies, waits for them, and re-layouts  14.4 us
    pallas_call x4, Pallas kernels, next_stage(): pl.pallas_call(kernel, grid_spec=pltpu.PrefetchScalarGridSpec(num_scalar_...  13.8 us
    ppermute x2, waiting for transfers between devices, chain_body(): far = lax.ppermute(keep[0] + got[0], 'vir', SWAP)  13.3 us
    ppermute x2, waiting for transfers between devices, chain_body(): ends = [send(x, perm=ENDS) for x in own]  11.2 us
    ppermute x4, starting transfers between devices, chain_body(): total = total + lax.ppermute(total, axis, perm)  9.08 us
    pallas_call x2, Pallas kernels, first_stage(): pl.pallas_call(kernel, grid_spec=pltpu.PrefetchScalarGridSpec(num_scalar_...  7.28 us
    ppermute x2, starting transfers between devices, chain_body(): ends = [send(x, perm=ENDS) for x in own]  6.85 us
    ppermute x4, waiting for transfers between devices, chain_body(): total = total + lax.ppermute(total, axis, perm)  6.47 us
  transfers between devices with their start and end apart: 18, of which 8 were waited for; matrix products, arithmetic and copies ran while one was open for 7% of the time, Pallas kernels for 22%

profile of v1, /device:TPU:0, one launch (start us, length us, event | category | flops | bytes accessed | tf_op | source)
XLA Modules:
  0.0 107.2 jit_solution(16480621136562051974)
XLA Ops:
  0.6 2.0 %pack.1 = (f32[656,128]{1,0:T(8,128)}, f32[600,128]{1,0:T(8,128)}) custom-call(f32[200,800]{1,0:T(8,128)} %bitcast.23), custom_call_target="tpu_custom_call" | custom-call | tf_op jit(solution)/shard_map/pack/pallas_call | solution.py:91
  2.6 3.0 %collective-permute-start = (f32[656,128]{1,0:T(8,128)}, f32[656,128]{1,0:T(8,128)S(1)}, u32[]{:S(2)}, u32[]{:S(2)}) collective-permute-start(f32[656,128]{1,0:T(8,128)} %get-tuple-element.22.own), channel_id=1, source_target_pairs={{0,4},{4,0},{8,12},{12,8},{1,5},{5,1},{9,13},{13,9},{2,6},{6,2},{1... | collective-permute-start | bytes 1007624 | tf_op jit(solution)/shard_map/ppermute | solution.py:317
  5.6 1.4 %collective-permute-start.3 = (f32[656,128]{1,0:T(8,128)}, f32[656,128]{1,0:T(8,128)}, u32[]{:S(2)}, u32[]{:S(2)}) collective-permute-start(f32[656,128]{1,0:T(8,128)} %get-tuple-element.22.own), channel_id=1, source_target_pairs={{4,8},{8,4},{5,9},{9,5},{6,10},{10,6},{7,11},{11,7},{20,24},{24,20... | collective-permute-start | bytes 1007624 | tf_op jit(solution)/shard_map/ppermute | solution.py:318
  7.0 6.7 %collective-permute-done.near = f32[656,128]{1,0:T(8,128)S(1)} collective-permute-done((f32[656,128]{1,0:T(8,128)}, f32[656,128]{1,0:T(8,128)S(1)}, u32[]{:S(2)}, u32[]{:S(2)}) %collective-permute-start) | collective-permute-done | bytes 335904 | tf_op jit(solution)/shard_map/ppermute | solution.py:317
  13.7 1.4 %collective-permute-start.1 = (f32[656,128]{1,0:T(8,128)S(1)}, f32[656,128]{1,0:T(8,128)}, u32[]{:S(2)}, u32[]{:S(2)}) collective-permute-start(f32[656,128]{1,0:T(8,128)S(1)} %collective-permute-done.near), channel_id=1, source_target_pairs={{4,8},{8,4},{5,9},{9,5},{6,10},{10,6},{7,11},{11,7},{20,24},{24,20... | collective-permute-start | bytes 1007624 | tf_op jit(solution)/shard_map/ppermute | solution.py:320
  15.9 3.8 %collective-permute-start.7 = (f32[600,128]{1,0:T(8,128)}, f32[600,128]{1,0:T(8,128)}, u32[]{:S(2)}, u32[]{:S(2)}) collective-permute-start(f32[600,128]{1,0:T(8,128)} %get-tuple-element.29.own), channel_id=1, source_target_pairs={{0,4},{4,0},{8,12},{12,8},{1,5},{5,1},{9,13},{13,9},{2,6},{6,2},{1... | collective-permute-start | bytes 921608 | tf_op jit(solution)/shard_map/ppermute | solution.py:317
  19.7 1.3 %collective-permute-start.4 = (f32[656,128]{1,0:T(8,128)}, f32[656,128]{1,0:T(8,128)}, u32[]{:S(2)}, u32[]{:S(2)}) collective-permute-start(f32[656,128]{1,0:T(8,128)} %collective-permute-done.3.inner), channel_id=1, source_target_pairs={{4,0},{8,12},{5,1},{9,13},{6,2},{10,14},{7,3},{11,15},{20,16},{24,... | collective-permute-start | bytes 1007624 | tf_op jit(solution)/shard_map/ppermute | solution.py:319
  21.0 1.3 %collective-permute-start.2 = (f32[656,128]{1,0:T(8,128)}, f32[656,128]{1,0:T(8,128)}, u32[]{:S(2)}, u32[]{:S(2)}) collective-permute-start(f32[656,128]{1,0:T(8,128)} %collective-permute-done.1.inner), channel_id=1, source_target_pairs={{4,0},{8,12},{5,1},{9,13},{6,2},{10,14},{7,3},{11,15},{20,16},{24,... | collective-permute-start | bytes 1007624 | tf_op jit(solution)/shard_map/ppermute | solution.py:321
  22.3 1.4 %collective-permute-start.10 = (f32[600,128]{1,0:T(8,128)}, f32[600,128]{1,0:T(8,128)}, u32[]{:S(2)}, u32[]{:S(2)}) collective-permute-start(f32[600,128]{1,0:T(8,128)} %get-tuple-element.29.own), channel_id=1, source_target_pairs={{4,8},{8,4},{5,9},{9,5},{6,10},{10,6},{7,11},{11,7},{20,24},{24,20... | collective-permute-start | bytes 921608 | tf_op jit(solution)/shard_map/ppermute | solution.py:318
  23.7 4.5 %collective-permute-done.7.near = f32[600,128]{1,0:T(8,128)} collective-permute-done((f32[600,128]{1,0:T(8,128)}, f32[600,128]{1,0:T(8,128)}, u32[]{:S(2)}, u32[]{:S(2)}) %collective-permute-start.7) | collective-permute-done | bytes 307232 | tf_op jit(solution)/shard_map/ppermute | solution.py:317
  28.2 1.4 %collective-permute-start.8 = (f32[600,128]{1,0:T(8,128)}, f32[600,128]{1,0:T(8,128)}, u32[]{:S(2)}, u32[]{:S(2)}) collective-permute-start(f32[600,128]{1,0:T(8,128)} %collective-permute-done.7.near), channel_id=1, source_target_pairs={{4,8},{8,4},{5,9},{9,5},{6,10},{10,6},{7,11},{11,7},{20,24},{24,20... | collective-permute-start | bytes 921608 | tf_op jit(solution)/shard_map/ppermute | solution.py:320
  31.6 6.6 %copy.12 = f32[1,8,800,200]{3,2,1,0:T(8,128)} copy(f32[1,8,800,200]{2,3,1,0:T(8,128)} %param.11) | data formatting | bytes 10240000 | tf_op args[2]
  39.1 2.9 %copy-done = f32[1,8,800,200]{3,2,1,0:T(8,128)S(1)} copy-done((f32[1,8,800,200]{3,2,1,0:T(8,128)S(1)}, f32[1,8,800,200]{3,2,1,0:T(8,128)}, u32[]{:S(2)}) %copy-start) | copy-done | bytes 5120024
  41.9 2.2 %sum_by_source.1 = (bf16[4,4,200,200]{3,2,1,0:T(8,128)(2,1)S(1)}, bf16[4,4,200,200]{3,2,1,0:T(8,128)(2,1)S(1)}) custom-call(s32[1,8]{1,0:T(1,128)S(1)} %copy-done.8, s32[1]{0:T(128)S(6)} %copy.16.count_ref, f32[8,800,200]{2,1,0:T(8,128)S(1)} %bitcast.19), custom_call_target="tpu_custom_call" | custom-call | tf_op jit(solution)/shard_map/sum_by_source/pallas_call | solution.py:118
  44.3 1.3 %collective-permute-start.11 = (f32[600,128]{1,0:T(8,128)}, f32[600,128]{1,0:T(8,128)S(1)}, u32[]{:S(2)}, u32[]{:S(2)}) collective-permute-start(f32[600,128]{1,0:T(8,128)} %collective-permute-done.10.inner), channel_id=1, source_target_pairs={{4,0},{8,12},{5,1},{9,13},{6,2},{10,14},{7,3},{11,15},{20,16},{24,... | collective-permute-start | bytes 921608 | tf_op jit(solution)/shard_map/ppermute | solution.py:319
  48.6 3.4 %first_stage.2 = (f32[2,656,128]{2,1,0:T(8,128)S(1)}, f32[2,656,128]{2,1,0:T(8,128)S(1)}) custom-call(s32[9]{0:T(128)S(1)} %stack.43.meta, s32[1,1]{1,0:T(1,128)S(6)} %copy.17.lad_src, f32[1,1]{1,0:T(1,128)S(6)} %copy.18.lad_coef, f32[1]{0:T(128)S(6)} %copy.19.energy, bf16[4,4,200,200]{3,2,1,0:T(8,128)(2,1)S(1)} %get-tuple-element.20.h0.h1.h, ...), custom_call_target="tpu_custom_call" | custom-call | tf_op jit(solution)/shard_map/first_stage/pallas_call | solution.py:175
  52.0 1.4 %collective-permute-start.9 = (f32[600,128]{1,0:T(8,128)}, f32[600,128]{1,0:T(8,128)S(1)}, u32[]{:S(2)}, u32[]{:S(2)}) collective-permute-start(f32[600,128]{1,0:T(8,128)} %collective-permute-done.8.inner), channel_id=1, source_target_pairs={{4,0},{8,12},{5,1},{9,13},{6,2},{10,14},{7,3},{11,15},{20,16},{24,... | collective-permute-start | bytes 921608 | tf_op jit(solution)/shard_map/ppermute | solution.py:321
  53.5 3.8 %next_stage.4 = (f32[2,656,128]{2,1,0:T(8,128)S(1)}, f32[2,656,128]{2,1,0:T(8,128)S(1)}) custom-call(s32[9]{0:T(128)S(1)} %stack.43.meta, s32[1,1]{1,0:T(1,128)S(6)} %copy.17.lad_src, f32[1,1]{1,0:T(1,128)S(6)} %copy.18.lad_coef, bf16[4,4,200,200]{3,2,1,0:T(8,128)(2,1)S(1)} %get-tuple-element.20.h0.h1.h, ...), custom_call_target="tpu_custom_call" | custom-call | tf_op jit(solution)/shard_map/next_stage/pallas_call | solution.py:234
  57.3 3.8 %next_stage.5 = (f32[2,656,128]{2,1,0:T(8,128)S(1)}, f32[2,656,128]{2,1,0:T(8,128)S(1)}) custom-call(s32[9]{0:T(128)S(1)} %stack.43.meta, s32[1,1]{1,0:T(1,128)S(6)} %copy.17.lad_src, f32[1,1]{1,0:T(1,128)S(6)} %copy.18.lad_coef, bf16[4,4,200,200]{3,2,1,0:T(8,128)(2,1)S(1)} %get-tuple-element.20.h0.h1.h, ...), custom_call_target="tpu_custom_call" | custom-call | tf_op jit(solution)/shard_map/next_stage/pallas_call | solution.py:234
  61.2 3.9 %first_stage.3 = (f32[2,600,128]{2,1,0:T(8,128)S(1)}, f32[2,600,128]{2,1,0:T(8,128)S(1)}) custom-call(s32[9]{0:T(128)S(1)} %stack.43.meta, s32[1,1]{1,0:T(1,128)S(6)} %copy.17.lad_src, f32[1,1]{1,0:T(1,128)S(6)} %copy.18.lad_coef, f32[1]{0:T(128)S(6)} %copy.19.energy, bf16[4,4,200,200]{3,2,1,0:T(8,128)(2,1)S(1)} %get-tuple-element.20.h0.h1.h, ...), custom_call_target="tpu_custom_call" | custom-call | tf_op jit(solution)/shard_map/first_stage/pallas_call | solution.py:175
  65.1 3.1 %next_stage.6 = (f32[2,600,128]{2,1,0:T(8,128)S(1)}, f32[2,600,128]{2,1,0:T(8,128)S(1)}) custom-call(s32[9]{0:T(128)S(1)} %stack.43.meta, s32[1,1]{1,0:T(1,128)S(6)} %copy.17.lad_src, f32[1,1]{1,0:T(1,128)S(6)} %copy.18.lad_coef, bf16[4,4,200,200]{3,2,1,0:T(8,128)(2,1)S(1)} %get-tuple-element.20.h0.h1.h, ...), custom_call_target="tpu_custom_call" | custom-call | tf_op jit(solution)/shard_map/next_stage/pallas_call | solution.py:234
  68.2 3.1 %next_stage.7 = (f32[2,600,128]{2,1,0:T(8,128)S(1)}, f32[2,600,128]{2,1,0:T(8,128)S(1)}) custom-call(s32[9]{0:T(128)S(1)} %stack.43.meta, s32[1,1]{1,0:T(1,128)S(6)} %copy.17.lad_src, f32[1,1]{1,0:T(1,128)S(6)} %copy.18.lad_coef, bf16[4,4,200,200]{3,2,1,0:T(8,128)(2,1)S(1)} %get-tuple-element.20.h0.h1.h, ...), custom_call_target="tpu_custom_call" | custom-call | tf_op jit(solution)/shard_map/next_stage/pallas_call | solution.py:234
  71.9 1.6 %collective-permute-start.6 = (f32[656,128]{1,0:T(8,128)S(1)}, f32[656,128]{1,0:T(8,128)S(1)}, u32[]{:S(2)}, u32[]{:S(2)}) collective-permute-start(f32[656,128]{1,0:T(8,128)S(1)} %fusion), channel_id=1, source_target_pairs={{0,2},{2,0},{1,3},{3,1},{4,6},{6,4},{5,7},{7,5},{8,10},{10,8},{9,1... | collective-permute-start | bytes 1007624 | tf_op jit(solution)/shard_map/ppermute | solution.py:332
  73.6 1.6 %collective-permute-start.13 = (f32[600,128]{1,0:T(8,128)S(1)}, f32[600,128]{1,0:T(8,128)S(1)}, u32[]{:S(2)}, u32[]{:S(2)}) collective-permute-start(f32[600,128]{1,0:T(8,128)S(1)} %fusion.1), channel_id=1, source_target_pairs={{0,2},{2,0},{1,3},{3,1},{4,6},{6,4},{5,7},{7,5},{8,10},{10,8},{9,1... | collective-permute-start | bytes 921608 | tf_op jit(solution)/shard_map/ppermute | solution.py:332
  75.2 13.3 %collective-permute-done.13.refs_5_ = f32[600,128]{1,0:T(8,128)S(1)} collective-permute-done((f32[600,128]{1,0:T(8,128)S(1)}, f32[600,128]{1,0:T(8,128)S(1)}, u32[]{:S(2)}, u32[]{:S(2)}) %collective-permute-start.13) | collective-permute-done | bytes 307232 | tf_op jit(solution)/shard_map/ppermute | solution.py:332
  89.5 1.2 %collective-permute-done.14 = f32[8,128]{1,0:T(8,128)S(1)} collective-permute-done((f32[8,128]{1,0:T(8,128)S(1)}, f32[8,128]{1,0:T(8,128)S(1)}, u32[]{:S(2)}, u32[]{:S(2)}) %collective-permute-start.14) | collective-permute-done | bytes 4128 | tf_op jit(solution)/shard_map/ppermute | solution.py:336
  90.6 1.5 %collective-permute-start.15 = (f32[8,128]{1,0:T(8,128)S(1)}, f32[8,128]{1,0:T(8,128)S(1)}, u32[]{:S(2)}, u32[]{:S(2)}) collective-permute-start(f32[8,128]{1,0:T(8,128)S(1)} %add.49), channel_id=1, source_target_pairs={{0,2},{2,0},{1,3},{3,1},{4,6},{6,4},{5,7},{7,5},{8,10},{10,8},{9,1... | collective-permute-start | bytes 12296 | tf_op jit(solution)/shard_map/ppermute | solution.py:336
  92.1 2.1 %collective-permute-done.15 = f32[8,128]{1,0:T(8,128)S(1)} collective-permute-done((f32[8,128]{1,0:T(8,128)S(1)}, f32[8,128]{1,0:T(8,128)S(1)}, u32[]{:S(2)}, u32[]{:S(2)}) %collective-permute-start.15) | collective-permute-done | bytes 4128 | tf_op jit(solution)/shard_map/ppermute | solution.py:336
  94.3 4.6 %collective-permute-start.16 = (f32[8,128]{1,0:T(8,128)S(1)}, f32[8,128]{1,0:T(8,128)S(1)}, u32[]{:S(2)}, u32[]{:S(2)}) collective-permute-start(f32[8,128]{1,0:T(8,128)S(1)} %add.50), channel_id=1, source_target_pairs={{0,4},{4,0},{8,12},{12,8},{1,5},{5,1},{9,13},{13,9},{2,6},{6,2},{1... | collective-permute-start | bytes 12296 | tf_op jit(solution)/shard_map/ppermute | solution.py:336
  98.8 1.6 %collective-permute-done.16 = f32[8,128]{1,0:T(8,128)S(1)} collective-permute-done((f32[8,128]{1,0:T(8,128)S(1)}, f32[8,128]{1,0:T(8,128)S(1)}, u32[]{:S(2)}, u32[]{:S(2)}) %collective-permute-start.16) | collective-permute-done | bytes 4128 | tf_op jit(solution)/shard_map/ppermute | solution.py:336
  100.4 3.0 %collective-permute-start.17 = (f32[8,128]{1,0:T(8,128)S(1)}, f32[8,128]{1,0:T(8,128)S(1)}, u32[]{:S(2)}, u32[]{:S(2)}) collective-permute-start(f32[8,128]{1,0:T(8,128)S(1)} %add.51), channel_id=1, source_target_pairs={{0,8},{8,0},{4,12},{12,4},{1,9},{9,1},{5,13},{13,5},{2,10},{10,2},... | collective-permute-start | bytes 12296 | tf_op jit(solution)/shard_map/ppermute | solution.py:336
  103.5 1.6 %collective-permute-done.17 = f32[8,128]{1,0:T(8,128)S(1)} collective-permute-done((f32[8,128]{1,0:T(8,128)S(1)}, f32[8,128]{1,0:T(8,128)S(1)}, u32[]{:S(2)}, u32[]{:S(2)}) %collective-permute-start.17) | collective-permute-done | bytes 4128 | tf_op jit(solution)/shard_map/ppermute | solution.py:336
  (45 shorter events, 8.1 us)
Async XLA Ops:
  2.6 11.1 %collective-permute-start = (f32[656,128]{1,0:T(8,128)}, f32[656,128]{1,0:T(8,128)S(1)}, u32[]{:S(2)}, u32[]{:S(2)}) collective-permute-start(f32[656,128]{1,0:T(8,128)} %get-tuple-element.22.own), channel_id=1, source_target_pairs={{0,4},{4,0},{8,12},{12,8},{1,5},{5,1},{9,13},{13,9},{2,6},{6,2},{1... | collective-permute-start | bytes 1007624 | tf_op jit(solution)/shard_map/ppermute | solution.py:317
  5.6 14.1 %collective-permute-start.3 = (f32[656,128]{1,0:T(8,128)}, f32[656,128]{1,0:T(8,128)}, u32[]{:S(2)}, u32[]{:S(2)}) collective-permute-start(f32[656,128]{1,0:T(8,128)} %get-tuple-element.22.own), channel_id=1, source_target_pairs={{4,8},{8,4},{5,9},{9,5},{6,10},{10,6},{7,11},{11,7},{20,24},{24,20... | collective-permute-start | bytes 1007624 | tf_op jit(solution)/shard_map/ppermute | solution.py:318
  13.7 7.2 %collective-permute-start.1 = (f32[656,128]{1,0:T(8,128)S(1)}, f32[656,128]{1,0:T(8,128)}, u32[]{:S(2)}, u32[]{:S(2)}) collective-permute-start(f32[656,128]{1,0:T(8,128)S(1)} %collective-permute-done.near), channel_id=1, source_target_pairs={{4,8},{8,4},{5,9},{9,5},{6,10},{10,6},{7,11},{11,7},{20,24},{24,20... | collective-permute-start | bytes 1007624 | tf_op jit(solution)/shard_map/ppermute | solution.py:320
  15.1 0.7 copy-start.5
  15.9 12.3 %collective-permute-start.7 = (f32[600,128]{1,0:T(8,128)}, f32[600,128]{1,0:T(8,128)}, u32[]{:S(2)}, u32[]{:S(2)}) collective-permute-start(f32[600,128]{1,0:T(8,128)} %get-tuple-element.29.own), channel_id=1, source_target_pairs={{0,4},{4,0},{8,12},{12,8},{1,5},{5,1},{9,13},{13,9},{2,6},{6,2},{1... | collective-permute-start | bytes 921608 | tf_op jit(solution)/shard_map/ppermute | solution.py:317
  19.7 33.8 %collective-permute-start.4 = (f32[656,128]{1,0:T(8,128)}, f32[656,128]{1,0:T(8,128)}, u32[]{:S(2)}, u32[]{:S(2)}) collective-permute-start(f32[656,128]{1,0:T(8,128)} %collective-permute-done.3.inner), channel_id=1, source_target_pairs={{4,0},{8,12},{5,1},{9,13},{6,2},{10,14},{7,3},{11,15},{20,16},{24,... | collective-permute-start | bytes 1007624 | tf_op jit(solution)/shard_map/ppermute | solution.py:319
  21.0 36.3 %collective-permute-start.2 = (f32[656,128]{1,0:T(8,128)}, f32[656,128]{1,0:T(8,128)}, u32[]{:S(2)}, u32[]{:S(2)}) collective-permute-start(f32[656,128]{1,0:T(8,128)} %collective-permute-done.1.inner), channel_id=1, source_target_pairs={{4,0},{8,12},{5,1},{9,13},{6,2},{10,14},{7,3},{11,15},{20,16},{24,... | collective-permute-start | bytes 1007624 | tf_op jit(solution)/shard_map/ppermute | solution.py:321
  22.3 22.0 %collective-permute-start.10 = (f32[600,128]{1,0:T(8,128)}, f32[600,128]{1,0:T(8,128)}, u32[]{:S(2)}, u32[]{:S(2)}) collective-permute-start(f32[600,128]{1,0:T(8,128)} %get-tuple-element.29.own), channel_id=1, source_target_pairs={{4,8},{8,4},{5,9},{9,5},{6,10},{10,6},{7,11},{11,7},{20,24},{24,20... | collective-permute-start | bytes 921608 | tf_op jit(solution)/shard_map/ppermute | solution.py:318
  28.2 23.8 %collective-permute-start.8 = (f32[600,128]{1,0:T(8,128)}, f32[600,128]{1,0:T(8,128)}, u32[]{:S(2)}, u32[]{:S(2)}) collective-permute-start(f32[600,128]{1,0:T(8,128)} %collective-permute-done.7.near), channel_id=1, source_target_pairs={{4,8},{8,4},{5,9},{9,5},{6,10},{10,6},{7,11},{11,7},{20,24},{24,20... | collective-permute-start | bytes 921608 | tf_op jit(solution)/shard_map/ppermute | solution.py:320
  31.5 7.3 %copy-start.9 = (f32[800]{0:T(1024)S(1)}, f32[800]{0:T(1024)}, u32[]{:S(2)}) copy-start(f32[800]{0:T(1024)} %param.16) | copy-start | bytes 9604
  31.5 7.5 %copy-start.8 = (s32[1,8]{1,0:T(1,128)S(1)}, s32[1,8]{1,0:T(1,128)}, u32[]{:S(2)}) copy-start(s32[1,8]{1,0:T(1,128)} %src_ref.1) | copy-start | bytes 100
  39.1 2.9 %copy-start = (f32[1,8,800,200]{3,2,1,0:T(8,128)S(1)}, f32[1,8,800,200]{3,2,1,0:T(8,128)}, u32[]{:S(2)}) copy-start(f32[1,8,800,200]{3,2,1,0:T(8,128)} %copy.12) | copy-start | bytes 15360004
  44.3 20.8 %collective-permute-start.11 = (f32[600,128]{1,0:T(8,128)}, f32[600,128]{1,0:T(8,128)S(1)}, u32[]{:S(2)}, u32[]{:S(2)}) collective-permute-start(f32[600,128]{1,0:T(8,128)} %collective-permute-done.10.inner), channel_id=1, source_target_pairs={{4,0},{8,12},{5,1},{9,13},{6,2},{10,14},{7,3},{11,15},{20,16},{24,... | collective-permute-start | bytes 921608 | tf_op jit(solution)/shard_map/ppermute | solution.py:319
  45.6 1.1 %copy-start.1 = (f32[1,200,800]{2,1,0:T(8,128)S(1)}, f32[1,200,800]{2,1,0:T(8,128)}, u32[]{:S(2)}) copy-start(f32[1,200,800]{2,1,0:T(8,128)} %param.10) | copy-start | bytes 1920004
  46.7 1.0 copy-start.4
  47.7 1.0 copy-start.6
  52.0 9.2 %copy-start.2 = (f32[1,200,800]{2,1,0:T(8,128)S(1)}, f32[1,200,800]{2,1,0:T(8,128)}, u32[]{:S(2)}) copy-start(f32[1,200,800]{2,1,0:T(8,128)} %param.10) | copy-start | bytes 1920004
  52.0 9.1 %copy-start.7 = (f32[600,128]{1,0:T(8,128)S(1)}, f32[600,128]{1,0:T(8,128)}, u32[]{:S(2)}) copy-start(f32[600,128]{1,0:T(8,128)} %get-tuple-element.29.own) | copy-start | bytes 921604
  52.0 16.2 %collective-permute-start.9 = (f32[600,128]{1,0:T(8,128)}, f32[600,128]{1,0:T(8,128)S(1)}, u32[]{:S(2)}, u32[]{:S(2)}) collective-permute-start(f32[600,128]{1,0:T(8,128)} %collective-permute-done.8.inner), channel_id=1, source_target_pairs={{4,0},{8,12},{5,1},{9,13},{6,2},{10,14},{7,3},{11,15},{20,16},{24,... | collective-permute-start | bytes 921608 | tf_op jit(solution)/shard_map/ppermute | solution.py:321
  61.1 10.8 %collective-permute-start.5 = (f32[2,656,128]{2,1,0:T(8,128)S(1)}, f32[2,656,128]{2,1,0:T(8,128)S(1)}, u32[]{:S(2)}, u32[]{:S(2)}) collective-permute-start(f32[2,656,128]{2,1,0:T(8,128)S(1)} %get-tuple-element.28), channel_id=1, source_target_pairs={{0,1},{1,0},{2,3},{3,2},{4,5},{5,4},{6,7},{7,6},{8,9},{9,8},{10,11... | collective-permute-start | bytes 2015240 | tf_op jit(solution)/shard_map/ppermute | solution.py:331
  71.4 2.2 %collective-permute-start.12 = (f32[2,600,128]{2,1,0:T(8,128)S(1)}, f32[2,600,128]{2,1,0:T(8,128)S(1)}, u32[]{:S(2)}, u32[]{:S(2)}) collective-permute-start(f32[2,600,128]{2,1,0:T(8,128)S(1)} %get-tuple-element.35), channel_id=1, source_target_pairs={{0,1},{1,0},{2,3},{3,2},{4,5},{5,4},{6,7},{7,6},{8,9},{9,8},{10,11... | collective-permute-start | bytes 1843208 | tf_op jit(solution)/shard_map/ppermute | solution.py:331
  71.9 16.5 %collective-permute-start.6 = (f32[656,128]{1,0:T(8,128)S(1)}, f32[656,128]{1,0:T(8,128)S(1)}, u32[]{:S(2)}, u32[]{:S(2)}) collective-permute-start(f32[656,128]{1,0:T(8,128)S(1)} %fusion), channel_id=1, source_target_pairs={{0,2},{2,0},{1,3},{3,1},{4,6},{6,4},{5,7},{7,5},{8,10},{10,8},{9,1... | collective-permute-start | bytes 1007624 | tf_op jit(solution)/shard_map/ppermute | solution.py:332
  73.6 14.8 %collective-permute-start.13 = (f32[600,128]{1,0:T(8,128)S(1)}, f32[600,128]{1,0:T(8,128)S(1)}, u32[]{:S(2)}, u32[]{:S(2)}) collective-permute-start(f32[600,128]{1,0:T(8,128)S(1)} %fusion.1), channel_id=1, source_target_pairs={{0,2},{2,0},{1,3},{3,1},{4,6},{6,4},{5,7},{7,5},{8,10},{10,8},{9,1... | collective-permute-start | bytes 921608 | tf_op jit(solution)/shard_map/ppermute | solution.py:332
  89.5 1.2 %collective-permute-start.14 = (f32[8,128]{1,0:T(8,128)S(1)}, f32[8,128]{1,0:T(8,128)S(1)}, u32[]{:S(2)}, u32[]{:S(2)}) collective-permute-start(f32[8,128]{1,0:T(8,128)S(1)} %get-tuple-element.37), channel_id=1, source_target_pairs={{0,1},{1,0},{2,3},{3,2},{4,5},{5,4},{6,7},{7,6},{8,9},{9,8},{10,11... | collective-permute-start | bytes 12296 | tf_op jit(solution)/shard_map/ppermute | solution.py:336
  90.6 3.6 %collective-permute-start.15 = (f32[8,128]{1,0:T(8,128)S(1)}, f32[8,128]{1,0:T(8,128)S(1)}, u32[]{:S(2)}, u32[]{:S(2)}) collective-permute-start(f32[8,128]{1,0:T(8,128)S(1)} %add.49), channel_id=1, source_target_pairs={{0,2},{2,0},{1,3},{3,1},{4,6},{6,4},{5,7},{7,5},{8,10},{10,8},{9,1... | collective-permute-start | bytes 12296 | tf_op jit(solution)/shard_map/ppermute | solution.py:336
  94.3 6.2 %collective-permute-start.16 = (f32[8,128]{1,0:T(8,128)S(1)}, f32[8,128]{1,0:T(8,128)S(1)}, u32[]{:S(2)}, u32[]{:S(2)}) collective-permute-start(f32[8,128]{1,0:T(8,128)S(1)} %add.50), channel_id=1, source_target_pairs={{0,4},{4,0},{8,12},{12,8},{1,5},{5,1},{9,13},{13,9},{2,6},{6,2},{1... | collective-permute-start | bytes 12296 | tf_op jit(solution)/shard_map/ppermute | solution.py:336
  100.4 4.6 %collective-permute-start.17 = (f32[8,128]{1,0:T(8,128)S(1)}, f32[8,128]{1,0:T(8,128)S(1)}, u32[]{:S(2)}, u32[]{:S(2)}) collective-permute-start(f32[8,128]{1,0:T(8,128)S(1)} %add.51), channel_id=1, source_target_pairs={{0,8},{8,0},{4,12},{12,4},{1,9},{9,1},{5,13},{13,5},{2,10},{10,2},... | collective-permute-start | bytes 12296 | tf_op jit(solution)/shard_map/ppermute | solution.py:336
  105.0 1.1 %copy-start.3 = (f32[200,800]{1,0:T(8,128)S(1)}, f32[200,800]{1,0:T(8,128)}, u32[]{:S(2)}) copy-start(f32[200,800]{1,0:T(8,128)} %get-tuple-element.36.residual) | copy-start | bytes 1920004

commit v2 on v0

v2 whole, which is shorter than its diff:
```python
import functools
import math

import jax
import jax.numpy as jnp
from jax import lax
from jax.experimental import pallas as pl
from jax.experimental.pallas import tpu as pltpu
from jax.sharding import PartitionSpec as P

clip_level = 0.5
LANES = 128
SMEM = pl.BlockSpec(memory_space=pltpu.SMEM)
VMEM = pl.BlockSpec(memory_space=pltpu.VMEM)
HBM = pl.BlockSpec(memory_space=pl.ANY)
SWAP = [(0, 1), (1, 0)]
NEAR = [(0, 1), (1, 0), (2, 3), (3, 2)]
FAR = [(0, 2), (2, 0), (1, 3), (3, 1)]
VMEM_MIB = 20
TILES_FIRST = 2
MERGE = True
FORCE = True


def limit(n):
    return pltpu.CompilerParams(vmem_limit_bytes=n << 20)


class Chunk:
    def __init__(self, rows, width, first, count, rest, start):
        self.rows, self.first, self.count, self.start = rows, first, count, start
        self.rest = width % LANES if rest else 0
        self.at = width - self.rest
        self.group = -(-rows // 32) * 8
        self.length = rows * count + (self.group if self.rest else 0)
        self.width = LANES * count + self.rest

    def take(self, ref):
        parts = [ref[:, self.first * LANES : (self.first + self.count) * LANES]]
        if self.rest:
            parts.append(ref[:, self.at : self.at + self.rest])
        return jnp.concatenate(parts, axis=1) if len(parts) > 1 else parts[0]

    def put(self, ref, value):
        span = LANES * self.count
        ref[:, self.first * LANES : self.first * LANES + span] = value[:, :span]
        if self.rest:
            ref[:, self.at : self.at + self.rest] = value[:, span:]

    def load(self, read):
        parts = [read(t * self.rows, self.rows) for t in range(self.count)]
        if self.rest:
            packed = read(self.count * self.rows, self.group)
            rest = [packed[:, g * self.rest : (g + 1) * self.rest] for g in range(4)]
            parts.append(jnp.concatenate(rest, axis=0)[: self.rows])
        return jnp.concatenate(parts, axis=1)

    def store(self, write, value):
        for t in range(self.count):
            write(t * self.rows, self.rows, value[:, t * LANES : (t + 1) * LANES])
        if self.rest:
            rest = value[:, self.count * LANES :]
            short = 4 * self.group - self.rows
            rest = jnp.concatenate([rest, jnp.zeros((short, self.rest), rest.dtype)], axis=0)
            groups = [rest[g * self.group : (g + 1) * self.group] for g in range(4)]
            write(self.count * self.rows, self.group, jnp.concatenate(groups, axis=1))


def reader(ref, lead=(), skip=0):
    return lambda start, size: ref[(*lead, pl.ds(skip + start, size), slice(None))]


def writer(ref, lead=(), skip=0):
    def write(start, size, value):
        ref[(*lead, pl.ds(skip + start, size), slice(None))] = value

    return write


def split(value):
    high = value.astype(jnp.bfloat16)
    return high, (value - high.astype(jnp.float32)).astype(jnp.bfloat16)


def product(high, low, x_high, x_low):
    dot = functools.partial(jnp.dot, preferred_element_type=jnp.float32)
    return dot(high, x_high) + (dot(low, x_high) + dot(high, x_low))


def pack(amps, chunks):
    def kernel(amps_ref, out):
        for chunk in chunks:
            chunk.store(writer(out, skip=chunk.start), chunk.take(amps_ref))

    length = sum(chunk.length for chunk in chunks)
    return pl.pallas_call(
        kernel,
        in_specs=[VMEM],
        out_specs=VMEM,
        out_shape=jax.ShapeDtypeStruct((length, LANES), jnp.float32),
        name="pack",
    )(amps)


def sum_by_source(meta, cycle_w, cycle_src, cycle_count, npair, blocks):
    nring, depth, height = cycle_w.shape
    rows = height // blocks
    tall, deep = -(-height // LANES) * LANES, -(-depth // LANES) * LANES

    def kernel(meta, src, count, w_ref, high_ref, low_ref, total, turned, ordered):
        s = pl.program_id(0)

        @pl.when(s == 0)
        def _():
            total[...] = jnp.zeros_like(total)

        @pl.when(s < count[0])
        def _():
            source = src[s]
            total[source, :depth, :height] = total[source, :depth, :height] + w_ref[0]

        @pl.when(s == nring - 1)
        def _():
            for m in range(npair):
                turned[...] = total[m].T
                for j in range(blocks):
                    start = pl.multiple_of(meta[4 + j] * rows, 8)
                    ordered[j * rows : (j + 1) * rows] = turned[pl.ds(start, rows), :depth]
                for h in range(2):
                    high_ref[m, h], low_ref[m, h] = split(ordered[h * height // 2 : (h + 1) * height // 2])

    block = pl.BlockSpec((npair, 2, height // 2, depth), lambda s, *_: (0, 0, 0, 0))
    shape = jax.ShapeDtypeStruct((npair, 2, height // 2, depth), jnp.bfloat16)
    return pl.pallas_call(
        kernel,
        grid_spec=pltpu.PrefetchScalarGridSpec(
            num_scalar_prefetch=3,
            grid=(nring,),
            in_specs=[
                pl.BlockSpec(
                    (1, depth, height), lambda s, meta, src, count: (jnp.minimum(s, count[0] - 1), 0, 0)
                )
            ],
            out_specs=[block, block],
            scratch_shapes=[
                pltpu.VMEM((npair, deep, tall), jnp.float32),
                pltpu.VMEM((tall, deep), jnp.float32),
                pltpu.VMEM((height, depth), jnp.float32),
            ],
        ),
        out_shape=[shape, shape],
        compiler_params=limit(VMEM_MIB),
        name="sum_by_source",
    )(meta, cycle_src.reshape(-1), cycle_count, cycle_w)


def ladder_weight(source, lad_src, lad_coef):
    weight = jnp.float32(0)
    for entry in range(lad_src.shape[1]):
        weight = weight + jnp.where(lad_src[0, entry] == source, lad_coef[0, entry], 0.0)
    return weight


def own_products(chunks, meta, lad_src, lad_coef, energy, weights, amps, drive, eps_row, eps_col):
    high, low = weights
    _, _, height, _ = high.shape
    rows = drive.shape[0]

    def kernel(meta, lad_src, lad_coef, energy, high, low, amps, drive, eps_row, eps_col, inverse, *outs):
        denom = eps_col[...] + eps_row[...] - energy[0]
        inverse[...] = 1.0 / denom
        weight = ladder_weight(meta[0], lad_src, lad_coef)
        for chunk, out in zip(chunks, outs, strict=True):
            mine = chunk.load(reader(amps, skip=chunk.start))
            x_high, x_low = split(mine)
            for h in range(2):
                out[h] = product(high[meta[0], h], low[meta[0], h], x_high, x_low)
            denom = eps_col[...] + chunk.take(eps_row) - energy[0]
            base = chunk.take(drive) - denom * mine + weight * mine
            out[1, height - rows :] = out[1, height - rows :] + base

    return pl.pallas_call(
        kernel,
        in_specs=[SMEM] * 4 + [VMEM] * 6,
        out_specs=[VMEM] * (1 + len(chunks)),
        out_shape=[jax.ShapeDtypeStruct(drive.shape, jnp.float32)]
        + [jax.ShapeDtypeStruct((2, height, c.width), jnp.float32) for c in chunks],
        compiler_params=limit(VMEM_MIB),
        name="own_products",
    )(meta, lad_src, lad_coef, energy, high, low, amps, drive, eps_row, eps_col)


def add_products(chunks, ks, meta, lad_src, lad_coef, weights, packed, sums):
    high, low = weights
    _, _, height, _ = high.shape
    rows = chunks[0].rows
    n = len(ks)

    def kernel(meta, lad_src, lad_coef, high, low, *refs):
        packed, refs = refs[:n], refs[n:]
        for c, chunk in enumerate(chunks):
            sums, out = refs[c :: len(chunks)]
            amps = [chunk.load(reader(ref, skip=chunk.start)) for ref in packed]
            parts = [split(x) for x in amps]
            for h in range(2):
                value = sums[h]
                for k, (x_high, x_low) in zip(ks, parts, strict=True):
                    value = value + product(high[meta[k], h], low[meta[k], h], x_high, x_low)
                out[h] = value
            value = out[1, height - rows :]
            for k, x in zip(ks, amps, strict=True):
                value = value + ladder_weight(meta[k], lad_src, lad_coef) * x
            out[1, height - rows :] = value

    return pl.pallas_call(
        kernel,
        in_specs=[SMEM] * 3 + [VMEM] * (2 + n + len(chunks)),
        out_specs=[VMEM] * len(chunks),
        out_shape=[jax.ShapeDtypeStruct(s.shape, jnp.float32) for s in sums],
        compiler_params=limit(VMEM_MIB),
        name="add_products",
    )(meta, lad_src, lad_coef, high, low, *packed, *sums)


def last_product(chunk, meta, lad_src, lad_coef, weights, amps, sums):
    high, low = weights
    npair, _, height, _ = high.shape
    rows = chunk.rows

    def kernel(meta, lad_src, lad_coef, high, low, amps, sums, *outs):
        k = meta[npair - 1]
        x = chunk.load(reader(amps))
        x_high, x_low = split(x)
        for h in range(2):
            value = sums[h] + product(high[k, h], low[k, h], x_high, x_low)
            for i in range(2):
                part = value[i * rows : (i + 1) * rows]
                if h and i:
                    part = part + ladder_weight(k, lad_src, lad_coef) * x
                chunk.store(writer(outs[2 * h + i]), part)

    return pl.pallas_call(
        kernel,
        in_specs=[SMEM] * 3 + [VMEM] * 4,
        out_specs=[VMEM] * 4,
        out_shape=[jax.ShapeDtypeStruct((chunk.length, LANES), jnp.float32)] * 4,
        compiler_params=limit(VMEM_MIB),
        name="last_product",
    )(meta, lad_src, lad_coef, high, low, amps, sums)


def finish(chunks, done, pieces, shape, copies):
    def kernel(*refs):
        *refs, out, total_ref = refs
        total = jnp.zeros((1, LANES), jnp.float32)
        for i, chunk in enumerate(chunks):
            parts = refs[i : i + 1] if i < len(done) else refs[len(done) + 3 * (i - len(done)) :][:3]
            value = sum(chunk.load(reader(ref)) for ref in parts)
            chunk.put(out, value)
            total = total + jnp.sum(value * value)
        total_ref[...] = jnp.broadcast_to(total, total_ref.shape)

    refs = [*done, *pieces]
    return pl.pallas_call(
        kernel,
        in_specs=[VMEM] * len(refs),
        out_specs=[VMEM, VMEM],
        out_shape=[
            jax.ShapeDtypeStruct(shape, jnp.float32),
            jax.ShapeDtypeStruct((copies, 8, LANES), jnp.float32),
        ],
        compiler_params=limit(VMEM_MIB),
        name="finish",
    )(*refs)


def jacobi(residual, total, inverse, bound):
    def kernel(residual, total, inverse, residual_out, update_out, update, sems):
        whole = pltpu.make_async_copy(residual, residual_out, sems.at[0])
        whole.start()
        scale = jnp.minimum(1.0, bound / jnp.sqrt(jnp.sum(total[...], axis=0)[0:1, 0:1]))
        update[...] = (scale * residual[...]) * inverse[...]
        moved = pltpu.make_async_copy(update, update_out, sems.at[1])
        moved.start()
        whole.wait()
        moved.wait()

    shape = jax.ShapeDtypeStruct(residual.shape, jnp.float32)
    return pl.pallas_call(
        kernel,
        in_specs=[VMEM, VMEM, VMEM],
        out_specs=[HBM, HBM],
        out_shape=[shape, shape],
        scratch_shapes=[pltpu.VMEM(residual.shape, jnp.float32), pltpu.SemaphoreType.DMA((2,))],
        compiler_params=limit(VMEM_MIB),
        name="jacobi",
    )(residual, total, inverse)


def chain_body(amps, drive, cycle_w, cycle_src, cycle_count, ladder_src, ladder_coef, eps_vir, pair_energy):
    _, rows, width = amps.shape
    npair, blocks = lax.axis_size("occ"), width // rows
    place, chip, core = lax.axis_index("occ"), lax.axis_index("vir"), lax.axis_index("rep")
    order = [
        place,
        place ^ 1,
        place ^ 2,
        place ^ 3,
        2 * (1 - chip) + (1 - core),
        2 * chip + (1 - core),
        2 * (1 - chip) + core,
        2 * chip + core,
    ]
    meta = jnp.stack([jnp.asarray(v, jnp.int32) for v in order])
    eps_row = eps_vir.reshape(1, width)
    eps_col = lax.dynamic_slice_in_dim(eps_vir, (2 * chip + core) * rows, rows).reshape(rows, 1)

    tiles = width // LANES
    half = TILES_FIRST
    first = Chunk(rows, width, 0, half, True, 0)
    chunks = [first, Chunk(rows, width, half, tiles - half, False, first.length)]
    own = pack(amps[0], chunks)
    far_amps = lax.ppermute(own, "occ", FAR)
    near_amps = lax.ppermute(own, "occ", NEAR)
    weights = sum_by_source(meta, jnp.swapaxes(cycle_w[0], 1, 2), cycle_src, cycle_count, npair, blocks)
    inverse, *sums = own_products(
        chunks, meta, ladder_src, ladder_coef, pair_energy, weights, own, drive[0], eps_row, eps_col
    )
    far_amps, sums = lax.optimization_barrier((far_amps, sums))
    last_amps = [lax.ppermute(far_amps[c.start : c.start + c.length], "occ", NEAR) for c in chunks]
    if MERGE:
        sums = add_products(
            chunks, (1, 2), meta, ladder_src, ladder_coef, weights, (near_amps, far_amps), sums
        )

    done, pieces = [], []
    for i, chunk in enumerate(chunks):
        if not MERGE:
            sums[i] = add_products(
                [chunk], (1, 2), meta, ladder_src, ladder_coef, weights, (near_amps, far_amps), [sums[i]]
            )[0]
        away = last_product(chunk, meta, ladder_src, ladder_coef, weights, last_amps[i], sums[i])
        away, keep = away[:2], away[2:]
        got = [lax.ppermute(x, "rep", SWAP) for x in away]
        for_far = keep[0] + got[0]
        if i and FORCE:
            done, for_far = lax.optimization_barrier((done, for_far))
        far = lax.ppermute(for_far, "vir", SWAP)
        if i < len(chunks) - 1 and FORCE:
            done.append(keep[1] + got[1] + far)
        else:
            pieces += [keep[1], got[1], far]
    residual, total = finish(chunks, done, pieces, (rows, width), npair * blocks)
    total = lax.all_to_all(total, ("occ", "vir", "rep"), split_axis=0, concat_axis=0, tiled=True)
    residual, update = jacobi(residual, total, inverse, clip_level * width * math.sqrt(npair))
    return residual[None], update[None]


def any_body(amps, drive, cycle_w, cycle_src, cycle_count, ladder_src, ladder_coef, eps_vir, pair_energy):
    largest_value = lax.Precision.HIGHEST
    pairs_per_unit, rows, width = amps.shape
    nring = cycle_w.shape[1]
    npair = pairs_per_unit * lax.axis_size("occ")
    all_rows = lax.all_gather(amps, "occ", axis=0, tiled=True)
    ladder = jnp.sum(ladder_coef[:, :, None, None] * all_rows[ladder_src], axis=1)
    selected_rows = jnp.take(all_rows, cycle_src.reshape(-1), axis=0).reshape(
        pairs_per_unit, nring, rows, width
    )
    live = (jnp.arange(nring)[None, :] < cycle_count[:, None]).astype(jnp.float32)
    partial_value = jnp.einsum(
        "ptac,ptcb->pab", cycle_w * live[:, :, None, None], selected_rows, precision=largest_value
    )
    cycle = lax.psum_scatter(partial_value, ("vir", "rep"), scatter_dimension=1, tiled=True)
    first_row = lax.axis_index(("vir", "rep")) * rows
    eps_rows = lax.dynamic_slice_in_dim(eps_vir, first_row, rows)
    denom = eps_rows[None, :, None] + eps_vir[None, None, :] - pair_energy[:, None, None]
    residual = drive + cycle + ladder - denom * amps
    total = lax.psum(jnp.sum(residual * residual), ("occ", "vir", "rep"))
    scale = jnp.minimum(1.0, clip_level * width * math.sqrt(npair) / jnp.sqrt(total))
    return residual, scale * residual / denom


def body(*args):
    amps, cycle_w = args[0], args[2]
    pairs_per_unit, rows, width = amps.shape
    chain = (
        pairs_per_unit == 1
        and (lax.axis_size("occ"), lax.axis_size("vir"), lax.axis_size("rep")) == (4, 2, 2)
        and cycle_w.shape[1] >= 4
        and rows % 8 == 0
        and width % LANES == LANES // 4
        and width >= 2 * LANES
    )
    return (chain_body if chain else any_body)(*args)


def solution(mesh):
    in_specs = (
        P(("groups", "occ"), ("vir", "rep"), None),
        P(("groups", "occ"), ("vir", "rep"), None),
        P(("groups", "occ"), None, None, ("vir", "rep")),
        P(("groups", "occ"), None),
        P(("groups", "occ")),
        P(("groups", "occ"), None),
        P(("groups", "occ"), None),
        P("groups"),
        P(("groups", "occ")),
    )
    out_specs = (
        P(("groups", "occ"), ("vir", "rep"), None),
        P(("groups", "occ"), ("vir", "rep"), None),
    )
    return jax.shard_map(body, mesh=mesh, in_specs=in_specs, out_specs=out_specs, check_vma=False)
```

time: 198 us -> 80.8 us (0.41)
  waiting for transfers between devices: 82.6 us -> 31.5 us
  blocking collectives: 48.2 us -> 13.2 us
  matrix products: 26.7 us -> 0 us
  Pallas kernels: 0 us -> 15.1 us
  between operations: 17.4 us -> 3.35 us
  other arithmetic: 4.69 us -> 0.12 us
  local copies, waits for them, and re-layouts: 9.46 us -> 5 us
  starting transfers between devices: 8.39 us -> 12.1 us
    all_gather x1 -> x0, waiting for transfers between devices: 61.3 us -> none  [body(): all_rows = lax.all_gather(amps, 'occ', axis=0, tiled=True)]
    ppermute x0 -> x10, waiting for transfers between devices: none -> 31.5 us  [the longest x1 13.9 us: chain_body(): far_amps = lax.ppermute(own, 'occ', FAR)]
    psum x1 -> x0, blocking collectives: 30.1 us -> none  [body(): total = lax.psum(jnp.sum(residual * residual), ('occ', 'vir', 'rep'))]
    dot_general x2 -> x0, matrix products: 26.7 us -> none  [the longest x1 25.2 us: body(): jnp.einsum('ptac,ptcb->pab', cycle_w * live[:, :, None, None], selected_r...]
    all_to_all x2 -> x0, waiting for transfers between devices: 20.6 us -> none  [the longest x1 19 us: body(): lax.all_to_all(mixed, 'occ', split_axis=0, concat_axis=2, tiled=True)]
    all_gather x1 -> x0, blocking collectives: 18.1 us -> none  [body(): full_ladder = lax.all_gather(own_ladder, 'occ', axis=0, tiled=True)]
    pallas_call x0 -> x8, Pallas kernels: none -> 15.1 us  [the longest x1 3.36 us: sum_by_source(): pl.pallas_call(kernel, grid_spec=pltpu.PrefetchScalarGridSpec(num_scalar_...]
    all_to_all x0 -> x1, blocking collectives: none -> 13.2 us  [chain_body(): lax.all_to_all(total, ('occ', 'vir', 'rep'), split_axis=0, concat_axis=0,...]
  transfers between devices with their start and end apart: 4 -> 10, of which waited for: 3 -> 6; matrix products, arithmetic and copies ran while one was open for 3% -> 2% of each run, Pallas kernels for 0% -> 14%
where the time goes in v2:
time: 80.8 us; the launch traced here: 80.4 us
  waiting for transfers between devices  31.5 us (39%)
  Pallas kernels  15.1 us (19%)
  blocking collectives  13.2 us (16%)
  starting transfers between devices  12.1 us (15%)
  local copies, waits for them, and re-layouts  5 us (6%)
  between operations  3.35 us (4%)
    ppermute x1, waiting for transfers between devices, chain_body(): far_amps = lax.ppermute(own, 'occ', FAR)  13.9 us
    all_to_all x1, blocking collectives, chain_body(): lax.all_to_all(total, ('occ', 'vir', 'rep'), split_axis=0, concat_axis=0,...  13.2 us
    ppermute x2, waiting for transfers between devices, chain_body(): far = lax.ppermute(for_far, 'vir', SWAP)  11.1 us
    ppermute x2, waiting for transfers between devices, chain_body(): lax.ppermute(far_amps[c.start:c.start + c.length], 'occ', NEAR)  5.46 us
    ppermute x1, starting transfers between devices, chain_body(): far_amps = lax.ppermute(own, 'occ', FAR)  4.04 us
    pallas_call x1, Pallas kernels, sum_by_source(): pl.pallas_call(kernel, grid_spec=pltpu.PrefetchScalarGridSpec(num_scalar_...  3.36 us
    pallas_call x1, Pallas kernels, add_products(): pl.pallas_call(kernel, in_specs=[SMEM] * 3 + [VMEM] * (2 + n + len(chunks...  3.33 us
    unnamed x8, local copies, waits for them, and re-layouts  3.29 us
  transfers between devices with their start and end apart: 10, of which 6 were waited for; matrix products, arithmetic and copies ran while one was open for 2% of the time, Pallas kernels for 14%

profile of v2, /device:TPU:0, one launch (start us, length us, event | category | flops | bytes accessed | tf_op | source)
XLA Modules:
  0.0 80.4 jit_solution(2620893936044214566)
XLA Ops:
  0.6 2.0 %pack.1.amps = f32[1256,128]{1,0:T(8,128)} custom-call(f32[200,800]{1,0:T(8,128)} %bitcast.20), custom_call_target="tpu_custom_call" | custom-call | tf_op jit(solution)/shard_map/pack/pallas_call | solution.py:96
  2.7 4.0 %collective-permute-start = (f32[1256,128]{1,0:T(8,128)}, f32[1256,128]{1,0:T(8,128)S(1)}, u32[]{:S(2)}, u32[]{:S(2)}) collective-permute-start(f32[1256,128]{1,0:T(8,128)} %pack.1.amps), channel_id=1, source_target_pairs={{0,8},{8,0},{4,12},{12,4},{1,9},{9,1},{5,13},{13,5},{2,10},{10,2},... | collective-permute-start | bytes 1929224 | tf_op jit(solution)/shard_map/ppermute | solution.py:323
  6.7 1.6 %collective-permute-start.2 = (f32[1256,128]{1,0:T(8,128)}, f32[1256,128]{1,0:T(8,128)S(1)}, u32[]{:S(2)}, u32[]{:S(2)}) collective-permute-start(f32[1256,128]{1,0:T(8,128)} %pack.1.amps), channel_id=1, source_target_pairs={{0,4},{4,0},{8,12},{12,8},{1,5},{5,1},{9,13},{13,9},{2,6},{6,2},{1... | collective-permute-start | bytes 1929224 | tf_op jit(solution)/shard_map/ppermute | solution.py:324
  10.9 0.7 reshape.14.eps_row
  11.6 0.8 dynamic_slice.3
  12.3 0.1 copy.11.eps_col
  12.4 0.1 stack.35.meta
  12.5 2.6 %copy-done = f32[1,8,800,200]{2,3,1,0:T(8,128)S(1)} copy-done((f32[1,8,800,200]{2,3,1,0:T(8,128)S(1)}, f32[1,8,800,200]{2,3,1,0:T(8,128)}, u32[]{:S(2)}) %copy-start) | copy-done | bytes 5120024
  15.2 0.7 copy-done.3
  15.8 3.4 %sum_by_source.1 = (bf16[4,2,400,200]{3,2,1,0:T(8,128)(2,1)S(1)}, bf16[4,2,400,200]{3,2,1,0:T(8,128)(2,1)S(1)}) custom-call(s32[8]{0:T(128)S(1)} %stack.35.meta, s32[8]{0:T(128)S(1)} %bitcast.19, s32[1]{0:T(128)S(6)} %copy.12.count, f32[8,200,800]{2,1,0:T(8,128)S(1)} %bitcast.17), custom_call_target="tpu_custom_call" | custom-call | tf_op jit(solution)/shard_map/sum_by_source/pallas_call | solution.py:134
  19.2 2.1 %own_products.1 = (f32[200,800]{1,0:T(8,128)S(1)}, f32[2,400,288]{2,1,0:T(8,128)S(1)}, f32[2,400,512]{2,1,0:T(8,128)S(1)}) custom-call(s32[8]{0:T(128)S(1)} %stack.35.meta, s32[1,1]{1,0:T(1,128)S(6)} %copy.13.lad_src, f32[1,1]{1,0:T(1,128)S(6)} %copy.14.lad_coef, f32[1]{0:T(128)S(6)} %copy.15.energy, bf16[4,2,400,200]{3,2,1,0:T(8,128)(2,1)S(1)} %get-tuple-element.26.high, ...), custom_call_target="tpu_custom_call" | custom-call | tf_op jit(solution)/shard_map/own_products/pallas_call | solution.py:182
  21.3 13.9 %collective-permute-done.refs_1_ = f32[1256,128]{1,0:T(8,128)S(1)} collective-permute-done((f32[1256,128]{1,0:T(8,128)}, f32[1256,128]{1,0:T(8,128)S(1)}, u32[]{:S(2)}, u32[]{:S(2)}) %collective-permute-start) | collective-permute-done | bytes 643104 | tf_op jit(solution)/shard_map/ppermute | solution.py:323
  35.3 0.8 collective-permute-start.1
  36.1 1.4 %collective-permute-start.6 = (f32[800,128]{1,0:T(8,128)S(1)}, f32[800,128]{1,0:T(8,128)S(1)}, u32[]{:S(2)}, u32[]{:S(2)}) collective-permute-start(f32[800,128]{1,0:T(8,128)S(1)} %slice.7), channel_id=1, source_target_pairs={{0,4},{4,0},{8,12},{12,8},{1,5},{5,1},{9,13},{13,9},{2,6},{6,2},{1... | collective-permute-start | bytes 1228808 | tf_op jit(solution)/shard_map/ppermute | solution.py:330
  37.5 0.0 collective-permute-done.2.refs_0_
  37.5 3.3 %add_products.1 = (f32[2,400,288]{2,1,0:T(8,128)S(1)}, f32[2,400,512]{2,1,0:T(8,128)S(1)}) custom-call(s32[8]{0:T(128)S(1)} %stack.35.meta, s32[1,1]{1,0:T(1,128)S(6)} %copy.13.lad_src, f32[1,1]{1,0:T(1,128)S(6)} %copy.14.lad_coef, bf16[4,2,400,200]{3,2,1,0:T(8,128)(2,1)S(1)} %get-tuple-element.26.high, bf16[4,2,400,200]{3,2,1,0:T(8,128)(2,1)S(1)} %get-tuple-element.27.low, ...), custom_call_target="tpu_custom_call" | custom-call | tf_op jit(solution)/shard_map/add_products/pallas_call | solution.py:215
  40.8 3.2 %collective-permute-done.1.amps = f32[456,128]{1,0:T(8,128)S(1)} collective-permute-done((f32[456,128]{1,0:T(8,128)S(1)}, f32[456,128]{1,0:T(8,128)S(1)}, u32[]{:S(2)}, u32[]{:S(2)}) %collective-permute-start.1) | collective-permute-done | bytes 233504 | tf_op jit(solution)/shard_map/ppermute | solution.py:330
  44.0 1.5 %last_product.2 = (f32[456,128]{1,0:T(8,128)S(1)}, f32[456,128]{1,0:T(8,128)S(1)}, f32[456,128]{1,0:T(8,128)S(1)}, f32[456,128]{1,0:T(8,128)S(1)}) custom-call(s32[8]{0:T(128)S(1)} %stack.35.meta, s32[1,1]{1,0:T(1,128)S(6)} %copy.13.lad_src, f32[1,1]{1,0:T(1,128)S(6)} %copy.14.lad_coef, bf16[4,2,400,200]{3,2,1,0:T(8,128)(2,1)S(1)} %get-tuple-element.26.high, ...), custom_call_target="tpu_custom_call" | custom-call | tf_op jit(solution)/shard_map/last_product/pallas_call | solution.py:242
  45.4 0.1 collective-permute-start.4
  45.5 0.5 collective-permute-start.3
  46.0 1.0 %collective-permute-done.4 = f32[456,128]{1,0:T(8,128)S(1)} collective-permute-done((f32[456,128]{1,0:T(8,128)S(1)}, f32[456,128]{1,0:T(8,128)S(1)}, u32[]{:S(2)}, u32[]{:S(2)}) %collective-permute-start.4) | collective-permute-done | bytes 233504 | tf_op jit(solution)/shard_map/ppermute | solution.py:344
  47.0 1.6 %collective-permute-start.5 = (f32[456,128]{1,0:T(8,128)S(1)}, f32[456,128]{1,0:T(8,128)S(1)}, u32[]{:S(2)}, u32[]{:S(2)}) collective-permute-start(f32[456,128]{1,0:T(8,128)S(1)} %add.34), channel_id=1, source_target_pairs={{0,2},{2,0},{1,3},{3,1},{4,6},{6,4},{5,7},{7,5},{8,10},{10,8},{9,1... | collective-permute-start | bytes 700424 | tf_op jit(solution)/shard_map/ppermute | solution.py:348
  48.6 2.3 %collective-permute-done.6.amps = f32[800,128]{1,0:T(8,128)S(1)} collective-permute-done((f32[800,128]{1,0:T(8,128)S(1)}, f32[800,128]{1,0:T(8,128)S(1)}, u32[]{:S(2)}, u32[]{:S(2)}) %collective-permute-start.6) | collective-permute-done | bytes 409632 | tf_op jit(solution)/shard_map/ppermute | solution.py:330
  50.9 1.4 %last_product.3 = (f32[800,128]{1,0:T(8,128)S(1)}, f32[800,128]{1,0:T(8,128)S(1)}, f32[800,128]{1,0:T(8,128)S(1)}, f32[800,128]{1,0:T(8,128)S(1)}) custom-call(s32[8]{0:T(128)S(1)} %stack.35.meta, s32[1,1]{1,0:T(1,128)S(6)} %copy.13.lad_src, f32[1,1]{1,0:T(1,128)S(6)} %copy.14.lad_coef, bf16[4,2,400,200]{3,2,1,0:T(8,128)(2,1)S(1)} %get-tuple-element.26.high, ...), custom_call_target="tpu_custom_call" | custom-call | tf_op jit(solution)/shard_map/last_product/pallas_call | solution.py:242
  52.3 0.1 collective-permute-start.7
  52.4 0.5 collective-permute-start.8
  52.9 1.9 %collective-permute-done.5 = f32[456,128]{1,0:T(8,128)S(1)} collective-permute-done((f32[456,128]{1,0:T(8,128)S(1)}, f32[456,128]{1,0:T(8,128)S(1)}, u32[]{:S(2)}, u32[]{:S(2)}) %collective-permute-start.5) | collective-permute-done | bytes 233504 | tf_op jit(solution)/shard_map/ppermute | solution.py:348
  54.9 1.6 %collective-permute-start.9 = (f32[800,128]{1,0:T(8,128)S(1)}, f32[800,128]{1,0:T(8,128)S(1)}, u32[]{:S(2)}, u32[]{:S(2)}) collective-permute-start(f32[800,128]{1,0:T(8,128)S(1)} %add.36), channel_id=1, source_target_pairs={{0,2},{2,0},{1,3},{3,1},{4,6},{6,4},{5,7},{7,5},{8,10},{10,8},{9,1... | collective-permute-start | bytes 1228808 | tf_op jit(solution)/shard_map/ppermute | solution.py:348
  56.6 9.2 %collective-permute-done.9.refs_3_ = f32[800,128]{1,0:T(8,128)S(1)} collective-permute-done((f32[800,128]{1,0:T(8,128)S(1)}, f32[800,128]{1,0:T(8,128)S(1)}, u32[]{:S(2)}, u32[]{:S(2)}) %collective-permute-start.9) | collective-permute-done | bytes 409632 | tf_op jit(solution)/shard_map/ppermute | solution.py:348
  65.7 0.3 finish.1
  66.1 13.2 %all_to_all.5.total = f32[16,8,128]{2,1,0:T(8,128)S(1)} all-to-all(f32[16,8,128]{2,1,0:T(8,128)S(1)} %get-tuple-element.46), channel_id=1, replica_groups=mesh['groups'=2,'occ'=4,'vir'=2,'rep'=2] {'occ','vir','rep'}, dimensions={0} | all-to-all | bytes 131072 | tf_op jit(solution)/shard_map/all_to_all | solution.py:354
  79.3 1.1 %jacobi.1 = (f32[200,800]{1,0:T(8,128)}, f32[200,800]{1,0:T(8,128)}) custom-call(f32[200,800]{1,0:T(8,128)S(1)} %get-tuple-element.45.residual, f32[16,8,128]{2,1,0:T(8,128)S(1)} %all_to_all.5.total, f32[200,800]{1,0:T(8,128)S(1)} %get-tuple-element.47.inverse), custom_call_target="tpu_custom_call" | custom-call | tf_op jit(solution)/shard_map/jacobi/pallas_call | solution.py:289
  (14 shorter events, 0.2 us)
Async XLA Ops:
  2.7 32.6 %collective-permute-start = (f32[1256,128]{1,0:T(8,128)}, f32[1256,128]{1,0:T(8,128)S(1)}, u32[]{:S(2)}, u32[]{:S(2)}) collective-permute-start(f32[1256,128]{1,0:T(8,128)} %pack.1.amps), channel_id=1, source_target_pairs={{0,8},{8,0},{4,12},{12,4},{1,9},{9,1},{5,13},{13,5},{2,10},{10,2},... | collective-permute-start | bytes 1929224 | tf_op jit(solution)/shard_map/ppermute | solution.py:323
  6.7 30.8 %collective-permute-start.2 = (f32[1256,128]{1,0:T(8,128)}, f32[1256,128]{1,0:T(8,128)S(1)}, u32[]{:S(2)}, u32[]{:S(2)}) collective-permute-start(f32[1256,128]{1,0:T(8,128)} %pack.1.amps), channel_id=1, source_target_pairs={{0,4},{4,0},{8,12},{12,8},{1,5},{5,1},{9,13},{13,9},{2,6},{6,2},{1... | collective-permute-start | bytes 1929224 | tf_op jit(solution)/shard_map/ppermute | solution.py:324
  12.5 2.6 %copy-start = (f32[1,8,800,200]{2,3,1,0:T(8,128)S(1)}, f32[1,8,800,200]{2,3,1,0:T(8,128)}, u32[]{:S(2)}) copy-start(f32[1,8,800,200]{2,3,1,0:T(8,128)} %param.11) | copy-start | bytes 15360004
  15.2 0.7 copy-start.3
  15.8 3.4 %copy-start.1 = (f32[1256,128]{1,0:T(8,128)S(1)}, f32[1256,128]{1,0:T(8,128)}, u32[]{:S(2)}) copy-start(f32[1256,128]{1,0:T(8,128)} %pack.1.amps) | copy-start | bytes 1929220
  15.8 3.4 %copy-start.2 = (f32[1,200,800]{2,1,0:T(8,128)S(1)}, f32[1,200,800]{2,1,0:T(8,128)}, u32[]{:S(2)}) copy-start(f32[1,200,800]{2,1,0:T(8,128)} %param.10) | copy-start | bytes 1920004
  35.3 8.7 %collective-permute-start.1 = (f32[456,128]{1,0:T(8,128)S(1)}, f32[456,128]{1,0:T(8,128)S(1)}, u32[]{:S(2)}, u32[]{:S(2)}) collective-permute-start(f32[456,128]{1,0:T(8,128)S(1)} %slice.6), channel_id=1, source_target_pairs={{0,4},{4,0},{8,12},{12,8},{1,5},{5,1},{9,13},{13,9},{2,6},{6,2},{1... | collective-permute-start | bytes 700424 | tf_op jit(solution)/shard_map/ppermute | solution.py:330
  36.1 14.8 %collective-permute-start.6 = (f32[800,128]{1,0:T(8,128)S(1)}, f32[800,128]{1,0:T(8,128)S(1)}, u32[]{:S(2)}, u32[]{:S(2)}) collective-permute-start(f32[800,128]{1,0:T(8,128)S(1)} %slice.7), channel_id=1, source_target_pairs={{0,4},{4,0},{8,12},{12,8},{1,5},{5,1},{9,13},{13,9},{2,6},{6,2},{1... | collective-permute-start | bytes 1228808 | tf_op jit(solution)/shard_map/ppermute | solution.py:330
  45.4 1.6 %collective-permute-start.4 = (f32[456,128]{1,0:T(8,128)S(1)}, f32[456,128]{1,0:T(8,128)S(1)}, u32[]{:S(2)}, u32[]{:S(2)}) collective-permute-start(f32[456,128]{1,0:T(8,128)S(1)} %get-tuple-element.37), channel_id=1, source_target_pairs={{0,1},{1,0},{2,3},{3,2},{4,5},{5,4},{6,7},{7,6},{8,9},{9,8},{10,11... | collective-permute-start | bytes 700424 | tf_op jit(solution)/shard_map/ppermute | solution.py:344
  45.5 7.4 %collective-permute-start.3 = (f32[456,128]{1,0:T(8,128)S(1)}, f32[456,128]{1,0:T(8,128)S(1)}, u32[]{:S(2)}, u32[]{:S(2)}) collective-permute-start(f32[456,128]{1,0:T(8,128)S(1)} %get-tuple-element.35), channel_id=1, source_target_pairs={{0,1},{1,0},{2,3},{3,2},{4,5},{5,4},{6,7},{7,6},{8,9},{9,8},{10,11... | collective-permute-start | bytes 700424 | tf_op jit(solution)/shard_map/ppermute | solution.py:344
  47.0 7.8 %collective-permute-start.5 = (f32[456,128]{1,0:T(8,128)S(1)}, f32[456,128]{1,0:T(8,128)S(1)}, u32[]{:S(2)}, u32[]{:S(2)}) collective-permute-start(f32[456,128]{1,0:T(8,128)S(1)} %add.34), channel_id=1, source_target_pairs={{0,2},{2,0},{1,3},{3,1},{4,6},{6,4},{5,7},{7,5},{8,10},{10,8},{9,1... | collective-permute-start | bytes 700424 | tf_op jit(solution)/shard_map/ppermute | solution.py:348
  52.3 2.6 %collective-permute-start.7 = (f32[800,128]{1,0:T(8,128)S(1)}, f32[800,128]{1,0:T(8,128)S(1)}, u32[]{:S(2)}, u32[]{:S(2)}) collective-permute-start(f32[800,128]{1,0:T(8,128)S(1)} %get-tuple-element.40), channel_id=1, source_target_pairs={{0,1},{1,0},{2,3},{3,2},{4,5},{5,4},{6,7},{7,6},{8,9},{9,8},{10,11... | collective-permute-start | bytes 1228808 | tf_op jit(solution)/shard_map/ppermute | solution.py:344
  52.4 4.2 %collective-permute-start.8 = (f32[800,128]{1,0:T(8,128)S(1)}, f32[800,128]{1,0:T(8,128)S(1)}, u32[]{:S(2)}, u32[]{:S(2)}) collective-permute-start(f32[800,128]{1,0:T(8,128)S(1)} %get-tuple-element.43), channel_id=1, source_target_pairs={{0,1},{1,0},{2,3},{3,2},{4,5},{5,4},{6,7},{7,6},{8,9},{9,8},{10,11... | collective-permute-start | bytes 1228808 | tf_op jit(solution)/shard_map/ppermute | solution.py:344
  54.9 10.8 %collective-permute-start.9 = (f32[800,128]{1,0:T(8,128)S(1)}, f32[800,128]{1,0:T(8,128)S(1)}, u32[]{:S(2)}, u32[]{:S(2)}) collective-permute-start(f32[800,128]{1,0:T(8,128)S(1)} %add.36), channel_id=1, source_target_pairs={{0,2},{2,0},{1,3},{3,1},{4,6},{6,4},{5,7},{7,5},{8,10},{10,8},{9,1... | collective-permute-start | bytes 1228808 | tf_op jit(solution)/shard_map/ppermute | solution.py:348

commit v3 on v2

--- a/solution.py
+++ b/solution.py
@@ -17,9 +17,7 @@
 NEAR = [(0, 1), (1, 0), (2, 3), (3, 2)]
 FAR = [(0, 2), (2, 0), (1, 3), (3, 1)]
 VMEM_MIB = 20
-TILES_FIRST = 2
-MERGE = True
-FORCE = True
+FIRST_TILES = 2
 
 
 def limit(n):
@@ -88,18 +86,18 @@
 
 
 def pack(amps, chunks):
-    def kernel(amps_ref, out):
+    def kernel(amps, out):
         for chunk in chunks:
-            chunk.store(writer(out, skip=chunk.start), chunk.take(amps_ref))
+            chunk.store(writer(out, skip=chunk.start), chunk.take(amps))
 
     length = sum(chunk.length for chunk in chunks)
     return pl.pallas_call(
         kernel,
         in_specs=[VMEM],
         out_specs=VMEM,
-        out_shape=jax.ShapeDtypeStruct((length, LANES), jnp.float32),
+        out_shape=pltpu.VMEM((length, LANES), jnp.float32),
         name="pack",
-    )(amps)
+    )(pltpu.with_memory_space_constraint(amps, pltpu.VMEM))
 
 
 def sum_by_source(meta, cycle_w, cycle_src, cycle_count, npair, blocks):
@@ -239,7 +237,7 @@
                     part = part + ladder_weight(k, lad_src, lad_coef) * x
                 chunk.store(writer(outs[2 * h + i]), part)
 
-    return pl.pallas_call(
+    outs = pl.pallas_call(
         kernel,
         in_specs=[SMEM] * 3 + [VMEM] * 4,
         out_specs=[VMEM] * 4,
@@ -247,6 +245,7 @@
         compiler_params=limit(VMEM_MIB),
         name="last_product",
     )(meta, lad_src, lad_coef, high, low, amps, sums)
+    return outs[:2], outs[2:]
 
 
 def finish(chunks, done, pieces, shape, copies):
@@ -254,7 +253,7 @@
         *refs, out, total_ref = refs
         total = jnp.zeros((1, LANES), jnp.float32)
         for i, chunk in enumerate(chunks):
-            parts = refs[i : i + 1] if i < len(done) else refs[len(done) + 3 * (i - len(done)) :][:3]
+            parts = refs[i : i + 1] if i < len(done) else refs[len(done) :]
             value = sum(chunk.load(reader(ref)) for ref in parts)
             chunk.put(out, value)
             total = total + jnp.sum(value * value)
@@ -267,11 +266,42 @@
         out_specs=[VMEM, VMEM],
         out_shape=[
             jax.ShapeDtypeStruct(shape, jnp.float32),
-            jax.ShapeDtypeStruct((copies, 8, LANES), jnp.float32),
+            jax.ShapeDtypeStruct((copies, 1, LANES), jnp.float32),
         ],
         compiler_params=limit(VMEM_MIB),
         name="finish",
     )(*refs)
+
+
+def jacobi(residual, total, inverse, bound):
+    rows, width = residual.shape
+    part = rows // 5 if rows % 40 == 0 else rows
+
+    def kernel(residual, total, inverse, residual_out, update_out, update, sems):
+        copies = [pltpu.make_async_copy(residual, residual_out, sems.at[0])]
+        copies[0].start()
+        scale = jnp.minimum(1.0, bound / jnp.sqrt(jnp.sum(total[...], axis=0)[0:1, 0:1]))
+        for start in range(0, rows, part):
+            span = pl.ds(start, part)
+            update[span] = (scale * residual[span]) * inverse[span]
+            copies.append(pltpu.make_async_copy(update.at[span], update_out.at[span], sems.at[len(copies)]))
+            copies[-1].start()
+        for copy in copies:
+            copy.wait()
+
+    shape = jax.ShapeDtypeStruct(residual.shape, jnp.float32)
+    return pl.pallas_call(
+        kernel,
+        in_specs=[VMEM, VMEM, VMEM],
+        out_specs=[HBM, HBM],
+        out_shape=[shape, shape],
+        scratch_shapes=[
+            pltpu.VMEM((rows, width), jnp.float32),
+            pltpu.SemaphoreType.DMA((1 + rows // part,)),
+        ],
+        compiler_params=limit(VMEM_MIB),
+        name="jacobi",
+    )(residual, total, inverse)
 
 
 def jacobi(residual, total, inverse, bound):
@@ -315,10 +345,10 @@
     eps_row = eps_vir.reshape(1, width)
     eps_col = lax.dynamic_slice_in_dim(eps_vir, (2 * chip + core) * rows, rows).reshape(rows, 1)
 
-    tiles = width // LANES
-    half = TILES_FIRST
-    first = Chunk(rows, width, 0, half, True, 0)
-    chunks = [first, Chunk(rows, width, half, tiles - half, False, first.length)]
+    chunks, first, start = [], 0, 0
+    for count in (FIRST_TILES, width // LANES - FIRST_TILES):
+        chunks.append(Chunk(rows, width, first, count, not first, start))
+        first, start = first + count, start + chunks[-1].length
     own = pack(amps[0], chunks)
     far_amps = lax.ppermute(own, "occ", FAR)
     near_amps = lax.ppermute(own, "occ", NEAR)
@@ -327,29 +357,23 @@
         chunks, meta, ladder_src, ladder_coef, pair_energy, weights, own, drive[0], eps_row, eps_col
     )
     far_amps, sums = lax.optimization_barrier((far_amps, sums))
-    last_amps = [lax.ppermute(far_amps[c.start : c.start + c.length], "occ", NEAR) for c in chunks]
-    if MERGE:
-        sums = add_products(
-            chunks, (1, 2), meta, ladder_src, ladder_coef, weights, (near_amps, far_amps), sums
-        )
-
-    done, pieces = [], []
+    sums = add_products(
+        chunks, (1, 2), meta, ladder_src, ladder_coef, weights, (near_amps, far_amps), sums
+    )
+    outgoing = [far_amps[c.start : c.start + c.length] for c in chunks]
+    outgoing[1:], sums = lax.optimization_barrier((outgoing[1:], sums))
+    last_amps = [lax.ppermute(x, "occ", NEAR) for x in outgoing]
+
+    done = []
     for i, chunk in enumerate(chunks):
-        if not MERGE:
-            sums[i] = add_products(
-                [chunk], (1, 2), meta, ladder_src, ladder_coef, weights, (near_amps, far_amps), [sums[i]]
-            )[0]
-        away = last_product(chunk, meta, ladder_src, ladder_coef, weights, last_amps[i], sums[i])
-        away, keep = away[:2], away[2:]
+        away, keep = last_product(chunk, meta, ladder_src, ladder_coef, weights, last_amps[i], sums[i])
         got = [lax.ppermute(x, "rep", SWAP) for x in away]
         for_far = keep[0] + got[0]
-        if i and FORCE:
-            done, for_far = lax.optimization_barrier((done, for_far))
+        done, for_far = lax.optimization_barrier((done, for_far))
         far = lax.ppermute(for_far, "vir", SWAP)
-        if i < len(chunks) - 1 and FORCE:
-            done.append(keep[1] + got[1] + far)
-        else:
-            pieces += [keep[1], got[1], far]
+        pieces = (keep[1], got[1], far)
+        if i < len(chunks) - 1:
+            done.append(sum(pieces))
     residual, total = finish(chunks, done, pieces, (rows, width), npair * blocks)
     total = lax.all_to_all(total, ("occ", "vir", "rep"), split_axis=0, concat_axis=0, tiled=True)
     residual, update = jacobi(residual, total, inverse, clip_level * width * math.sqrt(npair))
@@ -389,7 +413,7 @@
         and cycle_w.shape[1] >= 4
         and rows % 8 == 0
         and width % LANES == LANES // 4
-        and width >= 2 * LANES
+        and width > (FIRST_TILES + 1) * LANES
     )
     return (chain_body if chain else any_body)(*args)
 

time: 80.8 us -> 79.3 us (0.981)
  Pallas kernels: 15.1 us -> 12.8 us
  local copies, waits for them, and re-layouts: 5 us -> 6.1 us
  waiting for transfers between devices: 31.5 us -> 32.4 us
    pallas_call x1, Pallas kernels: 2.03 us -> 0.09 us  [pack(): pl.pallas_call(kernel, in_specs=[VMEM], out_specs=VMEM, out_shape=pltpu.V...]
    unnamed x8, local copies, waits for them, and re-layouts: 3.29 us -> 4.39 us
  transfers between devices with their start and end apart: 10 -> 10, of which waited for: 6 -> 7; matrix products, arithmetic and copies ran while one was open for 2% -> 2% of each run, Pallas kernels for 14% -> 14%
where the time goes in v3:
time: 79.3 us; the launch traced here: 79 us
  waiting for transfers between devices  32.4 us (41%)
  Pallas kernels  12.8 us (16%)
  blocking collectives  12.7 us (16%)
  starting transfers between devices  11.4 us (14%)
  local copies, waits for them, and re-layouts  6.1 us (8%)
  between operations  3.34 us (4%)
    ppermute x1, waiting for transfers between devices, chain_body(): far_amps = lax.ppermute(own, 'occ', FAR)  14.1 us
    all_to_all x1, blocking collectives, chain_body(): lax.all_to_all(total, ('occ', 'vir', 'rep'), split_axis=0, concat_axis=0,...  12.7 us
    ppermute x2, waiting for transfers between devices, chain_body(): far = lax.ppermute(for_far, 'vir', SWAP)  10.7 us
    ppermute x2, waiting for transfers between devices, chain_body(): last_amps = [lax.ppermute(x, 'occ', NEAR) for x in outgoing]  5.84 us
    unnamed x8, local copies, waits for them, and re-layouts  4.39 us
    ppermute x1, starting transfers between devices, chain_body(): far_amps = lax.ppermute(own, 'occ', FAR)  4.1 us
    pallas_call x1, Pallas kernels, add_products(): pl.pallas_call(kernel, in_specs=[SMEM] * 3 + [VMEM] * (2 + n + len(chunks...  3.4 us
    pallas_call x1, Pallas kernels, sum_by_source(): pl.pallas_call(kernel, grid_spec=pltpu.PrefetchScalarGridSpec(num_scalar_...  2.97 us
  transfers between devices with their start and end apart: 10, of which 7 were waited for; matrix products, arithmetic and copies ran while one was open for 2% of the time, Pallas kernels for 14%

profile of v3, /device:TPU:0, one launch (start us, length us, event | category | flops | bytes accessed | tf_op | source)
XLA Modules:
  0.0 79.0 jit_solution(4915966292770022521)
XLA Ops:
  0.6 1.1 %copy-done.1 = f32[1,200,800]{2,1,0:T(8,128)S(1)} copy-done((f32[1,200,800]{2,1,0:T(8,128)S(1)}, f32[1,200,800]{2,1,0:T(8,128)}, u32[]{:S(2)}) %copy-start.1) | copy-done | bytes 640024
  1.7 0.1 pack.1.amps
  1.8 4.1 %collective-permute-start = (f32[1256,128]{1,0:T(8,128)S(1)}, f32[1256,128]{1,0:T(8,128)S(1)}, u32[]{:S(2)}, u32[]{:S(2)}) collective-permute-start(f32[1256,128]{1,0:T(8,128)S(1)} %pack.1.amps), channel_id=1, source_target_pairs={{0,8},{8,0},{4,12},{12,4},{1,9},{9,1},{5,13},{13,5},{2,10},{10,2},... | collective-permute-start | bytes 1929224 | tf_op jit(solution)/shard_map/ppermute | solution.py:353
  5.9 1.6 %collective-permute-start.2 = (f32[1256,128]{1,0:T(8,128)S(1)}, f32[1256,128]{1,0:T(8,128)S(1)}, u32[]{:S(2)}, u32[]{:S(2)}) collective-permute-start(f32[1256,128]{1,0:T(8,128)S(1)} %pack.1.amps), channel_id=1, source_target_pairs={{0,4},{4,0},{8,12},{12,8},{1,5},{5,1},{9,13},{13,9},{2,6},{6,2},{1... | collective-permute-start | bytes 1929224 | tf_op jit(solution)/shard_map/ppermute | solution.py:354
  10.1 0.7 reshape.14.eps_row
  10.8 0.8 dynamic_slice.3
  11.6 0.1 copy.11.eps_col
  11.7 0.1 stack.35.meta
  11.8 2.6 %copy-done = f32[1,8,800,200]{2,3,1,0:T(8,128)S(1)} copy-done((f32[1,8,800,200]{2,3,1,0:T(8,128)S(1)}, f32[1,8,800,200]{2,3,1,0:T(8,128)}, u32[]{:S(2)}) %copy-start) | copy-done | bytes 5120024
  14.4 0.7 copy-done.3
  15.1 3.0 %sum_by_source.1 = (bf16[4,2,400,200]{3,2,1,0:T(8,128)(2,1)S(1)}, bf16[4,2,400,200]{3,2,1,0:T(8,128)(2,1)S(1)}) custom-call(s32[8]{0:T(128)S(1)} %stack.35.meta, s32[8]{0:T(128)S(1)} %bitcast.20, s32[1]{0:T(128)S(6)} %copy.12.count, f32[8,200,800]{2,1,0:T(8,128)S(1)} %bitcast.17), custom_call_target="tpu_custom_call" | custom-call | tf_op jit(solution)/shard_map/sum_by_source/pallas_call | solution.py:132
  18.1 2.1 %own_products.1 = (f32[200,800]{1,0:T(8,128)S(1)}, f32[2,400,288]{2,1,0:T(8,128)S(1)}, f32[2,400,512]{2,1,0:T(8,128)S(1)}) custom-call(s32[8]{0:T(128)S(1)} %stack.35.meta, s32[1,1]{1,0:T(1,128)S(6)} %copy.13.lad_src, f32[1,1]{1,0:T(1,128)S(6)} %copy.14.lad_coef, f32[1]{0:T(128)S(6)} %copy.15.energy, bf16[4,2,400,200]{3,2,1,0:T(8,128)(2,1)S(1)} %get-tuple-element.29.high, ...), custom_call_target="tpu_custom_call" | custom-call | tf_op jit(solution)/shard_map/own_products/pallas_call | solution.py:180
  20.2 14.1 %collective-permute-done.refs_1_ = f32[1256,128]{1,0:T(8,128)S(1)} collective-permute-done((f32[1256,128]{1,0:T(8,128)S(1)}, f32[1256,128]{1,0:T(8,128)S(1)}, u32[]{:S(2)}, u32[]{:S(2)}) %collective-permute-start) | collective-permute-done | bytes 643104 | tf_op jit(solution)/shard_map/ppermute | solution.py:353
  34.3 0.7 collective-permute-start.1
  35.0 3.4 %add_products.1 = (f32[2,400,288]{2,1,0:T(8,128)S(1)}, f32[2,400,512]{2,1,0:T(8,128)S(1)}) custom-call(s32[8]{0:T(128)S(1)} %stack.35.meta, s32[1,1]{1,0:T(1,128)S(6)} %copy.13.lad_src, f32[1,1]{1,0:T(1,128)S(6)} %copy.14.lad_coef, bf16[4,2,400,200]{3,2,1,0:T(8,128)(2,1)S(1)} %get-tuple-element.29.high, bf16[4,2,400,200]{3,2,1,0:T(8,128)(2,1)S(1)} %get-tuple-element.30.low, ...), custom_call_target="tpu_custom_call" | custom-call | tf_op jit(solution)/shard_map/add_products/pallas_call | solution.py:213
  38.4 1.5 %collective-permute-start.6 = (f32[800,128]{1,0:T(8,128)S(1)}, f32[800,128]{1,0:T(8,128)S(1)}, u32[]{:S(2)}, u32[]{:S(2)}) collective-permute-start(f32[800,128]{1,0:T(8,128)S(1)} %slice.7), channel_id=1, source_target_pairs={{0,4},{4,0},{8,12},{12,8},{1,5},{5,1},{9,13},{13,9},{2,6},{6,2},{1... | collective-permute-start | bytes 1228808 | tf_op jit(solution)/shard_map/ppermute | solution.py:365
  39.9 1.6 %collective-permute-done.1.amps = f32[456,128]{1,0:T(8,128)S(1)} collective-permute-done((f32[456,128]{1,0:T(8,128)S(1)}, f32[456,128]{1,0:T(8,128)S(1)}, u32[]{:S(2)}, u32[]{:S(2)}) %collective-permute-start.1) | collective-permute-done | bytes 233504 | tf_op jit(solution)/shard_map/ppermute | solution.py:365
  41.5 1.5 %last_product.2 = (f32[456,128]{1,0:T(8,128)S(1)}, f32[456,128]{1,0:T(8,128)S(1)}, f32[456,128]{1,0:T(8,128)S(1)}, f32[456,128]{1,0:T(8,128)S(1)}) custom-call(s32[8]{0:T(128)S(1)} %stack.35.meta, s32[1,1]{1,0:T(1,128)S(6)} %copy.13.lad_src, f32[1,1]{1,0:T(1,128)S(6)} %copy.14.lad_coef, bf16[4,2,400,200]{3,2,1,0:T(8,128)(2,1)S(1)} %get-tuple-element.29.high, ...), custom_call_target="tpu_custom_call" | custom-call | tf_op jit(solution)/shard_map/last_product/pallas_call | solution.py:240
  43.0 0.1 collective-permute-start.4
  43.0 0.5 collective-permute-start.3
  43.5 1.0 %collective-permute-done.4 = f32[456,128]{1,0:T(8,128)S(1)} collective-permute-done((f32[456,128]{1,0:T(8,128)S(1)}, f32[456,128]{1,0:T(8,128)S(1)}, u32[]{:S(2)}, u32[]{:S(2)}) %collective-permute-start.4) | collective-permute-done | bytes 233504 | tf_op jit(solution)/shard_map/ppermute | solution.py:370
  44.6 1.1 %collective-permute-start.5 = (f32[456,128]{1,0:T(8,128)S(1)}, f32[456,128]{1,0:T(8,128)S(1)}, u32[]{:S(2)}, u32[]{:S(2)}) collective-permute-start(f32[456,128]{1,0:T(8,128)S(1)} %add.34), channel_id=1, source_target_pairs={{0,2},{2,0},{1,3},{3,1},{4,6},{6,4},{5,7},{7,5},{8,10},{10,8},{9,1... | collective-permute-start | bytes 700424 | tf_op jit(solution)/shard_map/ppermute | solution.py:373
  45.7 4.3 %collective-permute-done.6.amps = f32[800,128]{1,0:T(8,128)S(1)} collective-permute-done((f32[800,128]{1,0:T(8,128)S(1)}, f32[800,128]{1,0:T(8,128)S(1)}, u32[]{:S(2)}, u32[]{:S(2)}) %collective-permute-start.6) | collective-permute-done | bytes 409632 | tf_op jit(solution)/shard_map/ppermute | solution.py:365
  50.0 1.4 %last_product.3 = (f32[800,128]{1,0:T(8,128)S(1)}, f32[800,128]{1,0:T(8,128)S(1)}, f32[800,128]{1,0:T(8,128)S(1)}, f32[800,128]{1,0:T(8,128)S(1)}) custom-call(s32[8]{0:T(128)S(1)} %stack.35.meta, s32[1,1]{1,0:T(1,128)S(6)} %copy.13.lad_src, f32[1,1]{1,0:T(1,128)S(6)} %copy.14.lad_coef, bf16[4,2,400,200]{3,2,1,0:T(8,128)(2,1)S(1)} %get-tuple-element.29.high, ...), custom_call_target="tpu_custom_call" | custom-call | tf_op jit(solution)/shard_map/last_product/pallas_call | solution.py:240
  51.4 0.5 collective-permute-start.8
  51.9 0.4 collective-permute-done.5
  52.4 0.7 collective-permute-done.7
  53.2 1.3 %collective-permute-start.9 = (f32[800,128]{1,0:T(8,128)S(1)}, f32[800,128]{1,0:T(8,128)S(1)}, u32[]{:S(2)}, u32[]{:S(2)}) collective-permute-start(f32[800,128]{1,0:T(8,128)S(1)} %add.36), channel_id=1, source_target_pairs={{0,2},{2,0},{1,3},{3,1},{4,6},{6,4},{5,7},{7,5},{8,10},{10,8},{9,1... | collective-permute-start | bytes 1228808 | tf_op jit(solution)/shard_map/ppermute | solution.py:373
  54.5 10.3 %collective-permute-done.9.refs_3_ = f32[800,128]{1,0:T(8,128)S(1)} collective-permute-done((f32[800,128]{1,0:T(8,128)S(1)}, f32[800,128]{1,0:T(8,128)S(1)}, u32[]{:S(2)}, u32[]{:S(2)}) %collective-permute-start.9) | collective-permute-done | bytes 409632 | tf_op jit(solution)/shard_map/ppermute | solution.py:373
  64.8 0.3 finish.1
  65.1 12.7 %all_to_all.5.total = f32[16,1,128]{2,1,0:T(1,128)S(1)} all-to-all(f32[16,1,128]{2,1,0:T(1,128)S(1)} %get-tuple-element.52), channel_id=1, replica_groups=mesh['groups'=2,'occ'=4,'vir'=2,'rep'=2] {'occ','vir','rep'}, dimensions={0} | all-to-all | bytes 16384 | tf_op jit(solution)/shard_map/all_to_all | solution.py:378
  77.9 1.1 %jacobi.1 = (f32[200,800]{1,0:T(8,128)}, f32[200,800]{1,0:T(8,128)}) custom-call(f32[200,800]{1,0:T(8,128)S(1)} %get-tuple-element.51.residual, f32[16,1,128]{2,1,0:T(1,128)S(1)} %all_to_all.5.total, f32[200,800]{1,0:T(8,128)S(1)} %get-tuple-element.53.inverse), custom_call_target="tpu_custom_call" | custom-call | tf_op jit(solution)/shard_map/jacobi/pallas_call | solution.py:319
  (14 shorter events, 0.3 us)
Async XLA Ops:
  0.6 1.1 %copy-start.1 = (f32[1,200,800]{2,1,0:T(8,128)S(1)}, f32[1,200,800]{2,1,0:T(8,128)}, u32[]{:S(2)}) copy-start(f32[1,200,800]{2,1,0:T(8,128)} %param.9) | copy-start | bytes 1920004
  1.8 32.5 %collective-permute-start = (f32[1256,128]{1,0:T(8,128)S(1)}, f32[1256,128]{1,0:T(8,128)S(1)}, u32[]{:S(2)}, u32[]{:S(2)}) collective-permute-start(f32[1256,128]{1,0:T(8,128)S(1)} %pack.1.amps), channel_id=1, source_target_pairs={{0,8},{8,0},{4,12},{12,4},{1,9},{9,1},{5,13},{13,5},{2,10},{10,2},... | collective-permute-start | bytes 1929224 | tf_op jit(solution)/shard_map/ppermute | solution.py:353
  5.9 29.1 %collective-permute-start.2 = (f32[1256,128]{1,0:T(8,128)S(1)}, f32[1256,128]{1,0:T(8,128)S(1)}, u32[]{:S(2)}, u32[]{:S(2)}) collective-permute-start(f32[1256,128]{1,0:T(8,128)S(1)} %pack.1.amps), channel_id=1, source_target_pairs={{0,4},{4,0},{8,12},{12,8},{1,5},{5,1},{9,13},{13,9},{2,6},{6,2},{1... | collective-permute-start | bytes 1929224 | tf_op jit(solution)/shard_map/ppermute | solution.py:354
  11.8 2.6 %copy-start = (f32[1,8,800,200]{2,3,1,0:T(8,128)S(1)}, f32[1,8,800,200]{2,3,1,0:T(8,128)}, u32[]{:S(2)}) copy-start(f32[1,8,800,200]{2,3,1,0:T(8,128)} %param.11) | copy-start | bytes 15360004
  14.4 0.7 copy-start.3
  15.1 3.0 %copy-start.2 = (f32[1,200,800]{2,1,0:T(8,128)S(1)}, f32[1,200,800]{2,1,0:T(8,128)}, u32[]{:S(2)}) copy-start(f32[1,200,800]{2,1,0:T(8,128)} %param.10) | copy-start | bytes 1920004
  34.3 7.2 %collective-permute-start.1 = (f32[456,128]{1,0:T(8,128)S(1)}, f32[456,128]{1,0:T(8,128)S(1)}, u32[]{:S(2)}, u32[]{:S(2)}) collective-permute-start(f32[456,128]{1,0:T(8,128)S(1)} %slice.6), channel_id=1, source_target_pairs={{0,4},{4,0},{8,12},{12,8},{1,5},{5,1},{9,13},{13,9},{2,6},{6,2},{1... | collective-permute-start | bytes 700424 | tf_op jit(solution)/shard_map/ppermute | solution.py:365
  38.4 11.5 %collective-permute-start.6 = (f32[800,128]{1,0:T(8,128)S(1)}, f32[800,128]{1,0:T(8,128)S(1)}, u32[]{:S(2)}, u32[]{:S(2)}) collective-permute-start(f32[800,128]{1,0:T(8,128)S(1)} %slice.7), channel_id=1, source_target_pairs={{0,4},{4,0},{8,12},{12,8},{1,5},{5,1},{9,13},{13,9},{2,6},{6,2},{1... | collective-permute-start | bytes 1228808 | tf_op jit(solution)/shard_map/ppermute | solution.py:365
  43.0 1.6 %collective-permute-start.4 = (f32[456,128]{1,0:T(8,128)S(1)}, f32[456,128]{1,0:T(8,128)S(1)}, u32[]{:S(2)}, u32[]{:S(2)}) collective-permute-start(f32[456,128]{1,0:T(8,128)S(1)} %get-tuple-element.42), channel_id=1, source_target_pairs={{0,1},{1,0},{2,3},{3,2},{4,5},{5,4},{6,7},{7,6},{8,9},{9,8},{10,11... | collective-permute-start | bytes 700424 | tf_op jit(solution)/shard_map/ppermute | solution.py:370
  43.0 8.9 %collective-permute-start.3 = (f32[456,128]{1,0:T(8,128)S(1)}, f32[456,128]{1,0:T(8,128)S(1)}, u32[]{:S(2)}, u32[]{:S(2)}) collective-permute-start(f32[456,128]{1,0:T(8,128)S(1)} %get-tuple-element.40), channel_id=1, source_target_pairs={{0,1},{1,0},{2,3},{3,2},{4,5},{5,4},{6,7},{7,6},{8,9},{9,8},{10,11... | collective-permute-start | bytes 700424 | tf_op jit(solution)/shard_map/ppermute | solution.py:370
  44.6 7.8 %collective-permute-start.5 = (f32[456,128]{1,0:T(8,128)S(1)}, f32[456,128]{1,0:T(8,128)S(1)}, u32[]{:S(2)}, u32[]{:S(2)}) collective-permute-start(f32[456,128]{1,0:T(8,128)S(1)} %add.34), channel_id=1, source_target_pairs={{0,2},{2,0},{1,3},{3,1},{4,6},{6,4},{5,7},{7,5},{8,10},{10,8},{9,1... | collective-permute-start | bytes 700424 | tf_op jit(solution)/shard_map/ppermute | solution.py:373
  51.3 1.8 %collective-permute-start.7 = (f32[800,128]{1,0:T(8,128)S(1)}, f32[800,128]{1,0:T(8,128)S(1)}, u32[]{:S(2)}, u32[]{:S(2)}) collective-permute-start(f32[800,128]{1,0:T(8,128)S(1)} %get-tuple-element.46), channel_id=1, source_target_pairs={{0,1},{1,0},{2,3},{3,2},{4,5},{5,4},{6,7},{7,6},{8,9},{9,8},{10,11... | collective-permute-start | bytes 1228808 | tf_op jit(solution)/shard_map/ppermute | solution.py:370
  51.4 3.1 %collective-permute-start.8 = (f32[800,128]{1,0:T(8,128)S(1)}, f32[800,128]{1,0:T(8,128)S(1)}, u32[]{:S(2)}, u32[]{:S(2)}) collective-permute-start(f32[800,128]{1,0:T(8,128)S(1)} %get-tuple-element.49), channel_id=1, source_target_pairs={{0,1},{1,0},{2,3},{3,2},{4,5},{5,4},{6,7},{7,6},{8,9},{9,8},{10,11... | collective-permute-start | bytes 1228808 | tf_op jit(solution)/shard_map/ppermute | solution.py:370
  53.2 11.6 %collective-permute-start.9 = (f32[800,128]{1,0:T(8,128)S(1)}, f32[800,128]{1,0:T(8,128)S(1)}, u32[]{:S(2)}, u32[]{:S(2)}) collective-permute-start(f32[800,128]{1,0:T(8,128)S(1)} %add.36), channel_id=1, source_target_pairs={{0,2},{2,0},{1,3},{3,1},{4,6},{6,4},{5,7},{7,5},{8,10},{10,8},{9,1... | collective-permute-start | bytes 1228808 | tf_op jit(solution)/shard_map/ppermute | solution.py:373

commit v4 on v3

--- a/solution.py
+++ b/solution.py
@@ -80,9 +80,11 @@
     return high, (value - high.astype(jnp.float32)).astype(jnp.bfloat16)
 
 
-def product(high, low, x_high, x_low):
+def product(weights, x_high, x_low):
+    rows = weights.shape[0] // 2
     dot = functools.partial(jnp.dot, preferred_element_type=jnp.float32)
-    return dot(high, x_high) + (dot(low, x_high) + dot(high, x_low))
+    value = dot(weights, x_high)
+    return value[:rows] + (value[rows:] + dot(weights[:rows], x_low))
 
 
 def pack(amps, chunks):
@@ -105,7 +107,7 @@
     rows = height // blocks
     tall, deep = -(-height // LANES) * LANES, -(-depth // LANES) * LANES
 
-    def kernel(meta, src, count, w_ref, high_ref, low_ref, total, turned, ordered):
+    def kernel(meta, src, count, w_ref, out, total, turned, ordered):
         s = pl.program_id(0)
 
         @pl.when(s == 0)
@@ -125,10 +127,11 @@
                     start = pl.multiple_of(meta[4 + j] * rows, 8)
                     ordered[j * rows : (j + 1) * rows] = turned[pl.ds(start, rows), :depth]
                 for h in range(2):
-                    high_ref[m, h], low_ref[m, h] = split(ordered[h * height // 2 : (h + 1) * height // 2])
-
-    block = pl.BlockSpec((npair, 2, height // 2, depth), lambda s, *_: (0, 0, 0, 0))
-    shape = jax.ShapeDtypeStruct((npair, 2, height // 2, depth), jnp.bfloat16)
+                    high, low = split(ordered[h * height // 2 : (h + 1) * height // 2])
+                    out[m, h, : height // 2] = high
+                    out[m, h, height // 2 :] = low
+
+    shape = (npair, 2, height, depth)
     return pl.pallas_call(
         kernel,
         grid_spec=pltpu.PrefetchScalarGridSpec(
@@ -139,14 +142,14 @@
                     (1, depth, height), lambda s, meta, src, count: (jnp.minimum(s, count[0] - 1), 0, 0)
                 )
             ],
-            out_specs=[block, block],
+            out_specs=pl.BlockSpec(shape, lambda s, *_: (0, 0, 0, 0)),
             scratch_shapes=[
                 pltpu.VMEM((npair, deep, tall), jnp.float32),
                 pltpu.VMEM((tall, deep), jnp.float32),
                 pltpu.VMEM((height, depth), jnp.float32),
             ],
         ),
-        out_shape=[shape, shape],
+        out_shape=jax.ShapeDtypeStruct(shape, jnp.bfloat16),
         compiler_params=limit(VMEM_MIB),
         name="sum_by_source",
     )(meta, cycle_src.reshape(-1), cycle_count, cycle_w)
@@ -160,11 +163,10 @@
 
 
 def own_products(chunks, meta, lad_src, lad_coef, energy, weights, amps, drive, eps_row, eps_col):
-    high, low = weights
-    _, _, height, _ = high.shape
+    height = weights.shape[2] // 2
     rows = drive.shape[0]
 
-    def kernel(meta, lad_src, lad_coef, energy, high, low, amps, drive, eps_row, eps_col, inverse, *outs):
+    def kernel(meta, lad_src, lad_coef, energy, weights, amps, drive, eps_row, eps_col, inverse, *outs):
         denom = eps_col[...] + eps_row[...] - energy[0]
         inverse[...] = 1.0 / denom
         weight = ladder_weight(meta[0], lad_src, lad_coef)
@@ -172,29 +174,28 @@
             mine = chunk.load(reader(amps, skip=chunk.start))
             x_high, x_low = split(mine)
             for h in range(2):
-                out[h] = product(high[meta[0], h], low[meta[0], h], x_high, x_low)
+                out[h] = product(weights[meta[0], h], x_high, x_low)
             denom = eps_col[...] + chunk.take(eps_row) - energy[0]
             base = chunk.take(drive) - denom * mine + weight * mine
             out[1, height - rows :] = out[1, height - rows :] + base
 
     return pl.pallas_call(
         kernel,
-        in_specs=[SMEM] * 4 + [VMEM] * 6,
+        in_specs=[SMEM] * 4 + [VMEM] * 5,
         out_specs=[VMEM] * (1 + len(chunks)),
         out_shape=[jax.ShapeDtypeStruct(drive.shape, jnp.float32)]
         + [jax.ShapeDtypeStruct((2, height, c.width), jnp.float32) for c in chunks],
         compiler_params=limit(VMEM_MIB),
         name="own_products",
-    )(meta, lad_src, lad_coef, energy, high, low, amps, drive, eps_row, eps_col)
+    )(meta, lad_src, lad_coef, energy, weights, amps, drive, eps_row, eps_col)
 
 
 def add_products(chunks, ks, meta, lad_src, lad_coef, weights, packed, sums):
-    high, low = weights
-    _, _, height, _ = high.shape
+    height = weights.shape[2] // 2
     rows = chunks[0].rows
     n = len(ks)
 
-    def kernel(meta, lad_src, lad_coef, high, low, *refs):
+    def kernel(meta, lad_src, lad_coef, weights, *refs):
         packed, refs = refs[:n], refs[n:]
         for c, chunk in enumerate(chunks):
             sums, out = refs[c :: len(chunks)]
@@ -203,7 +204,7 @@
             for h in range(2):
                 value = sums[h]
                 for k, (x_high, x_low) in zip(ks, parts, strict=True):
-                    value = value + product(high[meta[k], h], low[meta[k], h], x_high, x_low)
+                    value = value + product(weights[meta[k], h], x_high, x_low)
                 out[h] = value
             value = out[1, height - rows :]
             for k, x in zip(ks, amps, strict=True):
@@ -212,40 +213,37 @@
 
     return pl.pallas_call(
         kernel,
-        in_specs=[SMEM] * 3 + [VMEM] * (2 + n + len(chunks)),
+        in_specs=[SMEM] * 3 + [VMEM] * (1 + n + len(chunks)),
         out_specs=[VMEM] * len(chunks),
         out_shape=[jax.ShapeDtypeStruct(s.shape, jnp.float32) for s in sums],
         compiler_params=limit(VMEM_MIB),
         name="add_products",
-    )(meta, lad_src, lad_coef, high, low, *packed, *sums)
-
-
-def last_product(chunk, meta, lad_src, lad_coef, weights, amps, sums):
-    high, low = weights
-    npair, _, height, _ = high.shape
+    )(meta, lad_src, lad_coef, weights, *packed, *sums)
+
+
+def last_product(chunk, half, meta, lad_src, lad_coef, weights, amps, sums):
+    npair, height = weights.shape[0], weights.shape[2] // 2
     rows = chunk.rows
 
-    def kernel(meta, lad_src, lad_coef, high, low, amps, sums, *outs):
+    def kernel(meta, lad_src, lad_coef, weights, amps, sums, *outs):
         k = meta[npair - 1]
         x = chunk.load(reader(amps))
         x_high, x_low = split(x)
-        for h in range(2):
-            value = sums[h] + product(high[k, h], low[k, h], x_high, x_low)
-            for i in range(2):
-                part = value[i * rows : (i + 1) * rows]
-                if h and i:
-                    part = part + ladder_weight(k, lad_src, lad_coef) * x
-                chunk.store(writer(outs[2 * h + i]), part)
-
-    outs = pl.pallas_call(
-        kernel,
-        in_specs=[SMEM] * 3 + [VMEM] * 4,
-        out_specs=[VMEM] * 4,
-        out_shape=[jax.ShapeDtypeStruct((chunk.length, LANES), jnp.float32)] * 4,
+        value = sums[half] + product(weights[k, half], x_high, x_low)
+        for i in range(2):
+            part = value[i * rows : (i + 1) * rows]
+            if half and i:
+                part = part + ladder_weight(k, lad_src, lad_coef) * x
+            chunk.store(writer(outs[i]), part)
+
+    return pl.pallas_call(
+        kernel,
+        in_specs=[SMEM] * 3 + [VMEM] * 3,
+        out_specs=[VMEM] * 2,
+        out_shape=[jax.ShapeDtypeStruct((chunk.length, LANES), jnp.float32)] * 2,
         compiler_params=limit(VMEM_MIB),
         name="last_product",
-    )(meta, lad_src, lad_coef, high, low, amps, sums)
-    return outs[:2], outs[2:]
+    )(meta, lad_src, lad_coef, weights, amps, sums)
 
 
 def finish(chunks, done, pieces, shape, copies):
@@ -366,7 +364,10 @@
 
     done = []
     for i, chunk in enumerate(chunks):
-        away, keep = last_product(chunk, meta, ladder_src, ladder_coef, weights, last_amps[i], sums[i])
+        away, keep = [
+            last_product(chunk, half, meta, ladder_src, ladder_coef, weights, last_amps[i], sums[i])
+            for half in range(2)
+        ]
         got = [lax.ppermute(x, "rep", SWAP) for x in away]
         for_far = keep[0] + got[0]
         done, for_far = lax.optimization_barrier((done, for_far))

time: 79.3 us -> 79 us (level)
  waiting for transfers between devices: 32.4 us -> 30.6 us
  Pallas kernels: 12.8 us -> 14.3 us
    ppermute x4, waiting for transfers between devices: 1.73 us -> 0.13 us  [chain_body(): got = [lax.ppermute(x, 'rep', SWAP) for x in away]]
    pallas_call x4 -> x6, Pallas kernels: 8.33 us -> 9.81 us  [the longest x4 4.34 us: last_product(): pl.pallas_call(kernel, in_specs=[SMEM] * 3 + [VMEM] * 3, out_specs=[VMEM]...]
  transfers between devices with their start and end apart: 10 -> 10, of which waited for: 7 -> 5; matrix products, arithmetic and copies ran while one was open for 2% -> 2% of each run, Pallas kernels for 14% -> 16%
where the time goes in v4:
time: 79 us; the launch traced here: 78.6 us
  waiting for transfers between devices  30.6 us (39%)
  Pallas kernels  14.3 us (18%)
  blocking collectives  12.7 us (16%)
  starting transfers between devices  11.4 us (14%)
  local copies, waits for them, and re-layouts  6.1 us (8%)
  between operations  3.38 us (4%)
    ppermute x1, waiting for transfers between devices, chain_body(): far_amps = lax.ppermute(own, 'occ', FAR)  14.2 us
    all_to_all x1, blocking collectives, chain_body(): lax.all_to_all(total, ('occ', 'vir', 'rep'), split_axis=0, concat_axis=0,...  12.7 us
    ppermute x2, waiting for transfers between devices, chain_body(): far = lax.ppermute(for_far, 'vir', SWAP)  10.3 us
    ppermute x2, waiting for transfers between devices, chain_body(): last_amps = [lax.ppermute(x, 'occ', NEAR) for x in outgoing]  6.03 us
    unnamed x8, local copies, waits for them, and re-layouts  4.39 us
    pallas_call x4, Pallas kernels, last_product(): pl.pallas_call(kernel, in_specs=[SMEM] * 3 + [VMEM] * 3, out_specs=[VMEM]...  4.34 us
    ppermute x1, starting transfers between devices, chain_body(): far_amps = lax.ppermute(own, 'occ', FAR)  4.1 us
    pallas_call x1, Pallas kernels, add_products(): pl.pallas_call(kernel, in_specs=[SMEM] * 3 + [VMEM] * (1 + n + len(chunks...  3.38 us
  transfers between devices with their start and end apart: 10, of which 5 were waited for; matrix products, arithmetic and copies ran while one was open for 2% of the time, Pallas kernels for 16%

profile of v4, /device:TPU:0, one launch (start us, length us, event | category | flops | bytes accessed | tf_op | source)
XLA Modules:
  0.0 78.6 jit_solution(8795344794213972652)
XLA Ops:
  0.6 1.1 %copy-done.1 = f32[1,200,800]{2,1,0:T(8,128)S(1)} copy-done((f32[1,200,800]{2,1,0:T(8,128)S(1)}, f32[1,200,800]{2,1,0:T(8,128)}, u32[]{:S(2)}) %copy-start.1) | copy-done | bytes 640024
  1.7 0.1 pack.1.amps
  1.8 4.1 %collective-permute-start = (f32[1256,128]{1,0:T(8,128)S(1)}, f32[1256,128]{1,0:T(8,128)S(1)}, u32[]{:S(2)}, u32[]{:S(2)}) collective-permute-start(f32[1256,128]{1,0:T(8,128)S(1)} %pack.1.amps), channel_id=1, source_target_pairs={{0,8},{8,0},{4,12},{12,4},{1,9},{9,1},{5,13},{13,5},{2,10},{10,2},... | collective-permute-start | bytes 1929224 | tf_op jit(solution)/shard_map/ppermute | solution.py:351
  5.9 1.6 %collective-permute-start.2 = (f32[1256,128]{1,0:T(8,128)S(1)}, f32[1256,128]{1,0:T(8,128)S(1)}, u32[]{:S(2)}, u32[]{:S(2)}) collective-permute-start(f32[1256,128]{1,0:T(8,128)S(1)} %pack.1.amps), channel_id=1, source_target_pairs={{0,4},{4,0},{8,12},{12,8},{1,5},{5,1},{9,13},{13,9},{2,6},{6,2},{1... | collective-permute-start | bytes 1929224 | tf_op jit(solution)/shard_map/ppermute | solution.py:352
  10.1 0.7 reshape.14.eps_row
  10.8 0.8 dynamic_slice.3
  11.6 0.1 copy.11.eps_col
  11.7 0.1 stack.35.meta
  11.8 2.6 %copy-done = f32[1,8,800,200]{2,3,1,0:T(8,128)S(1)} copy-done((f32[1,8,800,200]{2,3,1,0:T(8,128)S(1)}, f32[1,8,800,200]{2,3,1,0:T(8,128)}, u32[]{:S(2)}) %copy-start) | copy-done | bytes 5120024
  14.4 0.7 copy-done.3
  15.1 2.9 %sum_by_source.1.weights = bf16[4,2,800,200]{3,2,1,0:T(8,128)(2,1)S(1)} custom-call(s32[8]{0:T(128)S(1)} %stack.35.meta, s32[8]{0:T(128)S(1)} %bitcast.20, s32[1]{0:T(128)S(6)} %copy.12.count, f32[8,200,800]{2,1,0:T(8,128)S(1)} %bitcast.17), custom_call_target="tpu_custom_call" | custom-call | tf_op jit(solution)/shard_map/sum_by_source/pallas_call | solution.py:135
  18.0 2.1 %own_products.1 = (f32[200,800]{1,0:T(8,128)S(1)}, f32[2,400,288]{2,1,0:T(8,128)S(1)}, f32[2,400,512]{2,1,0:T(8,128)S(1)}) custom-call(s32[8]{0:T(128)S(1)} %stack.35.meta, s32[1,1]{1,0:T(1,128)S(6)} %copy.13.lad_src, f32[1,1]{1,0:T(1,128)S(6)} %copy.14.lad_coef, f32[1]{0:T(128)S(6)} %copy.15.energy, bf16[4,2,800,200]{3,2,1,0:T(8,128)(2,1)S(1)} %sum_by_source.1.weights, ...), custom_call_target="tpu_custom_call" | custom-call | tf_op jit(solution)/shard_map/own_products/pallas_call | solution.py:182
  20.1 14.2 %collective-permute-done.refs_1_ = f32[1256,128]{1,0:T(8,128)S(1)} collective-permute-done((f32[1256,128]{1,0:T(8,128)S(1)}, f32[1256,128]{1,0:T(8,128)S(1)}, u32[]{:S(2)}, u32[]{:S(2)}) %collective-permute-start) | collective-permute-done | bytes 643104 | tf_op jit(solution)/shard_map/ppermute | solution.py:351
  34.3 0.7 collective-permute-start.1
  35.0 3.4 %add_products.1 = (f32[2,400,288]{2,1,0:T(8,128)S(1)}, f32[2,400,512]{2,1,0:T(8,128)S(1)}) custom-call(s32[8]{0:T(128)S(1)} %stack.35.meta, s32[1,1]{1,0:T(1,128)S(6)} %copy.13.lad_src, f32[1,1]{1,0:T(1,128)S(6)} %copy.14.lad_coef, bf16[4,2,800,200]{3,2,1,0:T(8,128)(2,1)S(1)} %sum_by_source.1.weights, f32[1256,128]{1,0:T(8,128)S(1)} %collective-permute-done.2.refs_0_, ...), custom_call_target="tpu_custom_call" | custom-call | tf_op jit(solution)/shard_map/add_products/pallas_call | solution.py:214
  38.4 1.5 %collective-permute-start.6 = (f32[800,128]{1,0:T(8,128)S(1)}, f32[800,128]{1,0:T(8,128)S(1)}, u32[]{:S(2)}, u32[]{:S(2)}) collective-permute-start(f32[800,128]{1,0:T(8,128)S(1)} %slice.7), channel_id=1, source_target_pairs={{0,4},{4,0},{8,12},{12,8},{1,5},{5,1},{9,13},{13,9},{2,6},{6,2},{1... | collective-permute-start | bytes 1228808 | tf_op jit(solution)/shard_map/ppermute | solution.py:363
  39.9 1.6 %collective-permute-done.1.amps = f32[456,128]{1,0:T(8,128)S(1)} collective-permute-done((f32[456,128]{1,0:T(8,128)S(1)}, f32[456,128]{1,0:T(8,128)S(1)}, u32[]{:S(2)}, u32[]{:S(2)}) %collective-permute-start.1) | collective-permute-done | bytes 233504 | tf_op jit(solution)/shard_map/ppermute | solution.py:363
  41.5 1.1 %last_product.5 = (f32[456,128]{1,0:T(8,128)S(1)}, f32[456,128]{1,0:T(8,128)S(1)}) custom-call(s32[8]{0:T(128)S(1)} %stack.35.meta, s32[1,1]{1,0:T(1,128)S(6)} %copy.13.lad_src, f32[1,1]{1,0:T(1,128)S(6)} %copy.14.lad_coef, bf16[4,2,800,200]{3,2,1,0:T(8,128)(2,1)S(1)} %sum_by_source.1.weights, f32[456,128]{1,0:T(8,128)S(1)} %collective-permute-done.1.amps, ...), custom_call_target="tpu_custom_call" | custom-call | tf_op jit(solution)/shard_map/last_product/pallas_call | solution.py:239
  42.6 0.1 collective-permute-start.4
  42.7 0.5 collective-permute-start.3
  43.2 1.1 %last_product.4 = (f32[456,128]{1,0:T(8,128)S(1)}, f32[456,128]{1,0:T(8,128)S(1)}) custom-call(s32[8]{0:T(128)S(1)} %stack.35.meta, s32[1,1]{1,0:T(1,128)S(6)} %copy.13.lad_src, f32[1,1]{1,0:T(1,128)S(6)} %copy.14.lad_coef, bf16[4,2,800,200]{3,2,1,0:T(8,128)(2,1)S(1)} %sum_by_source.1.weights, f32[456,128]{1,0:T(8,128)S(1)} %collective-permute-done.1.amps, ...), custom_call_target="tpu_custom_call" | custom-call | tf_op jit(solution)/shard_map/last_product/pallas_call | solution.py:239
  44.4 1.1 %collective-permute-start.5 = (f32[456,128]{1,0:T(8,128)S(1)}, f32[456,128]{1,0:T(8,128)S(1)}, u32[]{:S(2)}, u32[]{:S(2)}) collective-permute-start(f32[456,128]{1,0:T(8,128)S(1)} %add.34), channel_id=1, source_target_pairs={{0,2},{2,0},{1,3},{3,1},{4,6},{6,4},{5,7},{7,5},{8,10},{10,8},{9,1... | collective-permute-start | bytes 700424 | tf_op jit(solution)/shard_map/ppermute | solution.py:374
  45.5 4.4 %collective-permute-done.6.amps = f32[800,128]{1,0:T(8,128)S(1)} collective-permute-done((f32[800,128]{1,0:T(8,128)S(1)}, f32[800,128]{1,0:T(8,128)S(1)}, u32[]{:S(2)}, u32[]{:S(2)}) %collective-permute-start.6) | collective-permute-done | bytes 409632 | tf_op jit(solution)/shard_map/ppermute | solution.py:363
  50.0 1.0 %last_product.7 = (f32[800,128]{1,0:T(8,128)S(1)}, f32[800,128]{1,0:T(8,128)S(1)}) custom-call(s32[8]{0:T(128)S(1)} %stack.35.meta, s32[1,1]{1,0:T(1,128)S(6)} %copy.13.lad_src, f32[1,1]{1,0:T(1,128)S(6)} %copy.14.lad_coef, bf16[4,2,800,200]{3,2,1,0:T(8,128)(2,1)S(1)} %sum_by_source.1.weights, f32[800,128]{1,0:T(8,128)S(1)} %collective-permute-done.6.amps, ...), custom_call_target="tpu_custom_call" | custom-call | tf_op jit(solution)/shard_map/last_product/pallas_call | solution.py:239
  51.1 0.5 collective-permute-start.8
  51.6 1.0 %last_product.6 = (f32[800,128]{1,0:T(8,128)S(1)}, f32[800,128]{1,0:T(8,128)S(1)}) custom-call(s32[8]{0:T(128)S(1)} %stack.35.meta, s32[1,1]{1,0:T(1,128)S(6)} %copy.13.lad_src, f32[1,1]{1,0:T(1,128)S(6)} %copy.14.lad_coef, bf16[4,2,800,200]{3,2,1,0:T(8,128)(2,1)S(1)} %sum_by_source.1.weights, f32[800,128]{1,0:T(8,128)S(1)} %collective-permute-done.6.amps, ...), custom_call_target="tpu_custom_call" | custom-call | tf_op jit(solution)/shard_map/last_product/pallas_call | solution.py:239
  52.7 0.1 collective-permute-done.7
  52.9 1.3 %collective-permute-start.9 = (f32[800,128]{1,0:T(8,128)S(1)}, f32[800,128]{1,0:T(8,128)S(1)}, u32[]{:S(2)}, u32[]{:S(2)}) collective-permute-start(f32[800,128]{1,0:T(8,128)S(1)} %add.36), channel_id=1, source_target_pairs={{0,2},{2,0},{1,3},{3,1},{4,6},{6,4},{5,7},{7,5},{8,10},{10,8},{9,1... | collective-permute-start | bytes 1228808 | tf_op jit(solution)/shard_map/ppermute | solution.py:374
  54.2 10.3 %collective-permute-done.9.refs_3_ = f32[800,128]{1,0:T(8,128)S(1)} collective-permute-done((f32[800,128]{1,0:T(8,128)S(1)}, f32[800,128]{1,0:T(8,128)S(1)}, u32[]{:S(2)}, u32[]{:S(2)}) %collective-permute-start.9) | collective-permute-done | bytes 409632 | tf_op jit(solution)/shard_map/ppermute | solution.py:374
  64.4 0.3 finish.1
  64.8 12.7 %all_to_all.5.total = f32[16,1,128]{2,1,0:T(1,128)S(1)} all-to-all(f32[16,1,128]{2,1,0:T(1,128)S(1)} %get-tuple-element.48), channel_id=1, replica_groups=mesh['groups'=2,'occ'=4,'vir'=2,'rep'=2] {'occ','vir','rep'}, dimensions={0} | all-to-all | bytes 16384 | tf_op jit(solution)/shard_map/all_to_all | solution.py:379
  77.5 1.1 %jacobi.1 = (f32[200,800]{1,0:T(8,128)}, f32[200,800]{1,0:T(8,128)}) custom-call(f32[200,800]{1,0:T(8,128)S(1)} %get-tuple-element.47.residual, f32[16,1,128]{2,1,0:T(1,128)S(1)} %all_to_all.5.total, f32[200,800]{1,0:T(8,128)S(1)} %get-tuple-element.49.inverse), custom_call_target="tpu_custom_call" | custom-call | tf_op jit(solution)/shard_map/jacobi/pallas_call | solution.py:317
  (16 shorter events, 0.3 us)
Async XLA Ops:
  0.6 1.1 %copy-start.1 = (f32[1,200,800]{2,1,0:T(8,128)S(1)}, f32[1,200,800]{2,1,0:T(8,128)}, u32[]{:S(2)}) copy-start(f32[1,200,800]{2,1,0:T(8,128)} %param.9) | copy-start | bytes 1920004
  1.8 32.5 %collective-permute-start = (f32[1256,128]{1,0:T(8,128)S(1)}, f32[1256,128]{1,0:T(8,128)S(1)}, u32[]{:S(2)}, u32[]{:S(2)}) collective-permute-start(f32[1256,128]{1,0:T(8,128)S(1)} %pack.1.amps), channel_id=1, source_target_pairs={{0,8},{8,0},{4,12},{12,4},{1,9},{9,1},{5,13},{13,5},{2,10},{10,2},... | collective-permute-start | bytes 1929224 | tf_op jit(solution)/shard_map/ppermute | solution.py:351
  5.9 29.1 %collective-permute-start.2 = (f32[1256,128]{1,0:T(8,128)S(1)}, f32[1256,128]{1,0:T(8,128)S(1)}, u32[]{:S(2)}, u32[]{:S(2)}) collective-permute-start(f32[1256,128]{1,0:T(8,128)S(1)} %pack.1.amps), channel_id=1, source_target_pairs={{0,4},{4,0},{8,12},{12,8},{1,5},{5,1},{9,13},{13,9},{2,6},{6,2},{1... | collective-permute-start | bytes 1929224 | tf_op jit(solution)/shard_map/ppermute | solution.py:352
  11.8 2.6 %copy-start = (f32[1,8,800,200]{2,3,1,0:T(8,128)S(1)}, f32[1,8,800,200]{2,3,1,0:T(8,128)}, u32[]{:S(2)}) copy-start(f32[1,8,800,200]{2,3,1,0:T(8,128)} %param.11) | copy-start | bytes 15360004
  14.4 0.7 copy-start.3
  15.1 2.9 %copy-start.2 = (f32[1,200,800]{2,1,0:T(8,128)S(1)}, f32[1,200,800]{2,1,0:T(8,128)}, u32[]{:S(2)}) copy-start(f32[1,200,800]{2,1,0:T(8,128)} %param.10) | copy-start | bytes 1920004
  34.3 7.2 %collective-permute-start.1 = (f32[456,128]{1,0:T(8,128)S(1)}, f32[456,128]{1,0:T(8,128)S(1)}, u32[]{:S(2)}, u32[]{:S(2)}) collective-permute-start(f32[456,128]{1,0:T(8,128)S(1)} %slice.6), channel_id=1, source_target_pairs={{0,4},{4,0},{8,12},{12,8},{1,5},{5,1},{9,13},{13,9},{2,6},{6,2},{1... | collective-permute-start | bytes 700424 | tf_op jit(solution)/shard_map/ppermute | solution.py:363
  38.4 11.5 %collective-permute-start.6 = (f32[800,128]{1,0:T(8,128)S(1)}, f32[800,128]{1,0:T(8,128)S(1)}, u32[]{:S(2)}, u32[]{:S(2)}) collective-permute-start(f32[800,128]{1,0:T(8,128)S(1)} %slice.7), channel_id=1, source_target_pairs={{0,4},{4,0},{8,12},{12,8},{1,5},{5,1},{9,13},{13,9},{2,6},{6,2},{1... | collective-permute-start | bytes 1228808 | tf_op jit(solution)/shard_map/ppermute | solution.py:363
  42.6 1.7 %collective-permute-start.4 = (f32[456,128]{1,0:T(8,128)S(1)}, f32[456,128]{1,0:T(8,128)S(1)}, u32[]{:S(2)}, u32[]{:S(2)}) collective-permute-start(f32[456,128]{1,0:T(8,128)S(1)} %get-tuple-element.38), channel_id=1, source_target_pairs={{0,1},{1,0},{2,3},{3,2},{4,5},{5,4},{6,7},{7,6},{8,9},{9,8},{10,11... | collective-permute-start | bytes 700424 | tf_op jit(solution)/shard_map/ppermute | solution.py:371
  42.7 9.9 %collective-permute-start.3 = (f32[456,128]{1,0:T(8,128)S(1)}, f32[456,128]{1,0:T(8,128)S(1)}, u32[]{:S(2)}, u32[]{:S(2)}) collective-permute-start(f32[456,128]{1,0:T(8,128)S(1)} %get-tuple-element.36), channel_id=1, source_target_pairs={{0,1},{1,0},{2,3},{3,2},{4,5},{5,4},{6,7},{7,6},{8,9},{9,8},{10,11... | collective-permute-start | bytes 700424 | tf_op jit(solution)/shard_map/ppermute | solution.py:371
  44.4 8.2 %collective-permute-start.5 = (f32[456,128]{1,0:T(8,128)S(1)}, f32[456,128]{1,0:T(8,128)S(1)}, u32[]{:S(2)}, u32[]{:S(2)}) collective-permute-start(f32[456,128]{1,0:T(8,128)S(1)} %add.34), channel_id=1, source_target_pairs={{0,2},{2,0},{1,3},{3,1},{4,6},{6,4},{5,7},{7,5},{8,10},{10,8},{9,1... | collective-permute-start | bytes 700424 | tf_op jit(solution)/shard_map/ppermute | solution.py:374
  51.0 1.8 %collective-permute-start.7 = (f32[800,128]{1,0:T(8,128)S(1)}, f32[800,128]{1,0:T(8,128)S(1)}, u32[]{:S(2)}, u32[]{:S(2)}) collective-permute-start(f32[800,128]{1,0:T(8,128)S(1)} %get-tuple-element.42), channel_id=1, source_target_pairs={{0,1},{1,0},{2,3},{3,2},{4,5},{5,4},{6,7},{7,6},{8,9},{9,8},{10,11... | collective-permute-start | bytes 1228808 | tf_op jit(solution)/shard_map/ppermute | solution.py:371
  51.1 3.1 %collective-permute-start.8 = (f32[800,128]{1,0:T(8,128)S(1)}, f32[800,128]{1,0:T(8,128)S(1)}, u32[]{:S(2)}, u32[]{:S(2)}) collective-permute-start(f32[800,128]{1,0:T(8,128)S(1)} %get-tuple-element.45), channel_id=1, source_target_pairs={{0,1},{1,0},{2,3},{3,2},{4,5},{5,4},{6,7},{7,6},{8,9},{9,8},{10,11... | collective-permute-start | bytes 1228808 | tf_op jit(solution)/shard_map/ppermute | solution.py:371
  52.9 11.6 %collective-permute-start.9 = (f32[800,128]{1,0:T(8,128)S(1)}, f32[800,128]{1,0:T(8,128)S(1)}, u32[]{:S(2)}, u32[]{:S(2)}) collective-permute-start(f32[800,128]{1,0:T(8,128)S(1)} %add.36), channel_id=1, source_target_pairs={{0,2},{2,0},{1,3},{3,1},{4,6},{6,4},{5,7},{7,5},{8,10},{10,8},{9,1... | collective-permute-start | bytes 1228808 | tf_op jit(solution)/shard_map/ppermute | solution.py:374

commit v5 on v4

--- a/solution.py
+++ b/solution.py
@@ -17,7 +17,6 @@
 NEAR = [(0, 1), (1, 0), (2, 3), (3, 2)]
 FAR = [(0, 2), (2, 0), (1, 3), (3, 1)]
 VMEM_MIB = 20
-FIRST_TILES = 2
 
 
 def limit(n):
@@ -98,6 +97,7 @@
         in_specs=[VMEM],
         out_specs=VMEM,
         out_shape=pltpu.VMEM((length, LANES), jnp.float32),
+        compiler_params=limit(VMEM_MIB),
         name="pack",
     )(pltpu.with_memory_space_constraint(amps, pltpu.VMEM))
 
@@ -221,7 +221,7 @@
     )(meta, lad_src, lad_coef, weights, *packed, *sums)
 
 
-def last_product(chunk, half, meta, lad_src, lad_coef, weights, amps, sums):
+def last_product(chunk, halves, meta, lad_src, lad_coef, weights, amps, sums):
     npair, height = weights.shape[0], weights.shape[2] // 2
     rows = chunk.rows
 
@@ -229,21 +229,30 @@
         k = meta[npair - 1]
         x = chunk.load(reader(amps))
         x_high, x_low = split(x)
-        value = sums[half] + product(weights[k, half], x_high, x_low)
-        for i in range(2):
-            part = value[i * rows : (i + 1) * rows]
-            if half and i:
-                part = part + ladder_weight(k, lad_src, lad_coef) * x
-            chunk.store(writer(outs[i]), part)
-
-    return pl.pallas_call(
+        for n, half in enumerate(halves):
+            value = sums[half] + product(weights[k, half], x_high, x_low)
+            for i in range(2):
+                part = value[i * rows : (i + 1) * rows]
+                if half and i:
+                    part = part + ladder_weight(k, lad_src, lad_coef) * x
+                chunk.store(writer(outs[2 * n + i]), part)
+
+    outs = pl.pallas_call(
         kernel,
         in_specs=[SMEM] * 3 + [VMEM] * 3,
-        out_specs=[VMEM] * 2,
-        out_shape=[jax.ShapeDtypeStruct((chunk.length, LANES), jnp.float32)] * 2,
+        out_specs=[VMEM] * (2 * len(halves)),
+        out_shape=[jax.ShapeDtypeStruct((chunk.length, LANES), jnp.float32)] * (2 * len(halves)),
         compiler_params=limit(VMEM_MIB),
         name="last_product",
     )(meta, lad_src, lad_coef, weights, amps, sums)
+    return [list(outs[2 * n : 2 * n + 2]) for n in range(len(halves))]
+
+
+def from_other_core(parts):
+    n = parts[0].shape[0]
+    both = lax.all_gather(jnp.concatenate(parts), "rep", axis=0, tiled=True)
+    total = 0.5 * both[: 2 * n] + 0.5 * both[2 * n :]
+    return [2.0 * (total[i * n : (i + 1) * n] - 0.5 * part) for i, part in enumerate(parts)]
 
 
 def finish(chunks, done, pieces, shape, copies):
@@ -344,8 +353,9 @@
     eps_col = lax.dynamic_slice_in_dim(eps_vir, (2 * chip + core) * rows, rows).reshape(rows, 1)
 
     chunks, first, start = [], 0, 0
-    for count in (FIRST_TILES, width // LANES - FIRST_TILES):
-        chunks.append(Chunk(rows, width, first, count, not first, start))
+    third = width // LANES // 3
+    for count in (third, third, width // LANES - 2 * third):
+        chunks.append(Chunk(rows, width, first, count, first + count == width // LANES, start))
         first, start = first + count, start + chunks[-1].length
     own = pack(amps[0], chunks)
     far_amps = lax.ppermute(own, "occ", FAR)
@@ -360,20 +370,28 @@
     )
     outgoing = [far_amps[c.start : c.start + c.length] for c in chunks]
     outgoing[1:], sums = lax.optimization_barrier((outgoing[1:], sums))
-    last_amps = [lax.ppermute(x, "occ", NEAR) for x in outgoing]
+    last_amps = [lax.ppermute(x, "occ", NEAR) for x in outgoing[:2]]
 
     done = []
     for i, chunk in enumerate(chunks):
-        away, keep = [
-            last_product(chunk, half, meta, ladder_src, ladder_coef, weights, last_amps[i], sums[i])
-            for half in range(2)
-        ]
-        got = [lax.ppermute(x, "rep", SWAP) for x in away]
+        parts = (meta, ladder_src, ladder_coef, weights, last_amps[i], sums[i])
+        if i < 2:
+            away, keep = last_product(chunk, (0, 1), *parts)
+        else:
+            (away,), (keep,) = [last_product(chunk, (half,), *parts) for half in range(2)]
+        if i == 0:
+            away[0], outgoing[2] = lax.optimization_barrier((away[0], outgoing[2]))
+            last_amps.append(lax.ppermute(outgoing[2], "occ", NEAR))
+        if i < 2:
+            got = from_other_core(away)
+        else:
+            got = [lax.ppermute(x, "rep", SWAP) for x in away]
         for_far = keep[0] + got[0]
-        done, for_far = lax.optimization_barrier((done, for_far))
+        if i == 2:
+            done[0], for_far = lax.optimization_barrier((done[0], for_far))
         far = lax.ppermute(for_far, "vir", SWAP)
         pieces = (keep[1], got[1], far)
-        if i < len(chunks) - 1:
+        if i < 2:
             done.append(sum(pieces))
     residual, total = finish(chunks, done, pieces, (rows, width), npair * blocks)
     total = lax.all_to_all(total, ("occ", "vir", "rep"), split_axis=0, concat_axis=0, tiled=True)
@@ -414,7 +432,7 @@
         and cycle_w.shape[1] >= 4
         and rows % 8 == 0
         and width % LANES == LANES // 4
-        and width > (FIRST_TILES + 1) * LANES
+        and width >= 3 * LANES
     )
     return (chain_body if chain else any_body)(*args)
 

time: 79 us -> 77 us (0.975)
  waiting for transfers between devices: 30.6 us -> 21.9 us
  blocking collectives: 12.7 us -> 16.3 us
  starting transfers between devices: 11.4 us -> 14.3 us
    ppermute x2 -> x3, waiting for transfers between devices: 6.03 us -> 0.71 us  [the longest x2 0.7 us: chain_body(): last_amps = [lax.ppermute(x, 'occ', NEAR) for x in outgoing[:2]]]
    all_gather x0 -> x2, blocking collectives: none -> 4.79 us  [from_other_core(): both = lax.all_gather(jnp.concatenate(parts), 'rep', axis=0, tiled=True)]
    ppermute x2 -> x3, waiting for transfers between devices: 10.3 us -> 6.96 us  [chain_body(): far = lax.ppermute(for_far, 'vir', SWAP)]
    ppermute x2 -> x3, starting transfers between devices: 2.16 us -> 4.15 us  [the longest x2 2.16 us: chain_body(): last_amps = [lax.ppermute(x, 'occ', NEAR) for x in outgoing[:2]]]
    ppermute x2 -> x3, starting transfers between devices: 2.43 us -> 4.13 us  [chain_body(): far = lax.ppermute(for_far, 'vir', SWAP)]
    all_to_all x1, blocking collectives: 12.7 us -> 11.5 us  [chain_body(): lax.all_to_all(total, ('occ', 'vir', 'rep'), split_axis=0, concat_axis=0,...]
  transfers between devices with their start and end apart: 10 -> 10, of which waited for: 5 -> 5; matrix products, arithmetic and copies ran while one was open for 2% -> 3% of each run, Pallas kernels for 16% -> 17%
where the time goes in v5:
time: 77 us; the launch traced here: 76.6 us
  waiting for transfers between devices  21.9 us (28%)
  blocking collectives  16.3 us (21%)
  starting transfers between devices  14.3 us (19%)
  Pallas kernels  14.1 us (18%)
  local copies, waits for them, and re-layouts  6.1 us (8%)
  between operations  3.4 us (4%)
    ppermute x1, waiting for transfers between devices, chain_body(): far_amps = lax.ppermute(own, 'occ', FAR)  14.2 us
    all_to_all x1, blocking collectives, chain_body(): lax.all_to_all(total, ('occ', 'vir', 'rep'), split_axis=0, concat_axis=0,...  11.5 us
    ppermute x3, waiting for transfers between devices, chain_body(): far = lax.ppermute(for_far, 'vir', SWAP)  6.96 us
    all_gather x2, blocking collectives, from_other_core(): both = lax.all_gather(jnp.concatenate(parts), 'rep', axis=0, tiled=True)  4.79 us
    unnamed x8, local copies, waits for them, and re-layouts  4.39 us
    pallas_call x4, Pallas kernels, last_product(): pl.pallas_call(kernel, in_specs=[SMEM] * 3 + [VMEM] * 3, out_specs=[VMEM]...  4.31 us
    ppermute x3, starting transfers between devices, chain_body(): far = lax.ppermute(for_far, 'vir', SWAP)  4.13 us
    ppermute x1, starting transfers between devices, chain_body(): far_amps = lax.ppermute(own, 'occ', FAR)  4.1 us
  transfers between devices with their start and end apart: 10, of which 5 were waited for; matrix products, arithmetic and copies ran while one was open for 3% of the time, Pallas kernels for 17%

profile of v5, /device:TPU:0, one launch (start us, length us, event | category | flops | bytes accessed | tf_op | source)
XLA Modules:
  0.0 76.6 jit_solution(858609537366858140)
XLA Ops:
  0.6 1.1 %copy-done.1 = f32[1,200,800]{2,1,0:T(8,128)S(1)} copy-done((f32[1,200,800]{2,1,0:T(8,128)S(1)}, f32[1,200,800]{2,1,0:T(8,128)}, u32[]{:S(2)}) %copy-start.1) | copy-done | bytes 640024
  1.8 4.1 %collective-permute-start = (f32[1256,128]{1,0:T(8,128)S(1)}, f32[1256,128]{1,0:T(8,128)S(1)}, u32[]{:S(2)}, u32[]{:S(2)}) collective-permute-start(f32[1256,128]{1,0:T(8,128)S(1)} %pack.1.amps), channel_id=1, source_target_pairs={{0,8},{8,0},{4,12},{12,4},{1,9},{9,1},{5,13},{13,5},{2,10},{10,2},... | collective-permute-start | bytes 1929224 | tf_op jit(solution)/shard_map/ppermute | solution.py:361
  5.9 1.6 %collective-permute-start.2 = (f32[1256,128]{1,0:T(8,128)S(1)}, f32[1256,128]{1,0:T(8,128)S(1)}, u32[]{:S(2)}, u32[]{:S(2)}) collective-permute-start(f32[1256,128]{1,0:T(8,128)S(1)} %pack.1.amps), channel_id=1, source_target_pairs={{0,4},{4,0},{8,12},{12,8},{1,5},{5,1},{9,13},{13,9},{2,6},{6,2},{1... | collective-permute-start | bytes 1929224 | tf_op jit(solution)/shard_map/ppermute | solution.py:362
  10.1 0.7 reshape.14.eps_row
  10.8 0.8 dynamic_slice.3
  11.6 0.1 copy.11.eps_col
  11.8 2.6 %copy-done = f32[1,8,800,200]{2,3,1,0:T(8,128)S(1)} copy-done((f32[1,8,800,200]{2,3,1,0:T(8,128)S(1)}, f32[1,8,800,200]{2,3,1,0:T(8,128)}, u32[]{:S(2)}) %copy-start) | copy-done | bytes 5120024
  14.4 0.7 copy-done.3
  15.1 2.9 %sum_by_source.1.weights = bf16[4,2,800,200]{3,2,1,0:T(8,128)(2,1)S(1)} custom-call(s32[8]{0:T(128)S(1)} %stack.35.meta, s32[8]{0:T(128)S(1)} %bitcast.20, s32[1]{0:T(128)S(6)} %copy.12.count, f32[8,200,800]{2,1,0:T(8,128)S(1)} %bitcast.17), custom_call_target="tpu_custom_call" | custom-call | tf_op jit(solution)/shard_map/sum_by_source/pallas_call | solution.py:135
  18.0 2.1 %own_products.1 = (f32[200,800]{1,0:T(8,128)S(1)}, f32[2,400,256]{2,1,0:T(8,128)S(1)}, f32[2,400,256]{2,1,0:T(8,128)S(1)}, f32[2,400,288]{2,1,0:T(8,128)S(1)}) custom-call(s32[8]{0:T(128)S(1)} %stack.35.meta, s32[1,1]{1,0:T(1,128)S(6)} %copy.13.lad_src, f32[1,1]{1,0:T(1,128)S(6)} %copy.14.lad_coef, f32[1]{0:T(128)S(6)} %copy.15.energy, ...), custom_call_target="tpu_custom_call" | custom-call | tf_op jit(solution)/shard_map/own_products/pallas_call | solution.py:182
  20.1 14.2 %collective-permute-done.refs_1_ = f32[1256,128]{1,0:T(8,128)S(1)} collective-permute-done((f32[1256,128]{1,0:T(8,128)S(1)}, f32[1256,128]{1,0:T(8,128)S(1)}, u32[]{:S(2)}, u32[]{:S(2)}) %collective-permute-start) | collective-permute-done | bytes 643104 | tf_op jit(solution)/shard_map/ppermute | solution.py:361
  34.3 0.7 collective-permute-start.1
  35.0 3.4 %add_products.1 = (f32[2,400,256]{2,1,0:T(8,128)S(1)}, f32[2,400,256]{2,1,0:T(8,128)S(1)}, f32[2,400,288]{2,1,0:T(8,128)S(1)}) custom-call(s32[8]{0:T(128)S(1)} %stack.35.meta, s32[1,1]{1,0:T(1,128)S(6)} %copy.13.lad_src, f32[1,1]{1,0:T(1,128)S(6)} %copy.14.lad_coef, bf16[4,2,800,200]{3,2,1,0:T(8,128)(2,1)S(1)} %sum_by_source.1.weights, ...), custom_call_target="tpu_custom_call" | custom-call | tf_op jit(solution)/shard_map/add_products/pallas_call | solution.py:214
  38.4 1.5 %collective-permute-start.6 = (f32[400,128]{1,0:T(8,128)S(1)}, f32[400,128]{1,0:T(8,128)S(1)}, u32[]{:S(2)}, u32[]{:S(2)}) collective-permute-start(f32[400,128]{1,0:T(8,128)S(1)} %get-tuple-element.60), channel_id=1, source_target_pairs={{0,4},{4,0},{8,12},{12,8},{1,5},{5,1},{9,13},{13,9},{2,6},{6,2},{1... | collective-permute-start | bytes 614408 | tf_op jit(solution)/shard_map/ppermute | solution.py:373
  39.9 0.7 collective-permute-done.1.amps
  40.6 1.0 %last_product.4 = (f32[400,128]{1,0:T(8,128)S(1)}, f32[400,128]{1,0:T(8,128)S(1)}, f32[400,128]{1,0:T(8,128)S(1)}, f32[400,128]{1,0:T(8,128)S(1)}) custom-call(s32[8]{0:T(128)S(1)} %stack.35.meta, s32[1,1]{1,0:T(1,128)S(6)} %copy.13.lad_src, f32[1,1]{1,0:T(1,128)S(6)} %copy.14.lad_coef, bf16[4,2,800,200]{3,2,1,0:T(8,128)(2,1)S(1)} %sum_by_source.1.weights, ...), custom_call_target="tpu_custom_call" | custom-call | tf_op jit(solution)/shard_map/last_product/pallas_call | solution.py:240
  41.6 2.0 %collective-permute-start.4 = (f32[456,128]{1,0:T(8,128)S(1)}, f32[456,128]{1,0:T(8,128)S(1)}, u32[]{:S(2)}, u32[]{:S(2)}) collective-permute-start(f32[456,128]{1,0:T(8,128)S(1)} %slice.35), channel_id=1, source_target_pairs={{0,4},{4,0},{8,12},{12,8},{1,5},{5,1},{9,13},{13,9},{2,6},{6,2},{1... | collective-permute-start | bytes 700424 | tf_op jit(solution)/shard_map/ppermute | solution.py:384
  43.6 2.4 %all_gather.6 = f32[1600,128]{1,0:T(8,128)S(1)} all-gather(f32[800,128]{1,0:T(8,128)S(1)} %pad_maximum_fusion), channel_id=1, replica_groups=mesh['groups'=2,'occ'=4,'vir'=2,'rep'=2] {'rep'}, dimensions={0}, use_global_device_ids=true | all-gather | bytes 1228800 | tf_op jit(solution)/shard_map/all_gather | solution.py:253
  46.1 1.8 %collective-permute-start.3 = (f32[400,128]{1,0:T(8,128)S(1)}, f32[400,128]{1,0:T(8,128)S(1)}, u32[]{:S(2)}, u32[]{:S(2)}) collective-permute-start(f32[400,128]{1,0:T(8,128)S(1)} %fusion.8), channel_id=1, source_target_pairs={{0,2},{2,0},{1,3},{3,1},{4,6},{6,4},{5,7},{7,5},{8,10},{10,8},{9,1... | collective-permute-start | bytes 614408 | tf_op jit(solution)/shard_map/ppermute | solution.py:392
  47.9 1.0 %last_product.7 = (f32[400,128]{1,0:T(8,128)S(1)}, f32[400,128]{1,0:T(8,128)S(1)}, f32[400,128]{1,0:T(8,128)S(1)}, f32[400,128]{1,0:T(8,128)S(1)}) custom-call(s32[8]{0:T(128)S(1)} %stack.35.meta, s32[1,1]{1,0:T(1,128)S(6)} %copy.13.lad_src, f32[1,1]{1,0:T(1,128)S(6)} %copy.14.lad_coef, bf16[4,2,800,200]{3,2,1,0:T(8,128)(2,1)S(1)} %sum_by_source.1.weights, ...), custom_call_target="tpu_custom_call" | custom-call | tf_op jit(solution)/shard_map/last_product/pallas_call | solution.py:240
  49.0 2.4 %all_gather.7 = f32[1600,128]{1,0:T(8,128)S(1)} all-gather(f32[800,128]{1,0:T(8,128)S(1)} %pad_maximum_fusion.1), channel_id=1, replica_groups=mesh['groups'=2,'occ'=4,'vir'=2,'rep'=2] {'rep'}, dimensions={0}, use_global_device_ids=true | all-gather | bytes 1228800 | tf_op jit(solution)/shard_map/all_gather | solution.py:253
  51.5 0.4 collective-permute-start.7
  51.8 1.1 %last_product.6 = (f32[456,128]{1,0:T(8,128)S(1)}, f32[456,128]{1,0:T(8,128)S(1)}) custom-call(s32[8]{0:T(128)S(1)} %stack.35.meta, s32[1,1]{1,0:T(1,128)S(6)} %copy.13.lad_src, f32[1,1]{1,0:T(1,128)S(6)} %copy.14.lad_coef, bf16[4,2,800,200]{3,2,1,0:T(8,128)(2,1)S(1)} %sum_by_source.1.weights, f32[456,128]{1,0:T(8,128)S(1)} %collective-permute-done.4.amps, ...), custom_call_target="tpu_custom_call" | custom-call | tf_op jit(solution)/shard_map/last_product/pallas_call | solution.py:240
  53.1 0.2 collective-permute-done.3
  53.4 0.3 collective-permute-start.8
  53.7 1.1 %last_product.5 = (f32[456,128]{1,0:T(8,128)S(1)}, f32[456,128]{1,0:T(8,128)S(1)}) custom-call(s32[8]{0:T(128)S(1)} %stack.35.meta, s32[1,1]{1,0:T(1,128)S(6)} %copy.13.lad_src, f32[1,1]{1,0:T(1,128)S(6)} %copy.14.lad_coef, bf16[4,2,800,200]{3,2,1,0:T(8,128)(2,1)S(1)} %sum_by_source.1.weights, f32[456,128]{1,0:T(8,128)S(1)} %collective-permute-done.4.amps, ...), custom_call_target="tpu_custom_call" | custom-call | tf_op jit(solution)/shard_map/last_product/pallas_call | solution.py:240
  54.9 2.0 %collective-permute-start.9 = (f32[456,128]{1,0:T(8,128)S(1)}, f32[456,128]{1,0:T(8,128)S(1)}, u32[]{:S(2)}, u32[]{:S(2)}) collective-permute-start(f32[456,128]{1,0:T(8,128)S(1)} %add.54), channel_id=1, source_target_pairs={{0,2},{2,0},{1,3},{3,1},{4,6},{6,4},{5,7},{7,5},{8,10},{10,8},{9,1... | collective-permute-start | bytes 700424 | tf_op jit(solution)/shard_map/ppermute | solution.py:392
  56.9 2.2 %collective-permute-done.7 = f32[400,128]{1,0:T(8,128)S(1)} collective-permute-done((f32[400,128]{1,0:T(8,128)S(1)}, f32[400,128]{1,0:T(8,128)S(1)}, u32[]{:S(2)}, u32[]{:S(2)}) %collective-permute-start.7) | collective-permute-done | bytes 204832 | tf_op jit(solution)/shard_map/ppermute | solution.py:392
  59.1 4.5 %collective-permute-done.9.refs_4_ = f32[456,128]{1,0:T(8,128)S(1)} collective-permute-done((f32[456,128]{1,0:T(8,128)S(1)}, f32[456,128]{1,0:T(8,128)S(1)}, u32[]{:S(2)}, u32[]{:S(2)}) %collective-permute-start.9) | collective-permute-done | bytes 233504 | tf_op jit(solution)/shard_map/ppermute | solution.py:392
  63.7 0.3 finish.1
  63.9 11.5 %all_to_all.5.total = f32[16,1,128]{2,1,0:T(1,128)S(1)} all-to-all(f32[16,1,128]{2,1,0:T(1,128)S(1)} %get-tuple-element.70), channel_id=1, replica_groups=mesh['groups'=2,'occ'=4,'vir'=2,'rep'=2] {'occ','vir','rep'}, dimensions={0} | all-to-all | bytes 16384 | tf_op jit(solution)/shard_map/all_to_all | solution.py:397
  75.5 1.1 %jacobi.1 = (f32[200,800]{1,0:T(8,128)}, f32[200,800]{1,0:T(8,128)}) custom-call(f32[200,800]{1,0:T(8,128)S(1)} %get-tuple-element.69.residual, f32[16,1,128]{2,1,0:T(1,128)S(1)} %all_to_all.5.total, f32[200,800]{1,0:T(8,128)S(1)} %get-tuple-element.71.inverse), custom_call_target="tpu_custom_call" | custom-call | tf_op jit(solution)/shard_map/jacobi/pallas_call | solution.py:326
  (24 shorter events, 0.7 us)
Async XLA Ops:
  0.6 1.1 %copy-start.1 = (f32[1,200,800]{2,1,0:T(8,128)S(1)}, f32[1,200,800]{2,1,0:T(8,128)}, u32[]{:S(2)}) copy-start(f32[1,200,800]{2,1,0:T(8,128)} %param.9) | copy-start | bytes 1920004
  1.8 32.5 %collective-permute-start = (f32[1256,128]{1,0:T(8,128)S(1)}, f32[1256,128]{1,0:T(8,128)S(1)}, u32[]{:S(2)}, u32[]{:S(2)}) collective-permute-start(f32[1256,128]{1,0:T(8,128)S(1)} %pack.1.amps), channel_id=1, source_target_pairs={{0,8},{8,0},{4,12},{12,4},{1,9},{9,1},{5,13},{13,5},{2,10},{10,2},... | collective-permute-start | bytes 1929224 | tf_op jit(solution)/shard_map/ppermute | solution.py:361
  5.9 29.1 %collective-permute-start.2 = (f32[1256,128]{1,0:T(8,128)S(1)}, f32[1256,128]{1,0:T(8,128)S(1)}, u32[]{:S(2)}, u32[]{:S(2)}) collective-permute-start(f32[1256,128]{1,0:T(8,128)S(1)} %pack.1.amps), channel_id=1, source_target_pairs={{0,4},{4,0},{8,12},{12,8},{1,5},{5,1},{9,13},{13,9},{2,6},{6,2},{1... | collective-permute-start | bytes 1929224 | tf_op jit(solution)/shard_map/ppermute | solution.py:362
  11.8 2.6 %copy-start = (f32[1,8,800,200]{2,3,1,0:T(8,128)S(1)}, f32[1,8,800,200]{2,3,1,0:T(8,128)}, u32[]{:S(2)}) copy-start(f32[1,8,800,200]{2,3,1,0:T(8,128)} %param.11) | copy-start | bytes 15360004
  14.4 0.7 copy-start.3
  15.1 2.9 %copy-start.2 = (f32[1,200,800]{2,1,0:T(8,128)S(1)}, f32[1,200,800]{2,1,0:T(8,128)}, u32[]{:S(2)}) copy-start(f32[1,200,800]{2,1,0:T(8,128)} %param.10) | copy-start | bytes 1920004
  34.3 6.3 %collective-permute-start.1 = (f32[400,128]{1,0:T(8,128)S(1)}, f32[400,128]{1,0:T(8,128)S(1)}, u32[]{:S(2)}, u32[]{:S(2)}) collective-permute-start(f32[400,128]{1,0:T(8,128)S(1)} %get-tuple-element.75), channel_id=1, source_target_pairs={{0,4},{4,0},{8,12},{12,8},{1,5},{5,1},{9,13},{13,9},{2,6},{6,2},{1... | collective-permute-start | bytes 614408 | tf_op jit(solution)/shard_map/ppermute | solution.py:373
  38.4 9.5 %collective-permute-start.6 = (f32[400,128]{1,0:T(8,128)S(1)}, f32[400,128]{1,0:T(8,128)S(1)}, u32[]{:S(2)}, u32[]{:S(2)}) collective-permute-start(f32[400,128]{1,0:T(8,128)S(1)} %get-tuple-element.60), channel_id=1, source_target_pairs={{0,4},{4,0},{8,12},{12,8},{1,5},{5,1},{9,13},{13,9},{2,6},{6,2},{1... | collective-permute-start | bytes 614408 | tf_op jit(solution)/shard_map/ppermute | solution.py:373
  41.6 10.2 %collective-permute-start.4 = (f32[456,128]{1,0:T(8,128)S(1)}, f32[456,128]{1,0:T(8,128)S(1)}, u32[]{:S(2)}, u32[]{:S(2)}) collective-permute-start(f32[456,128]{1,0:T(8,128)S(1)} %slice.35), channel_id=1, source_target_pairs={{0,4},{4,0},{8,12},{12,8},{1,5},{5,1},{9,13},{13,9},{2,6},{6,2},{1... | collective-permute-start | bytes 700424 | tf_op jit(solution)/shard_map/ppermute | solution.py:384
  46.1 7.2 %collective-permute-start.3 = (f32[400,128]{1,0:T(8,128)S(1)}, f32[400,128]{1,0:T(8,128)S(1)}, u32[]{:S(2)}, u32[]{:S(2)}) collective-permute-start(f32[400,128]{1,0:T(8,128)S(1)} %fusion.8), channel_id=1, source_target_pairs={{0,2},{2,0},{1,3},{3,1},{4,6},{6,4},{5,7},{7,5},{8,10},{10,8},{9,1... | collective-permute-start | bytes 614408 | tf_op jit(solution)/shard_map/ppermute | solution.py:392
  51.5 7.6 %collective-permute-start.7 = (f32[400,128]{1,0:T(8,128)S(1)}, f32[400,128]{1,0:T(8,128)S(1)}, u32[]{:S(2)}, u32[]{:S(2)}) collective-permute-start(f32[400,128]{1,0:T(8,128)S(1)} %fusion.3), channel_id=1, source_target_pairs={{0,2},{2,0},{1,3},{3,1},{4,6},{6,4},{5,7},{7,5},{8,10},{10,8},{9,1... | collective-permute-start | bytes 614408 | tf_op jit(solution)/shard_map/ppermute | solution.py:392
  53.0 1.9 %collective-permute-start.5 = (f32[456,128]{1,0:T(8,128)S(1)}, f32[456,128]{1,0:T(8,128)S(1)}, u32[]{:S(2)}, u32[]{:S(2)}) collective-permute-start(f32[456,128]{1,0:T(8,128)S(1)} %get-tuple-element.58), channel_id=1, source_target_pairs={{0,1},{1,0},{2,3},{3,2},{4,5},{5,4},{6,7},{7,6},{8,9},{9,8},{10,11... | collective-permute-start | bytes 700424 | tf_op jit(solution)/shard_map/ppermute | solution.py:388
  53.4 5.8 %collective-permute-start.8 = (f32[456,128]{1,0:T(8,128)S(1)}, f32[456,128]{1,0:T(8,128)S(1)}, u32[]{:S(2)}, u32[]{:S(2)}) collective-permute-start(f32[456,128]{1,0:T(8,128)S(1)} %get-tuple-element.67), channel_id=1, source_target_pairs={{0,1},{1,0},{2,3},{3,2},{4,5},{5,4},{6,7},{7,6},{8,9},{9,8},{10,11... | collective-permute-start | bytes 700424 | tf_op jit(solution)/shard_map/ppermute | solution.py:388
  54.9 8.8 %collective-permute-start.9 = (f32[456,128]{1,0:T(8,128)S(1)}, f32[456,128]{1,0:T(8,128)S(1)}, u32[]{:S(2)}, u32[]{:S(2)}) collective-permute-start(f32[456,128]{1,0:T(8,128)S(1)} %add.54), channel_id=1, source_target_pairs={{0,2},{2,0},{1,3},{3,1},{4,6},{6,4},{5,7},{7,5},{8,10},{10,8},{9,1... | collective-permute-start | bytes 700424 | tf_op jit(solution)/shard_map/ppermute | solution.py:392

commit v6 on v5

--- a/solution.py
+++ b/solution.py
@@ -370,7 +370,7 @@
     )
     outgoing = [far_amps[c.start : c.start + c.length] for c in chunks]
     outgoing[1:], sums = lax.optimization_barrier((outgoing[1:], sums))
-    last_amps = [lax.ppermute(x, "occ", NEAR) for x in outgoing[:2]]
+    last_amps = [lax.ppermute(x, "occ", NEAR) for x in outgoing]
 
     done = []
     for i, chunk in enumerate(chunks):
@@ -379,9 +379,6 @@
             away, keep = last_product(chunk, (0, 1), *parts)
         else:
             (away,), (keep,) = [last_product(chunk, (half,), *parts) for half in range(2)]
-        if i == 0:
-            away[0], outgoing[2] = lax.optimization_barrier((away[0], outgoing[2]))
-            last_amps.append(lax.ppermute(outgoing[2], "occ", NEAR))
         if i < 2:
             got = from_other_core(away)
         else:

time: 77 us -> 76 us (0.987)
  starting transfers between devices: 14.3 us -> 12.6 us
    ppermute x3, starting transfers between devices: 4.15 us -> 2.77 us  [chain_body(): last_amps = [lax.ppermute(x, 'occ', NEAR) for x in outgoing]]
where the time goes in v6:
time: 76 us; the launch traced here: 75.7 us
  waiting for transfers between devices  21.8 us (29%)
  blocking collectives  16.8 us (22%)
  Pallas kernels  14.6 us (19%)
  starting transfers between devices  12.6 us (17%)
  local copies, waits for them, and re-layouts  6.1 us (8%)
  between operations  3.4 us (4%)
    ppermute x1, waiting for transfers between devices, chain_body(): far_amps = lax.ppermute(own, 'occ', FAR)  13.8 us
    all_to_all x1, blocking collectives, chain_body(): lax.all_to_all(total, ('occ', 'vir', 'rep'), split_axis=0, concat_axis=0,...  12 us
    ppermute x3, waiting for transfers between devices, chain_body(): far = lax.ppermute(for_far, 'vir', SWAP)  7.08 us
    all_gather x2, blocking collectives, from_other_core(): both = lax.all_gather(jnp.concatenate(parts), 'rep', axis=0, tiled=True)  4.79 us
    unnamed x8, local copies, waits for them, and re-layouts  4.39 us
    pallas_call x4, Pallas kernels, last_product(): pl.pallas_call(kernel, in_specs=[SMEM] * 3 + [VMEM] * 3, out_specs=[VMEM]...  4.31 us
    ppermute x1, starting transfers between devices, chain_body(): far_amps = lax.ppermute(own, 'occ', FAR)  4.1 us
    ppermute x3, starting transfers between devices, chain_body(): far = lax.ppermute(for_far, 'vir', SWAP)  3.63 us
  transfers between devices with their start and end apart: 10, of which 5 were waited for; matrix products, arithmetic and copies ran while one was open for 3% of the time, Pallas kernels for 17%

profile of v6, /device:TPU:0, one launch (start us, length us, event | category | flops | bytes accessed | tf_op | source)
XLA Modules:
  0.0 75.7 jit_solution(1524399053202111259)
XLA Ops:
  0.6 1.1 %copy-done.1 = f32[1,200,800]{2,1,0:T(8,128)S(1)} copy-done((f32[1,200,800]{2,1,0:T(8,128)S(1)}, f32[1,200,800]{2,1,0:T(8,128)}, u32[]{:S(2)}) %copy-start.1) | copy-done | bytes 640024
  1.8 4.1 %collective-permute-start = (f32[1256,128]{1,0:T(8,128)S(1)}, f32[1256,128]{1,0:T(8,128)S(1)}, u32[]{:S(2)}, u32[]{:S(2)}) collective-permute-start(f32[1256,128]{1,0:T(8,128)S(1)} %pack.1.amps), channel_id=1, source_target_pairs={{0,8},{8,0},{4,12},{12,4},{1,9},{9,1},{5,13},{13,5},{2,10},{10,2},... | collective-permute-start | bytes 1929224 | tf_op jit(solution)/shard_map/ppermute | solution.py:361
  5.9 1.6 %collective-permute-start.2 = (f32[1256,128]{1,0:T(8,128)S(1)}, f32[1256,128]{1,0:T(8,128)S(1)}, u32[]{:S(2)}, u32[]{:S(2)}) collective-permute-start(f32[1256,128]{1,0:T(8,128)S(1)} %pack.1.amps), channel_id=1, source_target_pairs={{0,4},{4,0},{8,12},{12,8},{1,5},{5,1},{9,13},{13,9},{2,6},{6,2},{1... | collective-permute-start | bytes 1929224 | tf_op jit(solution)/shard_map/ppermute | solution.py:362
  10.1 0.7 reshape.14.eps_row
  10.8 0.8 %dynamic_slice.3 = f32[200]{0:T(256)S(1)} dynamic-slice(f32[800]{0:T(1024)} %param.16, s32[]{:T(128)S(6)} %select_n.3), dynamic_slice_sizes={200} | dynamic-slice | bytes 1604 | tf_op jit(solution)/shard_map/dynamic_slice | solution.py:353
  11.6 0.1 copy.11.eps_col
  11.7 0.1 stack.35.meta
  11.8 2.6 %copy-done = f32[1,8,800,200]{2,3,1,0:T(8,128)S(1)} copy-done((f32[1,8,800,200]{2,3,1,0:T(8,128)S(1)}, f32[1,8,800,200]{2,3,1,0:T(8,128)}, u32[]{:S(2)}) %copy-start) | copy-done | bytes 5120024
  14.4 0.7 copy-done.3
  15.1 3.4 %sum_by_source.1.weights = bf16[4,2,800,200]{3,2,1,0:T(8,128)(2,1)S(1)} custom-call(s32[8]{0:T(128)S(1)} %stack.35.meta, s32[8]{0:T(128)S(1)} %bitcast.20, s32[1]{0:T(128)S(6)} %copy.12.count, f32[8,200,800]{2,1,0:T(8,128)S(1)} %bitcast.17), custom_call_target="tpu_custom_call" | custom-call | tf_op jit(solution)/shard_map/sum_by_source/pallas_call | solution.py:135
  18.4 2.1 %own_products.1 = (f32[200,800]{1,0:T(8,128)S(1)}, f32[2,400,256]{2,1,0:T(8,128)S(1)}, f32[2,400,256]{2,1,0:T(8,128)S(1)}, f32[2,400,288]{2,1,0:T(8,128)S(1)}) custom-call(s32[8]{0:T(128)S(1)} %stack.35.meta, s32[1,1]{1,0:T(1,128)S(6)} %copy.13.lad_src, f32[1,1]{1,0:T(1,128)S(6)} %copy.14.lad_coef, f32[1]{0:T(128)S(6)} %copy.15.energy, ...), custom_call_target="tpu_custom_call" | custom-call | tf_op jit(solution)/shard_map/own_products/pallas_call | solution.py:182
  20.5 13.8 %collective-permute-done.refs_1_ = f32[1256,128]{1,0:T(8,128)S(1)} collective-permute-done((f32[1256,128]{1,0:T(8,128)S(1)}, f32[1256,128]{1,0:T(8,128)S(1)}, u32[]{:S(2)}, u32[]{:S(2)}) %collective-permute-start) | collective-permute-done | bytes 643104 | tf_op jit(solution)/shard_map/ppermute | solution.py:361
  34.3 0.7 collective-permute-start.1
  35.0 3.4 %add_products.1 = (f32[2,400,256]{2,1,0:T(8,128)S(1)}, f32[2,400,256]{2,1,0:T(8,128)S(1)}, f32[2,400,288]{2,1,0:T(8,128)S(1)}) custom-call(s32[8]{0:T(128)S(1)} %stack.35.meta, s32[1,1]{1,0:T(1,128)S(6)} %copy.13.lad_src, f32[1,1]{1,0:T(1,128)S(6)} %copy.14.lad_coef, bf16[4,2,800,200]{3,2,1,0:T(8,128)(2,1)S(1)} %sum_by_source.1.weights, ...), custom_call_target="tpu_custom_call" | custom-call | tf_op jit(solution)/shard_map/add_products/pallas_call | solution.py:214
  38.4 1.5 %collective-permute-start.6 = (f32[400,128]{1,0:T(8,128)S(1)}, f32[400,128]{1,0:T(8,128)S(1)}, u32[]{:S(2)}, u32[]{:S(2)}) collective-permute-start(f32[400,128]{1,0:T(8,128)S(1)} %get-tuple-element.56), channel_id=1, source_target_pairs={{0,4},{4,0},{8,12},{12,8},{1,5},{5,1},{9,13},{13,9},{2,6},{6,2},{1... | collective-permute-start | bytes 614408 | tf_op jit(solution)/shard_map/ppermute | solution.py:373
  39.9 0.6 collective-permute-start.4
  40.6 1.0 %last_product.4 = (f32[400,128]{1,0:T(8,128)S(1)}, f32[400,128]{1,0:T(8,128)S(1)}, f32[400,128]{1,0:T(8,128)S(1)}, f32[400,128]{1,0:T(8,128)S(1)}) custom-call(s32[8]{0:T(128)S(1)} %stack.35.meta, s32[1,1]{1,0:T(1,128)S(6)} %copy.13.lad_src, f32[1,1]{1,0:T(1,128)S(6)} %copy.14.lad_coef, bf16[4,2,800,200]{3,2,1,0:T(8,128)(2,1)S(1)} %sum_by_source.1.weights, ...), custom_call_target="tpu_custom_call" | custom-call | tf_op jit(solution)/shard_map/last_product/pallas_call | solution.py:240
  41.6 2.4 %all_gather.6 = f32[1600,128]{1,0:T(8,128)S(1)} all-gather(f32[800,128]{1,0:T(8,128)S(1)} %pad_maximum_fusion), channel_id=1, replica_groups=mesh['groups'=2,'occ'=4,'vir'=2,'rep'=2] {'rep'}, dimensions={0}, use_global_device_ids=true | all-gather | bytes 1228800 | tf_op jit(solution)/shard_map/all_gather | solution.py:253
  44.1 1.5 %collective-permute-start.3 = (f32[400,128]{1,0:T(8,128)S(1)}, f32[400,128]{1,0:T(8,128)S(1)}, u32[]{:S(2)}, u32[]{:S(2)}) collective-permute-start(f32[400,128]{1,0:T(8,128)S(1)} %fusion.8), channel_id=1, source_target_pairs={{0,2},{2,0},{1,3},{3,1},{4,6},{6,4},{5,7},{7,5},{8,10},{10,8},{9,1... | collective-permute-start | bytes 614408 | tf_op jit(solution)/shard_map/ppermute | solution.py:389
  45.6 0.8 %collective-permute-done.6.amps = f32[400,128]{1,0:T(8,128)S(1)} collective-permute-done((f32[400,128]{1,0:T(8,128)S(1)}, f32[400,128]{1,0:T(8,128)S(1)}, u32[]{:S(2)}, u32[]{:S(2)}) %collective-permute-start.6) | collective-permute-done | bytes 204832 | tf_op jit(solution)/shard_map/ppermute | solution.py:373
  46.5 1.0 %last_product.7 = (f32[400,128]{1,0:T(8,128)S(1)}, f32[400,128]{1,0:T(8,128)S(1)}, f32[400,128]{1,0:T(8,128)S(1)}, f32[400,128]{1,0:T(8,128)S(1)}) custom-call(s32[8]{0:T(128)S(1)} %stack.35.meta, s32[1,1]{1,0:T(1,128)S(6)} %copy.13.lad_src, f32[1,1]{1,0:T(1,128)S(6)} %copy.14.lad_coef, bf16[4,2,800,200]{3,2,1,0:T(8,128)(2,1)S(1)} %sum_by_source.1.weights, ...), custom_call_target="tpu_custom_call" | custom-call | tf_op jit(solution)/shard_map/last_product/pallas_call | solution.py:240
  47.5 2.4 %all_gather.7 = f32[1600,128]{1,0:T(8,128)S(1)} all-gather(f32[800,128]{1,0:T(8,128)S(1)} %pad_maximum_fusion.1), channel_id=1, replica_groups=mesh['groups'=2,'occ'=4,'vir'=2,'rep'=2] {'rep'}, dimensions={0}, use_global_device_ids=true | all-gather | bytes 1228800 | tf_op jit(solution)/shard_map/all_gather | solution.py:253
  50.0 1.6 %collective-permute-start.7 = (f32[400,128]{1,0:T(8,128)S(1)}, f32[400,128]{1,0:T(8,128)S(1)}, u32[]{:S(2)}, u32[]{:S(2)}) collective-permute-start(f32[400,128]{1,0:T(8,128)S(1)} %fusion.3), channel_id=1, source_target_pairs={{0,2},{2,0},{1,3},{3,1},{4,6},{6,4},{5,7},{7,5},{8,10},{10,8},{9,1... | collective-permute-start | bytes 614408 | tf_op jit(solution)/shard_map/ppermute | solution.py:389
  51.6 1.1 %last_product.6 = (f32[456,128]{1,0:T(8,128)S(1)}, f32[456,128]{1,0:T(8,128)S(1)}) custom-call(s32[8]{0:T(128)S(1)} %stack.35.meta, s32[1,1]{1,0:T(1,128)S(6)} %copy.13.lad_src, f32[1,1]{1,0:T(1,128)S(6)} %copy.14.lad_coef, bf16[4,2,800,200]{3,2,1,0:T(8,128)(2,1)S(1)} %sum_by_source.1.weights, f32[456,128]{1,0:T(8,128)S(1)} %collective-permute-done.4.amps, ...), custom_call_target="tpu_custom_call" | custom-call | tf_op jit(solution)/shard_map/last_product/pallas_call | solution.py:240
  52.8 0.5 collective-permute-start.8
  53.3 1.1 %last_product.5 = (f32[456,128]{1,0:T(8,128)S(1)}, f32[456,128]{1,0:T(8,128)S(1)}) custom-call(s32[8]{0:T(128)S(1)} %stack.35.meta, s32[1,1]{1,0:T(1,128)S(6)} %copy.13.lad_src, f32[1,1]{1,0:T(1,128)S(6)} %copy.14.lad_coef, bf16[4,2,800,200]{3,2,1,0:T(8,128)(2,1)S(1)} %sum_by_source.1.weights, f32[456,128]{1,0:T(8,128)S(1)} %collective-permute-done.4.amps, ...), custom_call_target="tpu_custom_call" | custom-call | tf_op jit(solution)/shard_map/last_product/pallas_call | solution.py:240
  54.6 0.6 collective-permute-start.9
  55.1 2.0 %collective-permute-done.7 = f32[400,128]{1,0:T(8,128)S(1)} collective-permute-done((f32[400,128]{1,0:T(8,128)S(1)}, f32[400,128]{1,0:T(8,128)S(1)}, u32[]{:S(2)}, u32[]{:S(2)}) %collective-permute-start.7) | collective-permute-done | bytes 204832 | tf_op jit(solution)/shard_map/ppermute | solution.py:389
  57.3 5.0 %collective-permute-done.9.refs_4_ = f32[456,128]{1,0:T(8,128)S(1)} collective-permute-done((f32[456,128]{1,0:T(8,128)S(1)}, f32[456,128]{1,0:T(8,128)S(1)}, u32[]{:S(2)}, u32[]{:S(2)}) %collective-permute-start.9) | collective-permute-done | bytes 233504 | tf_op jit(solution)/shard_map/ppermute | solution.py:389
  62.3 0.3 finish.1
  62.6 12.0 %all_to_all.5.total = f32[16,1,128]{2,1,0:T(1,128)S(1)} all-to-all(f32[16,1,128]{2,1,0:T(1,128)S(1)} %get-tuple-element.66), channel_id=1, replica_groups=mesh['groups'=2,'occ'=4,'vir'=2,'rep'=2] {'occ','vir','rep'}, dimensions={0} | all-to-all | bytes 16384 | tf_op jit(solution)/shard_map/all_to_all | solution.py:394
  74.6 1.1 %jacobi.1 = (f32[200,800]{1,0:T(8,128)}, f32[200,800]{1,0:T(8,128)}) custom-call(f32[200,800]{1,0:T(8,128)S(1)} %get-tuple-element.65.residual, f32[16,1,128]{2,1,0:T(1,128)S(1)} %all_to_all.5.total, f32[200,800]{1,0:T(8,128)S(1)} %get-tuple-element.67.inverse), custom_call_target="tpu_custom_call" | custom-call | tf_op jit(solution)/shard_map/jacobi/pallas_call | solution.py:326
  (24 shorter events, 0.7 us)
Async XLA Ops:
  0.6 1.1 %copy-start.1 = (f32[1,200,800]{2,1,0:T(8,128)S(1)}, f32[1,200,800]{2,1,0:T(8,128)}, u32[]{:S(2)}) copy-start(f32[1,200,800]{2,1,0:T(8,128)} %param.9) | copy-start | bytes 1920004
  1.8 32.5 %collective-permute-start = (f32[1256,128]{1,0:T(8,128)S(1)}, f32[1256,128]{1,0:T(8,128)S(1)}, u32[]{:S(2)}, u32[]{:S(2)}) collective-permute-start(f32[1256,128]{1,0:T(8,128)S(1)} %pack.1.amps), channel_id=1, source_target_pairs={{0,8},{8,0},{4,12},{12,4},{1,9},{9,1},{5,13},{13,5},{2,10},{10,2},... | collective-permute-start | bytes 1929224 | tf_op jit(solution)/shard_map/ppermute | solution.py:361
  5.9 29.1 %collective-permute-start.2 = (f32[1256,128]{1,0:T(8,128)S(1)}, f32[1256,128]{1,0:T(8,128)S(1)}, u32[]{:S(2)}, u32[]{:S(2)}) collective-permute-start(f32[1256,128]{1,0:T(8,128)S(1)} %pack.1.amps), channel_id=1, source_target_pairs={{0,4},{4,0},{8,12},{12,8},{1,5},{5,1},{9,13},{13,9},{2,6},{6,2},{1... | collective-permute-start | bytes 1929224 | tf_op jit(solution)/shard_map/ppermute | solution.py:362
  11.8 2.6 %copy-start = (f32[1,8,800,200]{2,3,1,0:T(8,128)S(1)}, f32[1,8,800,200]{2,3,1,0:T(8,128)}, u32[]{:S(2)}) copy-start(f32[1,8,800,200]{2,3,1,0:T(8,128)} %param.11) | copy-start | bytes 15360004
  14.4 0.7 copy-start.3
  15.1 3.4 %copy-start.2 = (f32[1,200,800]{2,1,0:T(8,128)S(1)}, f32[1,200,800]{2,1,0:T(8,128)}, u32[]{:S(2)}) copy-start(f32[1,200,800]{2,1,0:T(8,128)} %param.10) | copy-start | bytes 1920004
  34.3 6.3 %collective-permute-start.1 = (f32[400,128]{1,0:T(8,128)S(1)}, f32[400,128]{1,0:T(8,128)S(1)}, u32[]{:S(2)}, u32[]{:S(2)}) collective-permute-start(f32[400,128]{1,0:T(8,128)S(1)} %get-tuple-element.71), channel_id=1, source_target_pairs={{0,4},{4,0},{8,12},{12,8},{1,5},{5,1},{9,13},{13,9},{2,6},{6,2},{1... | collective-permute-start | bytes 614408 | tf_op jit(solution)/shard_map/ppermute | solution.py:373
  38.4 8.0 %collective-permute-start.6 = (f32[400,128]{1,0:T(8,128)S(1)}, f32[400,128]{1,0:T(8,128)S(1)}, u32[]{:S(2)}, u32[]{:S(2)}) collective-permute-start(f32[400,128]{1,0:T(8,128)S(1)} %get-tuple-element.56), channel_id=1, source_target_pairs={{0,4},{4,0},{8,12},{12,8},{1,5},{5,1},{9,13},{13,9},{2,6},{6,2},{1... | collective-permute-start | bytes 614408 | tf_op jit(solution)/shard_map/ppermute | solution.py:373
  39.9 11.7 %collective-permute-start.4 = (f32[456,128]{1,0:T(8,128)S(1)}, f32[456,128]{1,0:T(8,128)S(1)}, u32[]{:S(2)}, u32[]{:S(2)}) collective-permute-start(f32[456,128]{1,0:T(8,128)S(1)} %slice.35), channel_id=1, source_target_pairs={{0,4},{4,0},{8,12},{12,8},{1,5},{5,1},{9,13},{13,9},{2,6},{6,2},{1... | collective-permute-start | bytes 700424 | tf_op jit(solution)/shard_map/ppermute | solution.py:373
  44.1 10.3 %collective-permute-start.3 = (f32[400,128]{1,0:T(8,128)S(1)}, f32[400,128]{1,0:T(8,128)S(1)}, u32[]{:S(2)}, u32[]{:S(2)}) collective-permute-start(f32[400,128]{1,0:T(8,128)S(1)} %fusion.8), channel_id=1, source_target_pairs={{0,2},{2,0},{1,3},{3,1},{4,6},{6,4},{5,7},{7,5},{8,10},{10,8},{9,1... | collective-permute-start | bytes 614408 | tf_op jit(solution)/shard_map/ppermute | solution.py:389
  50.0 7.2 %collective-permute-start.7 = (f32[400,128]{1,0:T(8,128)S(1)}, f32[400,128]{1,0:T(8,128)S(1)}, u32[]{:S(2)}, u32[]{:S(2)}) collective-permute-start(f32[400,128]{1,0:T(8,128)S(1)} %fusion.3), channel_id=1, source_target_pairs={{0,2},{2,0},{1,3},{3,1},{4,6},{6,4},{5,7},{7,5},{8,10},{10,8},{9,1... | collective-permute-start | bytes 614408 | tf_op jit(solution)/shard_map/ppermute | solution.py:389
  52.7 1.8 %collective-permute-start.5 = (f32[456,128]{1,0:T(8,128)S(1)}, f32[456,128]{1,0:T(8,128)S(1)}, u32[]{:S(2)}, u32[]{:S(2)}) collective-permute-start(f32[456,128]{1,0:T(8,128)S(1)} %get-tuple-element.54), channel_id=1, source_target_pairs={{0,1},{1,0},{2,3},{3,2},{4,5},{5,4},{6,7},{7,6},{8,9},{9,8},{10,11... | collective-permute-start | bytes 700424 | tf_op jit(solution)/shard_map/ppermute | solution.py:385
  52.8 4.5 %collective-permute-start.8 = (f32[456,128]{1,0:T(8,128)S(1)}, f32[456,128]{1,0:T(8,128)S(1)}, u32[]{:S(2)}, u32[]{:S(2)}) collective-permute-start(f32[456,128]{1,0:T(8,128)S(1)} %get-tuple-element.63), channel_id=1, source_target_pairs={{0,1},{1,0},{2,3},{3,2},{4,5},{5,4},{6,7},{7,6},{8,9},{9,8},{10,11... | collective-permute-start | bytes 700424 | tf_op jit(solution)/shard_map/ppermute | solution.py:385
  54.6 7.7 %collective-permute-start.9 = (f32[456,128]{1,0:T(8,128)S(1)}, f32[456,128]{1,0:T(8,128)S(1)}, u32[]{:S(2)}, u32[]{:S(2)}) collective-permute-start(f32[456,128]{1,0:T(8,128)S(1)} %add.54), channel_id=1, source_target_pairs={{0,2},{2,0},{1,3},{3,1},{4,6},{6,4},{5,7},{7,5},{8,10},{10,8},{9,1... | collective-permute-start | bytes 700424 | tf_op jit(solution)/shard_map/ppermute | solution.py:389
